TPU v7x, 32 devices: a whole 2x2x4 slice. The times are simulated.
32 devices in a mesh: ctx: 8 (over z, y), head: 4 (over x, core).
Axes of the slice: x: 2, y: 2, z: 4, core: 2. Of those that a mesh axis runs over, the one named last changes fastest.
Arguments:
- query_in: bfloat16 [1024, 2048], P('ctx', 'head'), may hold values from -6 to 6
- key_in: bfloat16 [1024, 2048], P('ctx', 'head'), may hold values from -6 to 6
- value_in: bfloat16 [1024, 4096], P('ctx', 'head'), may hold values from -6 to 6
- gate_in: bfloat16 [1024, 4096], P('ctx', 'head'), may hold values from -6 to 6
- conv_query: float32 [4, 2048], P(None, 'head'), may hold values from -3 to 3
- conv_key: float32 [4, 2048], P(None, 'head'), may hold values from -3 to 3
- conv_value: float32 [4, 4096], P(None, 'head'), may hold values from -3 to 3
- decay_in: float32 [32, 1024], P('head', 'ctx'), may hold values from -14 to 0.1
- beta_in: float32 [32, 1024], P('head', 'ctx'), may hold values from -2.5 to -1.5
- norm_gain: float32 [128], replicated, may hold values from 0.5 to 1.5
- doc_lengths: int32 [16], replicated, may hold values from 1 to 256, 1024 in all
- out_weight: bfloat16 [4096, 2048], P('head'), may hold values from -0.09375 to 0.09375
Outputs:
- projected: bfloat16 [2048, 1024], P('head', 'ctx')
Inputs may be any that keep to these rules, and one draw needn't show every extreme that they name: `doc_lengths`: lengths of the 16 packed documents in packing order; they sum to 1024, and the longest has exactly 256 tokens.
All inputs are finite; a program needn't handle non-finite values.
Results may differ from a plain program's by a relative error of at most 0.017.
Values may be sent and summed in bfloat16 or wider, within the bound.
No kernel may reach another device: no remote copies, remote signals or barrier semaphores. Data moves between devices by JAX's collectives and lax.ppermute only.
A program may use at most 192 MiB of HBM per device.

v0:
```python
import jax
import jax.numpy as jnp
from jax import lax
from jax.sharding import PartitionSpec as P

DK = 128
DV = 128
SPAN = 64


PRECISE = lax.Precision.HIGHEST


def passed_along(value, axis, by):
    devices = lax.axis_size(axis)
    pairs = [(i, i + by) for i in range(devices) if 0 <= i + by < devices]
    return lax.ppermute(value, axis, pairs)


def carried_in(value, axis, combine, identity):
    devices, mine = (lax.axis_size(axis), lax.axis_index(axis))
    everything = jax.tree.map(
        lambda part, kind: lax.all_gather(part.astype(kind), axis),
        value,
        (jnp.bfloat16, jnp.bfloat16),
    )
    start = jax.tree.map(
        lambda part, zero: jnp.broadcast_to(jnp.asarray(zero, part.dtype), part.shape),
        value,
        identity,
    )

    def hop(k, before):
        reached = k < mine
        new = combine(
            before, jax.tree.map(lambda part, own: part[k].astype(own.dtype), everything, value)
        )
        return jax.tree.map(lambda a, b: jnp.where(reached, a, b), new, before)

    return lax.fori_loop(0, devices, hop, start)


def shard_conv(before, current, weight, keep_masks):
    margin = weight.shape[0] - 1
    count_rows = current.shape[0]
    padded = jnp.concatenate([before, current], axis=0).astype(jnp.float32)
    summed = jnp.zeros((count_rows, current.shape[1]), jnp.float32)
    for offset in range(margin + 1):
        summed = (
            summed
            + weight[offset][None, :]
            * padded[offset : offset + count_rows]
            * keep_masks[margin - offset][:, None]
        )
    return jax.nn.silu(summed)


def unit_heads(vectors, head_count):
    reshaped = vectors.reshape(vectors.shape[0], head_count, -1)
    return reshaped / jnp.sqrt(jnp.sum(reshaped * reshaped, axis=-1, keepdims=True) + 1e-06)


def span_terms(queries, keys_unit, values, log_gamma, beta_values, resets):
    length = resets.shape[0]
    segment = jnp.cumsum(resets)
    cumulative = jnp.cumsum(log_gamma, axis=-1)
    row_index = jnp.arange(length, dtype=jnp.int32)[:, None]
    col_index = jnp.arange(length, dtype=jnp.int32)[None, :]
    same_doc = (segment[:, None] == segment[None, :]) & (row_index >= col_index)
    strict = same_doc & (row_index > col_index)
    log_ratio = cumulative[:, :, None] - cumulative[:, None, :]
    decay_pairs = jnp.exp(jnp.where(same_doc[None], log_ratio, -1e30))
    key_gram = jnp.einsum("hid,hjd->hij", keys_unit, keys_unit, precision=PRECISE)
    lower_part = jnp.where(strict[None], beta_values[:, :, None] * key_gram * decay_pairs, 0.0)
    head_start = jnp.where(segment[None, :] == 0, jnp.exp(cumulative), 0.0)
    last_segment = segment[length - 1]
    to_end = jnp.where(
        segment[None, :] == last_segment, jnp.exp(cumulative[:, length - 1 :] - cumulative), 0.0
    )
    through = jnp.where(last_segment == 0, jnp.exp(cumulative[:, length - 1]), 0.0)
    values_in = lax.linalg.triangular_solve(
        lower_part, beta_values[:, :, None] * values, left_side=True, lower=True, unit_diagonal=True
    )
    keys_in = lax.linalg.triangular_solve(
        lower_part,
        (beta_values * head_start)[:, :, None] * keys_unit,
        left_side=True,
        lower=True,
        unit_diagonal=True,
    )
    scores = jnp.einsum("hid,hjd->hij", queries, keys_unit, precision=PRECISE)
    inside = jnp.where(same_doc[None], scores * decay_pairs, 0.0)
    return (values_in, keys_in, inside, head_start, to_end, through)


def body(
    query_in,
    key_in,
    value_in,
    gate_in,
    conv_query,
    conv_key,
    conv_value,
    decay_in,
    beta_in,
    norm_gain,
    doc_lengths,
    out_weight,
):
    count_rows = query_in.shape[0]
    margin = conv_query.shape[0] - 1
    key_width = query_in.shape[1]
    value_heads = decay_in.shape[0]
    key_heads = key_width // DK
    tail_rows = jnp.concatenate(
        [
            query_in[count_rows - margin :],
            key_in[count_rows - margin :],
            value_in[count_rows - margin :],
        ],
        axis=1,
    )
    before = passed_along(tail_rows, "ctx", 1)
    first_row = lax.axis_index("ctx") * count_rows
    positions = first_row - margin + jnp.arange(count_rows + margin, dtype=jnp.int32)
    doc_starts = jnp.cumsum(doc_lengths) - doc_lengths
    start_flags = jnp.any(positions[:, None] == doc_starts[None, :], axis=1).astype(jnp.int32)
    running = jnp.cumsum(start_flags)
    keep_masks = [
        (
            running[margin:] - running[margin - lag_steps : margin - lag_steps + count_rows] == 0
        ).astype(jnp.float32)
        for lag_steps in range(margin + 1)
    ]
    resets = start_flags[margin:]
    queries = unit_heads(
        shard_conv(before[:, :key_width], query_in, conv_query, keep_masks), key_heads
    )
    keys_unit = unit_heads(
        shard_conv(before[:, key_width : 2 * key_width], key_in, conv_key, keep_masks), key_heads
    )
    values = shard_conv(before[:, 2 * key_width :], value_in, conv_value, keep_masks).reshape(
        count_rows, value_heads, DV
    )
    group_ratio = value_heads // key_heads
    queries = jnp.repeat(queries, group_ratio, axis=1)
    keys_unit = jnp.repeat(keys_unit, group_ratio, axis=1)
    log_gamma = -jax.nn.softplus(decay_in)
    beta_values = jax.nn.sigmoid(beta_in)
    spans = count_rows // SPAN

    def blocks(array):
        return array.reshape(spans, SPAN, value_heads, array.shape[-1]).transpose(0, 2, 1, 3)

    def gate_blocks(array):
        return array.reshape(value_heads, spans, SPAN).transpose(1, 0, 2)

    query_blocks = blocks(queries)
    key_blocks = blocks(keys_unit)
    value_blocks = blocks(values)
    values_in, keys_in, inside, head_start, to_end, through = jax.vmap(span_terms)(
        query_blocks,
        key_blocks,
        value_blocks,
        gate_blocks(log_gamma),
        gate_blocks(beta_values),
        resets.reshape(spans, SPAN),
    )
    key_end = key_blocks * to_end[..., None]
    zeros_state = jnp.zeros((value_heads, DK, DV), jnp.float32)
    identity = jnp.broadcast_to(jnp.eye(DK, dtype=jnp.float32), (value_heads, DK, DK))

    def state_step(carried, inputs):
        values_part, keys_part, end_keys, passing = inputs
        fresh_values = values_part - jnp.einsum(
            "hcd,hde->hce", keys_part, carried, precision=PRECISE
        )
        carried = passing[:, None, None] * carried + jnp.einsum(
            "hcd,hce->hde", end_keys, fresh_values, precision=PRECISE
        )
        return (carried, None)

    local_state, _ = lax.scan(state_step, zeros_state, (values_in, keys_in, key_end, through))

    def transition_step(carried, inputs):
        keys_part, end_keys, passing = inputs
        moved_rows = jnp.einsum("hcd,hde->hce", keys_part, carried, precision=PRECISE)
        return (
            passing[:, None, None] * carried
            - jnp.einsum("hcd,hce->hde", end_keys, moved_rows, precision=PRECISE),
            None,
        )

    final_map, _ = lax.scan(transition_step, identity, (keys_in, key_end, through))

    def compose(earlier, later):
        joined_map = jnp.einsum("hij,hjk->hik", later[0], earlier[0], precision=PRECISE)
        joined_state = (
            jnp.einsum("hij,hjk->hik", later[0], earlier[1], precision=PRECISE) + later[1]
        )
        return (joined_map, joined_state)

    prefix = carried_in((final_map, local_state), "ctx", compose, (identity, zeros_state))
    incoming = prefix[1]

    def output_step(carried, inputs):
        values_part, keys_part, query_part, inside_part, start_part, end_keys, passing = inputs
        fresh_values = values_part - jnp.einsum(
            "hcd,hde->hce", keys_part, carried, precision=PRECISE
        )
        result = jnp.einsum(
            "hcd,hde->hce", query_part * start_part[..., None], carried, precision=PRECISE
        ) + jnp.einsum("hij,hje->hie", inside_part, fresh_values, precision=PRECISE)
        carried = passing[:, None, None] * carried + jnp.einsum(
            "hcd,hce->hde", end_keys, fresh_values, precision=PRECISE
        )
        return (carried, result)

    _, results = lax.scan(
        output_step,
        incoming,
        (values_in, keys_in, query_blocks, inside, head_start, key_end, through),
    )
    heads_out = results.transpose(0, 2, 1, 3).reshape(count_rows, value_heads, DV)
    gate_values = gate_in.astype(jnp.float32).reshape(count_rows, value_heads, DV)
    normed = (
        heads_out
        / jnp.sqrt(jnp.mean(heads_out * heads_out, axis=-1, keepdims=True) + 1e-06)
        * norm_gain
        * jax.nn.silu(gate_values)
    )
    mixed_rows = normed.reshape(count_rows, value_heads * DV).astype(jnp.bfloat16)
    return lax.psum_scatter(
        lax.dot_general(
            out_weight, mixed_rows, (((0,), (1,)), ((), ())), preferred_element_type=jnp.float32
        ).astype(jnp.bfloat16),
        "head",
        scatter_dimension=0,
        tiled=True,
    )


def solution(mesh):
    return jax.shard_map(
        body,
        mesh=mesh,
        in_specs=(
            P("ctx", "head"),
            P("ctx", "head"),
            P("ctx", "head"),
            P("ctx", "head"),
            P(None, "head"),
            P(None, "head"),
            P(None, "head"),
            P("head", "ctx"),
            P("head", "ctx"),
            P(),
            P(),
            P("head", None),
        ),
        out_specs=P("head", "ctx"),
        check_vma=False,
    )
```

profile of v0, /device:TPU:0, one launch (start us, length us, event | category | flops | bytes accessed | tf_op | source)
XLA Modules:
  0.0 266.3 jit_solution(12358320228140601187)
XLA Ops:
  8.7 4.9 %collective-permute-start = (bf16[3,2048]{1,0:T(4,128)(2,1)S(1)}, bf16[3,2048]{1,0:T(4,128)(2,1)S(1)}, u32[]{:S(2)}, u32[]{:S(2)}) collective-permute-start(bf16[3,2048]{1,0:T(4,128)(2,1)S(1)} %pad_maximum_fusion), channel_id=1, source_target_pairs={{0,4},{4,8},{8,12},{12,16},{16,20},{20,24},{24,28},{1,5},{5,9},{9,... | collective-permute-start | bytes 36872 | tf_op jit(solution)/shard_map/ppermute | solution.py:17
  25.0 78.6 %custom-call.6 = f32[2,8,1,64,64]{3,4,2,1,0:T(8,128)S(1)} custom-call(f32[2,8,1,64,64]{4,3,2,1,0:T(8,128)S(1)} %fusion.49), custom_call_target="InvertDiagBlocksLowerTriangular" | custom-call | tf_op jit(solution)/shard_map/vmap()/triangular_solve/custom-call.1 | solution.py:84
  104.3 1.2 fusion.61
  106.9 3.5 %while.49 = (s32[]{:T(128)}, f32[8,128,128]{2,1,0:T(8,128)S(1)}, f32[2,8]{1,0:T(2,128)S(1)}, f32[2,8,64,128]{3,2,1,0:T(8,128)S(1)}, f32[2,8,64,128]{3,2,1,0:T(8,...) while((s32[]{:T(128)}, f32[8,128,128]{2,1,0:T(8,128)S(1)}, ...), condition=%wide.region_10.12_spmd.clone, body=%wide.region_9.11_spmd.clone.sunk | while | flops 201916416 | bytes 2885288 | solution.py:183
  111.3 3.5 %while.47 = (s32[]{:T(128)}, f32[8,128,128]{2,1,0:T(8,128)S(1)}, f32[2,8]{1,0:T(2,128)S(1)}, f32[2,8,64,128]{3,2,1,0:T(8,128)S(1)}, f32[2,8,64,128]{3,2,1,0:T(8,128)S(1)}, /*index=5*/s32[]{:T(128)}) while((s32[]{:T(128)}, f32[8,128,128]{2,1,0:T(8,128)S(1)}, f32[2,8]{1,0:T(2,128)S(1)}, f32[2,8,64,128]{3,2,1,0:T(8,128)S(1)}, ...), condition=%wide.region_8.10_spmd, body=%wide.region_7.9_spmd.sunk | while | flops 201588736 | bytes 2622097 | solution.py:194
  113.7 1.1 convolution_subtract_fusion.6
  116.5 2.0 fusion.44
  118.6 42.4 %all-gather.7.cloned.1.call-done = bf16[64,128,128]{2,1,0:T(8,128)(2,1)} async-done(((bf16[8,128,128]{2,1,0:T(8,128)(2,1)}), bf16[64,128,128]{2,1,0:T(8,128)(2,1)}) %all-gather.7.cloned.1.call-update) | async-done | bytes 2097168 | tf_op jit(solution)/shard_map/all_gather | solution.py:23
  160.9 49.9 %all-gather.5.cloned.1.call-done = bf16[64,128,128]{2,1,0:T(8,128)(2,1)} async-done(((bf16[8,128,128]{2,1,0:T(8,128)(2,1)}), bf16[64,128,128]{2,1,0:T(8,128)(2,1)}) %all-gather.5.cloned.1.call-update) | async-done | bytes 2097168 | tf_op jit(solution)/shard_map/all_gather | solution.py:23
  210.8 12.7 %while.50 = (s32[]{:T(128)}, f32[8,128,128]{2,1,0:T(8,128)S(1)}, s32[]{:T(128)}, bf16[8,8,128,128]{3,2,1,0:T(8,128)(2,1)}, bf16[8,8,128,128]{3,2,1,0:T(8,128)(2,1)}, /*index=5*/s32[]{:T(128)}, s32[]{:T(128)}) while((s32[]{:T(128)}, f32[8,128,128]{2,1,0:T(8,128)S(1)}, s32[]{:T(128)}, bf16[8,8,128,128]{3,2,1,0:T(8,128)(2,1)}, ...), condition=%wide.region_12.14_spmd.clone, body=%wide.region_11.13_spmd.clone.sunk | while | flops 201981952 | bytes 3148383 | solution.py:40
  210.9 1.5 fusion.152
  212.5 1.5 fusion.152
  214.1 1.5 fusion.152
  215.7 1.5 fusion.152
  217.3 1.5 fusion.152
  218.9 1.5 fusion.152
  220.5 1.5 fusion.152
  222.1 1.5 fusion.152
  223.6 7.3 %while.48 = (s32[]{:T(128)}, f32[8,128,128]{2,1,0:T(8,128)S(1)}, f32[2,8,64,128]{3,2,1,0:T(8,128)}, f32[2,8]{1,0:T(2,128)S(1)}, f32[2,8,64,128]{3,2,1,0:T(8,128)...) while((s32[]{:T(128)}, f32[8,128,128]{2,1,0:T(8,128)S(1)}, ...), condition=%wide.region_15.17_spmd, body=%wide.region_14.16_spmd.sunk | while | flops 352780288 | bytes 9186037 | solution.py:219
  230.9 1.3 multiply_reduce_fusion
  232.3 1.4 copy.108
  233.9 3.9 %fusion.43 = bf16[2048,128]{0,1:T(8,128)(2,1)} fusion(bf16[1024,2048]{1,0:T(8,128)(2,1)} %param.33, bf16[128,1024]{1,0:T(8,128)(2,1)S(1)} %copy-done.5, f32[16,8,8,128]{3,2,1,0:T(8,128)S(1)} %bitcast.190, f32[16,8,8,128]{3,2,1,0:T(8,128)S(1)} %bitcast.191, f32[1024]{0:T(1024)S(1)} %broadcast_bitcast_fusion), kind=kOutput, calls=%fused_computation.56 | convolution fusion | flops 538312704 | bytes 6033408 | tf_op jit(solution)/shard_map/dot_general | solution.py:234
  237.8 20.3 %reduce-scatter.2.cloned.1.call-done = bf16[512,128]{0,1:T(8,128)(2,1)} async-done(((bf16[2048,128]{0,1:T(8,128)(2,1)}), bf16[512,128]{0,1:T(8,128)(2,1)}) %reduce-scatter.2.cloned.1.call-update) | async-done | bytes 131088 | tf_op jit(solution)/shard_map/reduce_scatter | solution.py:233
  258.1 1.7 copy.111
  (133 shorter events, 31.4 us)
Async XLA Ops:
  6.5 109.3 %copy-start = (f32[128]{0:T(128)S(1)}, f32[128]{0:T(128)}, u32[]{:S(2)}) copy-start(f32[128]{0:T(128)} %param.31) | copy-start | bytes 1540
  6.5 154.4 %all-gather.7.cloned.1.call-start = ((), (), s32[]{:S(2)}) async-start(), calls=%async_computation.3 | async-start | bytes 2359296 | tf_op jit(solution)/shard_map/all_gather | solution.py:23
  8.7 13.2 %collective-permute-start = (bf16[3,2048]{1,0:T(4,128)(2,1)S(1)}, bf16[3,2048]{1,0:T(4,128)(2,1)S(1)}, u32[]{:S(2)}, u32[]{:S(2)}) collective-permute-start(bf16[3,2048]{1,0:T(4,128)(2,1)S(1)} %pad_maximum_fusion), channel_id=1, source_target_pairs={{0,4},{4,8},{8,12},{12,16},{16,20},{20,24},{24,28},{1,5},{5,9},{9,... | collective-permute-start | bytes 36872 | tf_op jit(solution)/shard_map/ppermute | solution.py:17
  23.4 80.2 %copy-start.4 = (bf16[128,1024]{1,0:T(8,128)(2,1)S(1)}, bf16[128,1024]{1,0:T(8,128)(2,1)}, u32[]{:S(2)}) copy-start(bf16[128,1024]{1,0:T(8,128)(2,1)} %param.24) | copy-start | bytes 786436
  24.0 81.5 %copy-start.1 = (f32[128,4,2,128]{3,0,2,1:T(8,128)}, f32[128,4,2,128]{3,0,2,1:T(8,128)S(1)}, u32[]{:S(2)}) copy-start(f32[128,4,2,128]{3,0,2,1:T(8,128)S(1)} %broadcast_in_dim.112) | copy-start | bytes 1572868
  111.2 99.7 %all-gather.5.cloned.1.call-start = ((), (), s32[]{:S(2)}) async-start(), calls=%async_computation.2 | async-start | bytes 2359296 | tf_op jit(solution)/shard_map/all_gather | solution.py:23
  115.6 142.5 %reduce-scatter.2.cloned.1.call-start = ((), (), s32[]{:S(2)}) async-start(), calls=%async_computation.1 | async-start | bytes 655360 | tf_op jit(solution)/shard_map/reduce_scatter | solution.py:233
  223.6 1.3 copy-start.2
  225.3 0.8 copy-start.3
  227.3 1.3 copy-start.2
  229.0 0.8 copy-start.3
  230.9 3.0 %copy-start.5 = (bf16[128,1024]{1,0:T(8,128)(2,1)S(1)}, bf16[128,1024]{1,0:T(8,128)(2,1)}, u32[]{:S(2)}) copy-start(bf16[128,1024]{1,0:T(8,128)(2,1)} %param.25) | copy-start | bytes 786436
Sparse Core Ops, SparseCore 0:
  111.3 49.5 all-gather.6
  163.0 47.7 all-gather.4
  237.9 20.1 reduce-scatter.1
where the time goes:
time: 267 us; the launch traced here: 266 us
  waiting for transfers between devices  113 us (42%)
  other arithmetic  88.6 us (33%)
  matrix products  33.6 us (13%)
  between operations  13.5 us (5%)
  local copies, waits for them, and re-layouts  12.2 us (5%)
  starting transfers between devices  5.14 us (2%)
    all_gather x2, waiting for transfers between devices, carried_in(): lax.all_gather(part.astype(kind), axis)  92.3 us
    another operation x3, other arithmetic, span_terms(): lax.linalg.triangular_solve(lower_part, (beta_values * head_start)[:, :,...  78.7 us
    reduce_scatter x1, waiting for transfers between devices, body(): lax.psum_scatter(lax.dot_general(out_weight, mixed_rows, (((0,), (1,)), (...  20.3 us
    dot_general x8, matrix products, compose(): jnp.einsum('hij,hjk->hik', later[0], earlier[1], precision=PRECISE)  12.2 us
  transfers between devices with their start and end apart: 4, of which 3 were waited for; matrix products, arithmetic and copies ran while one was open for 6% of the time, Pallas kernels for 0%

commit v1 on v0

v1 whole, which is shorter than its diff:
```python
import jax
import jax.numpy as jnp
from jax import lax
from jax.experimental import pallas as pl
from jax.experimental.pallas import tpu as pltpu
from jax.sharding import PartitionSpec as P

DK = 128
DV = 128
EDGE = 16
F32 = jnp.float32
BF16 = jnp.bfloat16
VMEM_LIMIT = 48 * 1024 * 1024


def dot(a, b):
    return jnp.dot(a.astype(BF16), b.astype(BF16), preferred_element_type=F32)


def exact_dot(a, b):
    return jnp.dot(a, b, precision=lax.Precision.HIGHEST, preferred_element_type=F32)


def where_y(flag, a, b):
    return jnp.where(flag == 1, a, b)


def three_terms(value):
    high = value.astype(BF16)
    rest = value - high.astype(F32)
    middle = rest.astype(BF16)
    low = (rest - middle.astype(F32)).astype(BF16)
    return high, middle, low


def pack_kernel(q_ref, k_ref, v_ref, g_ref, decay_ref, beta_ref, pack_ref, edge_ref, own_edge_ref, gate_ref):
    y = lax.axis_index("ctx") % 2
    rows, key_width = q_ref.shape
    value_width = v_ref.shape[1]
    hk, hv = key_width // 2, value_width // 2
    heads = decay_ref.shape[0] // 2
    parts = ((q_ref, 0, hk), (k_ref, hk, hk), (v_ref, 2 * hk, hv))
    for ref, at, width in parts:
        other = where_y(y, ref[:, :width], ref[:, width:])
        pack_ref[0:rows, at : at + width] = other
        edge_ref[:, at : at + width] = other[rows - EDGE :]
        own_edge_ref[:, at : at + width] = where_y(y, ref[rows - EDGE :, width:], ref[rows - EDGE :, :width])
    gate_ref[...] = where_y(y, g_ref[:, :hv], g_ref[:, hv:])
    pack_ref[rows : rows + EDGE, :] = jnp.zeros((EDGE, pack_ref.shape[1]), BF16)
    at = 0
    for ref in (decay_ref, beta_ref):
        for term in three_terms(where_y(y, ref[0:heads], ref[heads:])):
            pack_ref[rows : rows + heads, at : at + rows] = term
            at += rows


def document_counts(doc_ref, base, rows):
    down = lax.broadcasted_iota(jnp.int32, (rows + 8, rows), 0) + (base - 8)
    along = lax.broadcasted_iota(jnp.int32, (8, rows), 1) + base
    docs = doc_ref.shape[0]

    def one(d, carried):
        start, count_down, count_along = carried
        count_down = count_down + (down >= start).astype(jnp.int32)
        count_along = count_along + (along >= start).astype(jnp.int32)
        return start + doc_ref[d], count_down, count_along

    state = (jnp.int32(0), jnp.zeros_like(down), jnp.zeros_like(along))
    if docs <= 16:
        for d in range(docs):
            state = one(d, state)
    else:
        state = lax.fori_loop(0, docs, one, state)
    return state[1], state[2]


def conv_silu(halo, current, weight, keeps):
    rows = current.shape[0]
    padded = jnp.concatenate([halo.astype(F32)[EDGE - 8 :], current.astype(F32)], axis=0)
    margin = weight.shape[0] - 1
    summed = weight[margin : margin + 1] * padded[8:]
    for lag in range(1, margin + 1):
        summed = summed + weight[margin - lag : margin - lag + 1] * padded[8 - lag : 8 - lag + rows] * keeps[lag]
    return summed / (1.0 + jnp.exp(-summed))


def unit(vectors):
    return vectors * lax.rsqrt(jnp.sum(vectors * vectors, axis=-1, keepdims=True) + 1e-6)


def block_terms(doc_ref, base, halo, q, k, v, weights, decay, beta_raw):
    rows = decay.shape[1]
    heads = decay.shape[0]
    key_heads = heads // 2
    seg_down, seg_along = document_counts(doc_ref, base, rows)
    seg = seg_down[8:]
    keeps = [None] + [(seg_down[8 - lag : 8 - lag + rows] == seg).astype(F32) for lag in (1, 2, 3)]
    before = seg_down[7:8]
    last = seg_down[rows + 7 : rows + 8]
    row = lax.broadcasted_iota(jnp.int32, (rows, rows), 0)
    col = lax.broadcasted_iota(jnp.int32, (rows, rows), 1)
    same = (seg == seg_along[0:1]) & (row >= col)

    log_gamma = -(jnp.maximum(decay, 0.0) + jnp.log1p(jnp.exp(-jnp.abs(decay))))
    beta = 1.0 / (1.0 + jnp.exp(-beta_raw))
    padded_gamma = jnp.concatenate([log_gamma, jnp.zeros((8 - heads, rows), F32)], axis=0)
    upper = (row <= col).astype(F32)
    sums = exact_dot(padded_gamma, upper)
    stacked = jnp.concatenate([sums[:heads], beta, jnp.zeros((rows - 2 * heads, rows), F32)], axis=0)
    columns = stacked.T

    queries = [unit(conv_silu(halo(0, g), q(g), weights(0, g), keeps)) for g in range(key_heads)]
    keys = [unit(conv_silu(halo(1, g), k(g), weights(1, g), keeps)) for g in range(key_heads)]
    values = [conv_silu(halo(2, g), v(g), weights(2, g), keeps) for g in range(heads)]
    keys_t = [key.T for key in keys]
    keys_t16 = [key.astype(BF16) for key in keys_t]
    grams = [dot(key, key_t) for key, key_t in zip(keys, keys_t16)]
    scores = [dot(query, key_t) for query, key_t in zip(queries, keys_t16)]

    lower, inside, rhs, starts, ends, throughs = [], [], [], [], [], []
    for h in range(heads):
        g = h // 2
        down = jnp.broadcast_to(columns[:, h : h + 1], (rows, rows))
        beta_down = jnp.broadcast_to(columns[:, heads + h : heads + h + 1], (rows, rows))
        along = sums[h : h + 1]
        end = jnp.broadcast_to(columns[rows - 1 : rows, h : h + 1], (1, rows))
        decays = jnp.exp(jnp.where(same, down - along, -1e30))
        lower.append(jnp.where(row > col, beta_down * grams[g] * decays, 0.0))
        inside.append((scores[g] * decays).astype(BF16))
        start = jnp.where(seg == before, jnp.exp(down), 0.0)
        starts.append((queries[g] * start).astype(BF16))
        rhs.append(
            jnp.concatenate([(beta_down * values[h]).astype(BF16), (beta_down * start * keys[g]).astype(BF16)], axis=1)
        )
        ends.append((keys_t[g] * jnp.where(seg_along[0:1] == last, jnp.exp(end - along), 0.0)).astype(BF16))
        throughs.append(jnp.where(last == before, jnp.exp(end), 0.0))

    small = 16
    eye = (row == col).astype(F32)
    power = [jnp.where(row // small == col // small, -x, 0.0) for x in lower]
    inverse = [eye + x for x in power]
    power = [x.astype(BF16) for x in power]
    reach = 2
    while reach < small:
        power = [dot(x, x).astype(BF16) for x in power]
        inverse = [x + dot(x, p) for x, p in zip(inverse, power)]
        reach *= 2
    reach = small
    while reach < rows:
        here = (row // (2 * reach) == col // (2 * reach)) & (row // reach != col // reach)
        moved = [dot(jnp.where(here, x, 0.0), i) for x, i in zip(lower, inverse)]
        inverse = [i - dot(i, m) for i, m in zip(inverse, moved)]
        reach *= 2
    solved = [dot(i, r).astype(BF16) for i, r in zip(inverse, rhs)]
    ended = [dot(e, s) for e, s in zip(ends, solved)]
    states = [e[:, :DV] for e in ended]
    maps = [t * eye - e[:, DV:] for t, e in zip(throughs, ended)]
    return states, maps, inside, solved, starts


def own_kernel(doc_ref, q_ref, k_ref, v_ref, cq_ref, ck_ref, cv_ref, decay_ref, beta_ref, halo_ref,
               state_ref, map_ref, out_ref, through_ref):
    ctx = lax.axis_index("ctx")
    y = ctx % 2
    rows = q_ref.shape[0]
    heads = decay_ref.shape[0] // 2
    widths = (q_ref.shape[1] // 2, k_ref.shape[1] // 2, v_ref.shape[1] // 2)
    at = (0, widths[0], widths[0] + widths[1])

    def half(ref, which, g):
        low = slice(g * 128, g * 128 + 128)
        high = slice(widths[which] + g * 128, widths[which] + g * 128 + 128)
        return where_y(y, ref[:, high], ref[:, low])

    weight_refs = (cq_ref, ck_ref, cv_ref)
    states, maps, inside, solved, starts = block_terms(
        doc_ref,
        ctx * rows,
        lambda which, g: halo_ref[:, at[which] + g * 128 : at[which] + g * 128 + 128],
        lambda g: half(q_ref, 0, g),
        lambda g: half(k_ref, 1, g),
        lambda g: half(v_ref, 2, g),
        lambda which, g: half(weight_refs[which], which, g),
        where_y(y, decay_ref[heads:], decay_ref[:heads]),
        where_y(y, beta_ref[heads:], beta_ref[:heads]),
    )
    results = [dot(i, s) for i, s in zip(inside, solved)]
    for h in range(heads):
        state_ref[h] = states[h]
        map_ref[h] = maps[h].astype(BF16)
        out_ref[:, h * DV : h * DV + DV] = results[h][:, :DV]
        through_ref[:, h * DK : h * DK + DK] = (starts[h].astype(F32) - results[h][:, DV:]).astype(BF16)


def peer_kernel(hops, doc_ref, pack_ref, own_edge_ref, edge_ref, cq_ref, ck_ref, cv_ref, own_state_ref, own_map_ref,
                state_ref, map_ref, inside_ref, solved_ref, start_ref, end_ref, *pair_map_ref):
    ctx = lax.axis_index("ctx")
    y = ctx % 2
    rows = pack_ref.shape[0] - EDGE
    heads = own_state_ref.shape[0]
    widths = (cq_ref.shape[1] // 2, ck_ref.shape[1] // 2, cv_ref.shape[1] // 2)
    at = (0, widths[0], widths[0] + widths[1])
    weight_refs = (cq_ref, ck_ref, cv_ref)

    def columns(which, g):
        return slice(at[which] + g * 128, at[which] + g * 128 + 128)

    def weights(which, g):
        ref, low = weight_refs[which], g * 128
        return where_y(y, ref[:, widths[which] + low : widths[which] + low + 128], ref[:, low : low + 128])

    gates = [
        sum(pack_ref[rows : rows + heads, (3 * part + i) * rows : (3 * part + i + 1) * rows].astype(F32) for i in range(3))
        for part in range(2)
    ]
    states, maps, inside, solved, starts = block_terms(
        doc_ref,
        (ctx + 1 - 2 * y) * rows,
        lambda which, g: where_y(y, edge_ref[:, columns(which, g)], own_edge_ref[:, columns(which, g)]),
        lambda g: pack_ref[0:rows, columns(0, g)],
        lambda g: pack_ref[0:rows, columns(1, g)],
        lambda g: pack_ref[0:rows, columns(2, g)],
        weights,
        gates[0],
        gates[1],
    )
    for h in range(heads):
        own_state, own_map = own_state_ref[h], own_map_ref[h]
        maps16 = maps[h].astype(BF16)
        state_0, state_1 = where_y(y, states[h], own_state), where_y(y, own_state, states[h])
        map_0, map_1 = where_y(y, maps16, own_map), where_y(y, own_map, maps16)
        end_ref[h] = (state_1 + dot(map_1, state_0)).astype(BF16)
        if hops > 1:
            pair_map_ref[0][h] = dot(map_1, map_0).astype(BF16)
    for h in range(heads):
        state_ref[h] = states[h]
        map_ref[h] = maps[h].astype(BF16)
        inside_ref[h] = inside[h]
        solved_ref[h] = solved[h]
        start_ref[:, h * DK : h * DK + DK] = starts[h]


def local_kernel(own_state_ref, own_map_ref, own_out_ref, own_through_ref, state_ref, map_ref, inside_ref, solved_ref,
                 start_ref, out_ref, through_ref):
    y = lax.axis_index("ctx") % 2
    rows = own_out_ref.shape[0]
    heads = own_state_ref.shape[0]
    results = [dot(inside_ref[h], solved_ref[h]) for h in range(heads)]
    for h in range(heads):
        lanes = slice(h * DV, h * DV + DV)
        own_out, own_through = own_out_ref[:, lanes], own_through_ref[:, lanes]
        out = results[h][:, :DV]
        through = (start_ref[:, lanes].astype(F32) - results[h][:, DV:]).astype(BF16)
        state_0 = where_y(y, state_ref[h], own_state_ref[h]).astype(BF16)
        map_0 = where_y(y, map_ref[h], own_map_ref[h])
        through_1 = where_y(y, own_through, through)
        more = dot(through_1, jnp.concatenate([state_0, map_0], axis=1))
        extra, moved = more[:, :DV], more[:, DV:].astype(BF16)
        out_ref[0:rows, lanes] = own_out + where_y(y, extra, jnp.zeros_like(extra))
        out_ref[rows:, lanes] = out + where_y(y, jnp.zeros_like(extra), extra)
        through_ref[0:rows, lanes] = where_y(y, moved, own_through)
        through_ref[rows:, lanes] = where_y(y, through, moved)


def project_kernel(out_ref, through_ref, enter_ref, gate_ref, peer_gate_ref, gain_ref, weight_ref, send_ref, keep_ref,
                   weight_vmem, sems):
    y = lax.axis_index("ctx") % 2
    head = lax.axis_index("head")
    core, x = head % 2, head // 2
    heads = enter_ref.shape[0]
    rows = gate_ref.shape[0]
    depth = weight_vmem.shape[1]
    width = weight_vmem.shape[2]
    copies = []
    for i, (c, xx) in enumerate(((1 - core, x), (1 - core, 1 - x), (core, x), (core, 1 - x))):
        copies.append(
            pltpu.make_async_copy(
                weight_ref.at[
                    pl.ds(pl.multiple_of(y * depth, depth), depth),
                    pl.ds(pl.multiple_of((xx * 2 + c) * width, width), width),
                ],
                weight_vmem.at[i],
                sems.at[i],
            )
        )
    for copy in copies:
        copy.start()
    mixed = []
    for h in range(heads):
        lanes = slice(h * DV, h * DV + DV)
        high = slice(heads * DV + h * DV, heads * DV + h * DV + DV)
        o = out_ref[:, lanes] + dot(through_ref[:, lanes], enter_ref[h])
        gate = jnp.concatenate([where_y(y, gate_ref[:, high], gate_ref[:, lanes]), peer_gate_ref[:, lanes]], axis=0)
        gate = gate.astype(F32)
        scale = lax.rsqrt(jnp.mean(o * o, axis=-1, keepdims=True) + 1e-6)
        mixed.append((o * scale * gain_ref[...] * (gate / (1.0 + jnp.exp(-gate)))).astype(BF16))
    mixed = jnp.concatenate(mixed, axis=1)
    for i, copy in enumerate(copies):
        copy.wait()
        to_ref = (send_ref, keep_ref)[i // 2]
        to_ref[:, (i % 2) * width : (i % 2 + 1) * width] = jnp.dot(
            mixed, weight_vmem[i], preferred_element_type=F32
        ).astype(BF16)


def core_sum_kernel(keep_ref, got_ref, mine_ref, x_ref, y_ref, xy_ref):
    rows, width = mine_ref.shape
    for ref, r, c in ((xy_ref, 1, 1), (x_ref, 0, 1), (y_ref, 1, 0), (mine_ref, 0, 0)):
        at = (slice(r * rows, r * rows + rows), slice(c * width, c * width + width))
        ref[...] = (keep_ref[at].astype(F32) + got_ref[at].astype(F32)).astype(ref.dtype)


def last_kernel(mine_ref, x_ref, y_ref, xy_ref, out_ref):
    total = mine_ref[...] + x_ref[...].astype(F32) + (y_ref[...].astype(F32) + xy_ref[...].astype(F32))
    out_ref[...] = total.T.astype(BF16)


def call(kernel, outs, args, name, smem=0, any_space=(), scratch=(), flops=0, moved=0):
    space = [
        pl.BlockSpec(memory_space=pltpu.SMEM if i < smem else pl.ANY if i in any_space else pltpu.VMEM)
        for i in range(len(args))
    ]
    return pl.pallas_call(
        kernel,
        out_shape=[jax.ShapeDtypeStruct(shape, kind) for shape, kind in outs],
        in_specs=space,
        out_specs=[pl.BlockSpec(memory_space=pltpu.VMEM)] * len(outs),
        scratch_shapes=list(scratch),
        compiler_params=pltpu.CompilerParams(vmem_limit_bytes=VMEM_LIMIT),
        cost_estimate=pl.CostEstimate(flops=flops, bytes_accessed=moved, transcendentals=0),
        name=name,
    )(*args)


def body(
    query_in,
    key_in,
    value_in,
    gate_in,
    conv_query,
    conv_key,
    conv_value,
    decay_in,
    beta_in,
    norm_gain,
    doc_lengths,
    out_weight,
):
    rows = query_in.shape[0]
    ctx_count, head_count = lax.axis_size("ctx"), lax.axis_size("head")
    heads = decay_in.shape[0] // 2
    half_width = query_in.shape[1] + value_in.shape[1] // 2
    value_width = value_in.shape[1] // 2
    width = out_weight.shape[1] // head_count
    longest = ctx_count * rows // 4
    hops = -(-(longest - 1) // (2 * rows))

    swap = [(i, i ^ 1) for i in range(ctx_count)]
    ahead_1 = [(i, (i + 1) % ctx_count) for i in range(ctx_count)]
    ahead_2 = [(i, (i + 2) % ctx_count) for i in range(ctx_count)]

    pack, edge, own_edge, gate_out = call(
        pack_kernel,
        [((rows + EDGE, half_width), BF16), ((EDGE, half_width), BF16), ((EDGE, half_width), BF16), ((rows, value_width), BF16)],
        (query_in, key_in, value_in, gate_in, decay_in, beta_in),
        "pack",
    )
    got_edge = lax.ppermute(edge, "ctx", ahead_1)
    got_far_edge = lax.ppermute(own_edge, "ctx", ahead_2)
    got_pack = lax.ppermute(pack, "ctx", swap)

    square = (heads, DK, DV)
    own_state, own_map, own_out, own_through = call(
        own_kernel,
        [(square, F32), (square, BF16), ((rows, value_width), F32), ((rows, value_width), BF16)],
        (doc_lengths, query_in, key_in, value_in, conv_query, conv_key, conv_value, decay_in, beta_in, got_edge),
        "own_terms",
        smem=1,
        flops=2_000_000_000,
        moved=4_000_000,
    )
    peer = call(
        lambda *refs: peer_kernel(hops, *refs),
        [
            (square, F32),
            (square, BF16),
            ((heads, rows, rows), BF16),
            ((heads, rows, DK + DV), BF16),
            ((rows, value_width), BF16),
            (square, BF16),
        ]
        + ([(square, BF16)] if hops > 1 else []),
        (doc_lengths, got_pack, own_edge, got_far_edge, conv_query, conv_key, conv_value, own_state, own_map),
        "peer_terms",
        smem=1,
        flops=2_000_000_000,
        moved=4_000_000,
    )
    state, map_, inside, solved, start, end = peer[:6]
    gate_out, end = lax.optimization_barrier((gate_out, end))
    entering = lax.ppermute(end, "ctx", ahead_2)
    for _ in range(hops - 1):
        moved = jnp.einsum("hij,hjk->hik", peer[6], entering, preferred_element_type=F32)
        entering = lax.ppermute((end.astype(F32) + moved).astype(BF16), "ctx", ahead_2)
    got_gate = lax.ppermute(gate_out, "ctx", swap)
    out, through = call(
        local_kernel,
        [((2 * rows, value_width), F32), ((2 * rows, value_width), BF16)],
        (own_state, own_map, own_out, own_through, state, map_, inside, solved, start),
        "local_outputs",
        flops=1_000_000_000,
        moved=4_000_000,
    )
    send, keep = call(
        project_kernel,
        [((2 * rows, 2 * width), BF16), ((2 * rows, 2 * width), BF16)],
        (out, through, entering, gate_in, got_gate, norm_gain.reshape(1, DV), out_weight),
        "project",
        any_space=(6,),
        scratch=(pltpu.VMEM((4, value_width, width), BF16), pltpu.SemaphoreType.DMA((4,))),
    )
    got = lax.ppermute(send, "head", [(i, i ^ 1) for i in range(head_count)])
    mine, to_x, to_y, to_xy = call(
        core_sum_kernel,
        [((rows, width), F32), ((rows, width), BF16), ((rows, width), BF16), ((rows, width), BF16)],
        (keep, got),
        "core_sum",
    )
    both = [
        (c * head_count + h, (c ^ 1) * head_count + (h ^ 2)) for c in range(ctx_count) for h in range(head_count)
    ]
    got_xy = lax.ppermute(to_xy, ("ctx", "head"), both)
    got_x = lax.ppermute(to_x, "head", [(i, i ^ 2) for i in range(head_count)])
    got_y = lax.ppermute(to_y, "ctx", swap)
    (projected,) = call(
        last_kernel, [((width, rows), BF16)], (mine, got_x, got_y, got_xy), "last_sum"
    )
    return projected


def solution(mesh):
    return jax.shard_map(
        body,
        mesh=mesh,
        in_specs=(
            P("ctx", "head"),
            P("ctx", "head"),
            P("ctx", "head"),
            P("ctx", "head"),
            P(None, "head"),
            P(None, "head"),
            P(None, "head"),
            P("head", "ctx"),
            P("head", "ctx"),
            P(),
            P(),
            P("head", None),
        ),
        out_specs=P("head", "ctx"),
        check_vma=False,
    )
```

time: 267 us -> 49.5 us (0.19)
  waiting for transfers between devices: 113 us -> 15.7 us
  other arithmetic: 88.6 us -> 0 us
  matrix products: 33.6 us -> 0 us
  between operations: 13.5 us -> 0.12 us
  Pallas kernels: 0 us -> 10.8 us
  starting transfers between devices: 5.14 us -> 13.1 us
  local copies, waits for them, and re-layouts: 12.2 us -> 9.24 us
    all_gather x2 -> x0, waiting for transfers between devices: 92.3 us -> none  [carried_in(): lax.all_gather(part.astype(kind), axis)]
    another operation x11 -> x0, other arithmetic: 80.1 us -> none  [the longest x3 78.7 us: span_terms(): lax.linalg.triangular_solve(lower_part, (beta_values * head_start)[:, :,...]
    dot_general x27 -> x0, matrix products: 31.4 us -> none  [the longest x8 12.2 us: compose(): jnp.einsum('hij,hjk->hik', later[0], earlier[1], precision=PRECISE)]
    reduce_scatter x1 -> x0, waiting for transfers between devices: 20.3 us -> none  [body(): lax.psum_scatter(lax.dot_general(out_weight, mixed_rows, (((0,), (1,)), (...]
    ppermute x1 -> x9, waiting for transfers between devices: 0.01 us -> 15.7 us  [the longest x1 4.89 us: body(): got_edge = lax.ppermute(edge, 'ctx', ahead_1)]
    pallas_call x0 -> x7, Pallas kernels: none -> 10.8 us  [call(): pl.pallas_call(kernel, out_shape=[jax.ShapeDtypeStruct(shape, kind) for s...]
    unnamed x9 -> x32, local copies, waits for them, and re-layouts: 0.12 us -> 9.24 us
    ppermute x1 -> x9, starting transfers between devices: 4.87 us -> 13.1 us  [the longest x1 3.03 us: body(): got_pack = lax.ppermute(pack, 'ctx', swap)]
  transfers between devices with their start and end apart: 4 -> 9, of which waited for: 3 -> 7; matrix products, arithmetic and copies ran while one was open for 6% -> 0% of each run, Pallas kernels for 0% -> 8%
where the time goes in v1:
time: 49.5 us; the launch traced here: 49 us
  waiting for transfers between devices  15.7 us (32%)
  starting transfers between devices  13.1 us (26%)
  Pallas kernels  10.8 us (22%)
  local copies, waits for them, and re-layouts  9.24 us (19%)
    pallas_call x7, Pallas kernels, call(): pl.pallas_call(kernel, out_shape=[jax.ShapeDtypeStruct(shape, kind) for s...  10.8 us
    unnamed x32, local copies, waits for them, and re-layouts  9.24 us
    ppermute x1, waiting for transfers between devices, body(): got_edge = lax.ppermute(edge, 'ctx', ahead_1)  4.89 us
    ppermute x1, waiting for transfers between devices, body(): got_y = lax.ppermute(to_y, 'ctx', swap)  3.81 us
    ppermute x1, starting transfers between devices, body(): got_pack = lax.ppermute(pack, 'ctx', swap)  3.03 us
    ppermute x1, starting transfers between devices, body(): got_gate = lax.ppermute(gate_out, 'ctx', swap)  2.47 us
    ppermute x1, waiting for transfers between devices, body(): entering = lax.ppermute(end, 'ctx', ahead_2)  2.35 us
    ppermute x1, starting transfers between devices, body(): got_y = lax.ppermute(to_y, 'ctx', swap)  2.26 us
  transfers between devices with their start and end apart: 9, of which 7 were waited for; matrix products, arithmetic and copies ran while one was open for 0% of the time, Pallas kernels for 8%

profile of v1, /device:TPU:0, one launch (start us, length us, event | category | flops | bytes accessed | tf_op | source)
XLA Modules:
  0.0 49.0 jit_solution(11392650518250335172)
XLA Ops:
  0.0 0.9 %copy-done = bf16[128,1024]{1,0:T(8,128)(2,1)S(1)} copy-done((bf16[128,1024]{1,0:T(8,128)(2,1)S(1)}, bf16[128,1024]{1,0:T(8,128)(2,1)}, u32[]{:S(2)}) %copy-start) | copy-done | bytes 262168
  1.0 0.9 %copy-done.2 = bf16[128,1024]{1,0:T(8,128)(2,1)S(1)} copy-done((bf16[128,1024]{1,0:T(8,128)(2,1)S(1)}, bf16[128,1024]{1,0:T(8,128)(2,1)}, u32[]{:S(2)}) %copy-start.2) | copy-done | bytes 262168
  1.9 0.9 %copy-done.3 = bf16[128,512]{1,0:T(8,128)(2,1)S(1)} copy-done((bf16[128,512]{1,0:T(8,128)(2,1)S(1)}, bf16[128,512]{1,0:T(8,128)(2,1)}, u32[]{:S(2)}) %copy-start.3) | copy-done | bytes 131096
  2.8 0.9 %copy-done.4 = bf16[128,512]{1,0:T(8,128)(2,1)S(1)} copy-done((bf16[128,512]{1,0:T(8,128)(2,1)S(1)}, bf16[128,512]{1,0:T(8,128)(2,1)}, u32[]{:S(2)}) %copy-start.4) | copy-done | bytes 131096
  4.4 0.7 %copy-done.7 = f32[8,128]{1,0:T(8,128)S(1)} copy-done((f32[8,128]{1,0:T(8,128)S(1)}, f32[8,128]{1,0:T(8,128)}, u32[]{:S(2)}) %copy-start.7) | copy-done | bytes 4120
  5.2 3.0 %collective-permute-start.1 = (bf16[144,1024]{1,0:T(8,128)(2,1)S(1)}, bf16[144,1024]{1,0:T(8,128)(2,1)S(1)}, u32[]{:S(2)}, u32[]{:S(2)}) collective-permute-start(bf16[144,1024]{1,0:T(8,128)(2,1)S(1)} %get-tuple-element.34), channel_id=1, source_target_pairs={{0,4},{4,0},{8,12},{12,8},{16,20},{20,16},{24,28},{28,24},{1,5},{5... | collective-permute-start | bytes 884744 | tf_op jit(solution)/shard_map/ppermute | solution.py:370
  8.3 2.0 %collective-permute-start.2 = (bf16[16,1024]{1,0:T(8,128)(2,1)S(1)}, bf16[16,1024]{1,0:T(8,128)(2,1)S(1)}, u32[]{:S(2)}, u32[]{:S(2)}) collective-permute-start(bf16[16,1024]{1,0:T(8,128)(2,1)S(1)} %get-tuple-element.35.refs_2_), channel_id=1, source_target_pairs={{0,8},{4,12},{8,16},{12,20},{16,24},{20,28},{24,0},{28,4},{1,9},{5... | collective-permute-start | bytes 98312 | tf_op jit(solution)/shard_map/ppermute | solution.py:369
  10.3 4.9 %collective-permute-done.halo_ref = bf16[16,1024]{1,0:T(8,128)(2,1)S(1)} collective-permute-done((bf16[16,1024]{1,0:T(8,128)(2,1)S(1)}, bf16[16,1024]{1,0:T(8,128)(2,1)S(1)}, u32[]{:S(2)}, u32[]{:S(2)}) %collective-permute-start) | collective-permute-done | bytes 32800 | tf_op jit(solution)/shard_map/ppermute | solution.py:368
  16.5 0.7 %copy-done.10 = f32[4,1024]{1,0:T(4,128)S(1)} copy-done((f32[4,1024]{1,0:T(4,128)S(1)}, f32[4,1024]{1,0:T(4,128)}, u32[]{:S(2)}) %copy-start.10) | copy-done | bytes 16408
  17.2 0.7 %copy-done.12 = f32[4,512]{1,0:T(4,128)S(1)} copy-done((f32[4,512]{1,0:T(4,128)S(1)}, f32[4,512]{1,0:T(4,128)}, u32[]{:S(2)}) %copy-start.12) | copy-done | bytes 8216
  17.9 0.7 %copy-done.13 = f32[4,512]{1,0:T(4,128)S(1)} copy-done((f32[4,512]{1,0:T(4,128)S(1)}, f32[4,512]{1,0:T(4,128)}, u32[]{:S(2)}) %copy-start.13) | copy-done | bytes 8216
  19.3 3.4 %own_terms.1 = (f32[4,128,128]{2,1,0:T(8,128)S(1)}, bf16[4,128,128]{2,1,0:T(8,128)(2,1)S(1)}, f32[128,512]{1,0:T(8,128)S(1)}, bf16[128,512]{1,0:T(8,128)(2,1)S(1)}) custom-call(s32[16]{0:T(128)S(1)} %copy-done.15, bf16[128,512]{1,0:T(8,128)(2,1)S(1)} %copy-done.3, bf16[128,512]{1,0:T(8,128)(2,1)S(1)} %copy-done.4, bf16[128,1024]{1,0:T(8,128)(2,1)S(1)} %copy-done.2, ...), custom_call_target="tpu_custom_call" | custom-call | flops 2000000000 | bytes 4000000 | tf_op jit(solution)/shard_map/own_terms/pallas_call | solution.py:323
  22.8 3.5 %peer_terms.1 = (f32[4,128,128]{2,1,0:T(8,128)S(1)}, bf16[4,128,128]{2,1,0:T(8,128)(2,1)S(1)}, bf16[4,128,128]{2,1,0:T(8,128)(2,1)S(1)}, bf16[4,128,256]{2,1,0:T...) custom-call(s32[16]{0:T(128)S(1)} %copy-done.15, ...), custom_call_target="tpu_custom_call" | custom-call | flops 2000000000 | bytes 4000000 | tf_op jit(solution)/shard_map/peer_terms/pallas_call | solution.py:323
  26.3 1.6 %collective-permute-start.3 = (bf16[4,128,128]{2,1,0:T(8,128)(2,1)S(1)}, bf16[4,128,128]{2,1,0:T(8,128)(2,1)S(1)}, u32[]{:S(2)}, u32[]{:S(2)}) collective-permute-start(bf16[4,128,128]{2,1,0:T(8,128)(2,1)S(1)} %get-tuple-element.45), channel_id=1, source_target_pairs={{0,8},{4,12},{8,16},{12,20},{16,24},{20,28},{24,0},{28,4},{1,9},{5... | collective-permute-start | bytes 393224 | tf_op jit(solution)/shard_map/ppermute | solution.py:401
  27.9 2.5 %collective-permute-start.4 = (bf16[128,512]{1,0:T(8,128)(2,1)S(1)}, bf16[128,512]{1,0:T(8,128)(2,1)S(1)}, u32[]{:S(2)}, u32[]{:S(2)}) collective-permute-start(bf16[128,512]{1,0:T(8,128)(2,1)S(1)} %get-tuple-element.46), channel_id=1, source_target_pairs={{0,4},{4,0},{8,12},{12,8},{16,20},{20,16},{24,28},{28,24},{1,5},{5... | collective-permute-start | bytes 393224 | tf_op jit(solution)/shard_map/ppermute | solution.py:405
  30.8 2.4 %collective-permute-done.3.enter_ref = bf16[4,128,128]{2,1,0:T(8,128)(2,1)S(1)} collective-permute-done((bf16[4,128,128]{2,1,0:T(8,128)(2,1)S(1)}, bf16[4,128,128]{2,1,0:T(8,128)(2,1)S(1)}, u32[]{:S(2)}, u32[]{:S(2)}) %collective-permute-start.3) | collective-permute-done | bytes 131104 | tf_op jit(solution)/shard_map/ppermute | solution.py:401
  33.4 2.5 %project.1 = (bf16[256,1024]{1,0:T(8,128)(2,1)S(1)}, bf16[256,1024]{1,0:T(8,128)(2,1)S(1)}) custom-call(f32[256,512]{1,0:T(8,128)S(1)} %get-tuple-element.41.out_ref, bf16[256,512]{1,0:T(8,128)(2,1)S(1)} %get-tuple-element.42.through_ref, bf16[4,128,128]{2,1,0:T(8,128)(2,1)S(1)} %collective-permute-done.3.enter_ref, bf16[128,1024]{1,0:T(8,128)(2,1)S(1)} %copy-done.1, ...), custom_call_target="tpu_custom_call" | custom-call | tf_op jit(solution)/shard_map/project/pallas_call | solution.py:323
  36.0 1.9 %collective-permute-done.5.got_ref = bf16[256,1024]{1,0:T(8,128)(2,1)S(1)} collective-permute-done((bf16[256,1024]{1,0:T(8,128)(2,1)S(1)}, bf16[256,1024]{1,0:T(8,128)(2,1)S(1)}, u32[]{:S(2)}, u32[]{:S(2)}) %collective-permute-start.5) | collective-permute-done | bytes 524320 | tf_op jit(solution)/shard_map/ppermute | solution.py:422
  38.0 1.6 %collective-permute-start.6 = (bf16[128,512]{1,0:T(8,128)(2,1)S(1)}, bf16[128,512]{1,0:T(8,128)(2,1)S(1)}, u32[]{:S(2)}, u32[]{:S(2)}) collective-permute-start(bf16[128,512]{1,0:T(8,128)(2,1)S(1)} %get-tuple-element.50), channel_id=1, source_target_pairs={{0,2},{1,3},{2,0},{3,1},{4,6},{5,7},{6,4},{7,5},{8,10},{9,11},{10,... | collective-permute-start | bytes 393224 | tf_op jit(solution)/shard_map/ppermute | solution.py:433
  39.6 2.3 %collective-permute-start.7 = (bf16[128,512]{1,0:T(8,128)(2,1)S(1)}, bf16[128,512]{1,0:T(8,128)(2,1)S(1)}, u32[]{:S(2)}, u32[]{:S(2)}) collective-permute-start(bf16[128,512]{1,0:T(8,128)(2,1)S(1)} %get-tuple-element.51), channel_id=1, source_target_pairs={{0,4},{4,0},{8,12},{12,8},{16,20},{20,16},{24,28},{28,24},{1,5},{5... | collective-permute-start | bytes 393224 | tf_op jit(solution)/shard_map/ppermute | solution.py:434
  41.8 1.8 %collective-permute-done.6.x_ref = bf16[128,512]{1,0:T(8,128)(2,1)S(1)} collective-permute-done((bf16[128,512]{1,0:T(8,128)(2,1)S(1)}, bf16[128,512]{1,0:T(8,128)(2,1)S(1)}, u32[]{:S(2)}, u32[]{:S(2)}) %collective-permute-start.6) | collective-permute-done | bytes 131104 | tf_op jit(solution)/shard_map/ppermute | solution.py:433
  43.6 3.8 %collective-permute-done.7.y_ref = bf16[128,512]{1,0:T(8,128)(2,1)S(1)} collective-permute-done((bf16[128,512]{1,0:T(8,128)(2,1)S(1)}, bf16[128,512]{1,0:T(8,128)(2,1)S(1)}, u32[]{:S(2)}, u32[]{:S(2)}) %collective-permute-start.7) | collective-permute-done | bytes 131104 | tf_op jit(solution)/shard_map/ppermute | solution.py:434
  47.4 0.7 %collective-permute-done.8.xy_ref = bf16[128,512]{1,0:T(8,128)(2,1)S(1)} collective-permute-done((bf16[128,512]{1,0:T(8,128)(2,1)S(1)}, bf16[128,512]{1,0:T(8,128)(2,1)S(1)}, u32[]{:S(2)}, u32[]{:S(2)}) %collective-permute-start.8) | collective-permute-done | bytes 131104 | tf_op jit(solution)/shard_map/ppermute | solution.py:432
  48.2 0.8 %last_sum.1 = bf16[512,128]{1,0:T(8,128)(2,1)} custom-call(f32[128,512]{1,0:T(8,128)S(1)} %get-tuple-element.49.mine_ref, bf16[128,512]{1,0:T(8,128)(2,1)S(1)} %collective-permute-done.6.x_ref, bf16[128,512]{1,0:T(8,128)(2,1)S(1)} %collective-permute-done.7.y_ref, bf16[128,512]{1,0:T(8,128)(2,1)S(1)} %collective-permute-done.8.xy_ref), custom_call_target="tpu_custom_call" | custom-call | tf_op jit(solution)/shard_map/last_sum/pallas_call | solution.py:323
  (33 shorter events, 3.7 us)
Async XLA Ops:
  0.0 0.9 %copy-start = (bf16[128,1024]{1,0:T(8,128)(2,1)S(1)}, bf16[128,1024]{1,0:T(8,128)(2,1)}, u32[]{:S(2)}) copy-start(bf16[128,1024]{1,0:T(8,128)(2,1)} %gate_ref.1) | copy-start | bytes 786436
  1.0 0.9 %copy-start.2 = (bf16[128,1024]{1,0:T(8,128)(2,1)S(1)}, bf16[128,1024]{1,0:T(8,128)(2,1)}, u32[]{:S(2)}) copy-start(bf16[128,1024]{1,0:T(8,128)(2,1)} %v_ref.3) | copy-start | bytes 786436
  1.9 0.9 %copy-start.3 = (bf16[128,512]{1,0:T(8,128)(2,1)S(1)}, bf16[128,512]{1,0:T(8,128)(2,1)}, u32[]{:S(2)}) copy-start(bf16[128,512]{1,0:T(8,128)(2,1)} %q_ref.3) | copy-start | bytes 393220
  2.8 0.9 %copy-start.4 = (bf16[128,512]{1,0:T(8,128)(2,1)S(1)}, bf16[128,512]{1,0:T(8,128)(2,1)}, u32[]{:S(2)}) copy-start(bf16[128,512]{1,0:T(8,128)(2,1)} %k_ref.3) | copy-start | bytes 393220
  3.7 0.7 %copy-start.5 = (f32[8,128]{1,0:T(8,128)S(1)}, f32[8,128]{1,0:T(8,128)}, u32[]{:S(2)}) copy-start(f32[8,128]{1,0:T(8,128)} %decay_ref.3) | copy-start | bytes 12292
  4.4 0.7 %copy-start.7 = (f32[8,128]{1,0:T(8,128)S(1)}, f32[8,128]{1,0:T(8,128)}, u32[]{:S(2)}) copy-start(f32[8,128]{1,0:T(8,128)} %beta_ref.3) | copy-start | bytes 12292
  5.1 17.7 %copy-start.11 = (f32[4,1024]{1,0:T(4,128)S(1)}, f32[4,1024]{1,0:T(4,128)}, u32[]{:S(2)}) copy-start(f32[4,1024]{1,0:T(4,128)} %refs_6_.1) | copy-start | bytes 49156
  5.1 17.7 %copy-start.14 = (f32[4,512]{1,0:T(4,128)S(1)}, f32[4,512]{1,0:T(4,128)}, u32[]{:S(2)}) copy-start(f32[4,512]{1,0:T(4,128)} %refs_5_.1) | copy-start | bytes 24580
  5.2 17.6 %collective-permute-start.1 = (bf16[144,1024]{1,0:T(8,128)(2,1)S(1)}, bf16[144,1024]{1,0:T(8,128)(2,1)S(1)}, u32[]{:S(2)}, u32[]{:S(2)}) collective-permute-start(bf16[144,1024]{1,0:T(8,128)(2,1)S(1)} %get-tuple-element.34), channel_id=1, source_target_pairs={{0,4},{4,0},{8,12},{12,8},{16,20},{20,16},{24,28},{28,24},{1,5},{5... | collective-permute-start | bytes 884744 | tf_op jit(solution)/shard_map/ppermute | solution.py:370
  8.2 7.0 %collective-permute-start = (bf16[16,1024]{1,0:T(8,128)(2,1)S(1)}, bf16[16,1024]{1,0:T(8,128)(2,1)S(1)}, u32[]{:S(2)}, u32[]{:S(2)}) collective-permute-start(bf16[16,1024]{1,0:T(8,128)(2,1)S(1)} %get-tuple-element.29), channel_id=1, source_target_pairs={{0,4},{4,8},{8,12},{12,16},{16,20},{20,24},{24,28},{28,0},{1,5},{5... | collective-permute-start | bytes 98312 | tf_op jit(solution)/shard_map/ppermute | solution.py:368
  8.3 14.5 %collective-permute-start.2 = (bf16[16,1024]{1,0:T(8,128)(2,1)S(1)}, bf16[16,1024]{1,0:T(8,128)(2,1)S(1)}, u32[]{:S(2)}, u32[]{:S(2)}) collective-permute-start(bf16[16,1024]{1,0:T(8,128)(2,1)S(1)} %get-tuple-element.35.refs_2_), channel_id=1, source_target_pairs={{0,8},{4,12},{8,16},{12,20},{16,24},{20,28},{24,0},{28,4},{1,9},{5... | collective-permute-start | bytes 98312 | tf_op jit(solution)/shard_map/ppermute | solution.py:369
  15.2 0.7 %copy-start.6 = (f32[8,128]{1,0:T(8,128)S(1)}, f32[8,128]{1,0:T(8,128)}, u32[]{:S(2)}) copy-start(f32[8,128]{1,0:T(8,128)} %decay_ref.3) | copy-start | bytes 12292
  15.8 0.7 %copy-start.8 = (f32[8,128]{1,0:T(8,128)S(1)}, f32[8,128]{1,0:T(8,128)}, u32[]{:S(2)}) copy-start(f32[8,128]{1,0:T(8,128)} %beta_ref.3) | copy-start | bytes 12292
  16.5 0.7 %copy-start.10 = (f32[4,1024]{1,0:T(4,128)S(1)}, f32[4,1024]{1,0:T(4,128)}, u32[]{:S(2)}) copy-start(f32[4,1024]{1,0:T(4,128)} %refs_6_.1) | copy-start | bytes 49156
  17.2 0.7 %copy-start.12 = (f32[4,512]{1,0:T(4,128)S(1)}, f32[4,512]{1,0:T(4,128)}, u32[]{:S(2)}) copy-start(f32[4,512]{1,0:T(4,128)} %refs_4_.1) | copy-start | bytes 24580
  17.9 0.7 %copy-start.13 = (f32[4,512]{1,0:T(4,128)S(1)}, f32[4,512]{1,0:T(4,128)}, u32[]{:S(2)}) copy-start(f32[4,512]{1,0:T(4,128)} %refs_5_.1) | copy-start | bytes 24580
  22.8 10.6 %copy-start.1 = (bf16[128,1024]{1,0:T(8,128)(2,1)S(1)}, bf16[128,1024]{1,0:T(8,128)(2,1)}, u32[]{:S(2)}) copy-start(bf16[128,1024]{1,0:T(8,128)(2,1)} %gate_ref.1) | copy-start | bytes 786436
  22.8 10.6 %copy-start.9 = (f32[128]{0:T(128)S(1)}, f32[128]{0:T(128)}, u32[]{:S(2)}) copy-start(f32[128]{0:T(128)} %param.21) | copy-start | bytes 1540
  26.3 6.8 %collective-permute-start.3 = (bf16[4,128,128]{2,1,0:T(8,128)(2,1)S(1)}, bf16[4,128,128]{2,1,0:T(8,128)(2,1)S(1)}, u32[]{:S(2)}, u32[]{:S(2)}) collective-permute-start(bf16[4,128,128]{2,1,0:T(8,128)(2,1)S(1)} %get-tuple-element.45), channel_id=1, source_target_pairs={{0,8},{4,12},{8,16},{12,20},{16,24},{20,28},{24,0},{28,4},{1,9},{5... | collective-permute-start | bytes 393224 | tf_op jit(solution)/shard_map/ppermute | solution.py:401
  27.9 5.4 %collective-permute-start.4 = (bf16[128,512]{1,0:T(8,128)(2,1)S(1)}, bf16[128,512]{1,0:T(8,128)(2,1)S(1)}, u32[]{:S(2)}, u32[]{:S(2)}) collective-permute-start(bf16[128,512]{1,0:T(8,128)(2,1)S(1)} %get-tuple-element.46), channel_id=1, source_target_pairs={{0,4},{4,0},{8,12},{12,8},{16,20},{20,16},{24,28},{28,24},{1,5},{5... | collective-permute-start | bytes 393224 | tf_op jit(solution)/shard_map/ppermute | solution.py:405
  35.9 2.0 %collective-permute-start.5 = (bf16[256,1024]{1,0:T(8,128)(2,1)S(1)}, bf16[256,1024]{1,0:T(8,128)(2,1)S(1)}, u32[]{:S(2)}, u32[]{:S(2)}) collective-permute-start(bf16[256,1024]{1,0:T(8,128)(2,1)S(1)} %get-tuple-element.48), channel_id=1, source_target_pairs={{0,1},{1,0},{2,3},{3,2},{4,5},{5,4},{6,7},{7,6},{8,9},{9,8},{10,11... | collective-permute-start | bytes 1572872 | tf_op jit(solution)/shard_map/ppermute | solution.py:422
  38.0 5.6 %collective-permute-start.6 = (bf16[128,512]{1,0:T(8,128)(2,1)S(1)}, bf16[128,512]{1,0:T(8,128)(2,1)S(1)}, u32[]{:S(2)}, u32[]{:S(2)}) collective-permute-start(bf16[128,512]{1,0:T(8,128)(2,1)S(1)} %get-tuple-element.50), channel_id=1, source_target_pairs={{0,2},{1,3},{2,0},{3,1},{4,6},{5,7},{6,4},{7,5},{8,10},{9,11},{10,... | collective-permute-start | bytes 393224 | tf_op jit(solution)/shard_map/ppermute | solution.py:433
  39.6 7.8 %collective-permute-start.7 = (bf16[128,512]{1,0:T(8,128)(2,1)S(1)}, bf16[128,512]{1,0:T(8,128)(2,1)S(1)}, u32[]{:S(2)}, u32[]{:S(2)}) collective-permute-start(bf16[128,512]{1,0:T(8,128)(2,1)S(1)} %get-tuple-element.51), channel_id=1, source_target_pairs={{0,4},{4,0},{8,12},{12,8},{16,20},{20,16},{24,28},{28,24},{1,5},{5... | collective-permute-start | bytes 393224 | tf_op jit(solution)/shard_map/ppermute | solution.py:434
  41.8 6.3 %collective-permute-start.8 = (bf16[128,512]{1,0:T(8,128)(2,1)S(1)}, bf16[128,512]{1,0:T(8,128)(2,1)S(1)}, u32[]{:S(2)}, u32[]{:S(2)}) collective-permute-start(bf16[128,512]{1,0:T(8,128)(2,1)S(1)} %get-tuple-element.52), channel_id=1, source_target_pairs={{0,6},{1,7},{2,4},{3,5},{4,2},{5,3},{6,0},{7,1},{8,14},{9,15},{10,... | collective-permute-start | bytes 393224 | tf_op jit(solution)/shard_map/ppermute | solution.py:432
  (1 other events, 0.7 us)

commit v2 on v1

--- a/solution.py
+++ b/solution.py
@@ -33,25 +33,50 @@
     return high, middle, low
 
 
-def pack_kernel(q_ref, k_ref, v_ref, g_ref, decay_ref, beta_ref, pack_ref, edge_ref, own_edge_ref, gate_ref):
+def pack_kernel(q_ref, k_ref, v_ref, g_ref, cq_ref, ck_ref, cv_ref, decay_ref, beta_ref,
+                edge_ref, own_edge_ref, pack_ref, gate_ref, own_ref, weight_ref, gates_ref, own_gate_ref,
+                raw_gates, sems):
     y = lax.axis_index("ctx") % 2
-    rows, key_width = q_ref.shape
-    value_width = v_ref.shape[1]
-    hk, hv = key_width // 2, value_width // 2
+    rows = q_ref.shape[0]
     heads = decay_ref.shape[0] // 2
-    parts = ((q_ref, 0, hk), (k_ref, hk, hk), (v_ref, 2 * hk, hv))
-    for ref, at, width in parts:
-        other = where_y(y, ref[:, :width], ref[:, width:])
-        pack_ref[0:rows, at : at + width] = other
-        edge_ref[:, at : at + width] = other[rows - EDGE :]
-        own_edge_ref[:, at : at + width] = where_y(y, ref[rows - EDGE :, width:], ref[rows - EDGE :, :width])
-    gate_ref[...] = where_y(y, g_ref[:, :hv], g_ref[:, hv:])
+    started = []
+
+    def copy(source, target):
+        one = pltpu.make_async_copy(source, target, sems.at[len(started)])
+        one.start()
+        started.append(one)
+
+    def columns(ref, which):
+        width = ref.shape[1] // 2
+        return pl.ds(pl.multiple_of(which * width, width), width)
+
+    copy(decay_ref, raw_gates.at[0])
+    copy(beta_ref, raw_gates.at[1])
+    at = 0
+    for ref, weights in ((q_ref, cq_ref), (k_ref, ck_ref), (v_ref, cv_ref)):
+        width = ref.shape[1] // 2
+        here = pl.ds(at, width)
+        tail = pl.ds(rows - EDGE, EDGE)
+        copy(ref.at[tail, columns(ref, 1 - y)], edge_ref.at[:, here])
+        copy(ref.at[tail, columns(ref, y)], own_edge_ref.at[:, here])
+        copy(ref.at[:, columns(ref, 1 - y)], pack_ref.at[pl.ds(0, rows), here])
+        copy(ref.at[:, columns(ref, y)], own_ref.at[:, here])
+        copy(weights.at[:, columns(ref, y)], weight_ref.at[:, here])
+        at += width
+    copy(g_ref.at[:, columns(g_ref, 1 - y)], gate_ref)
+    copy(g_ref.at[:, columns(g_ref, y)], own_gate_ref)
     pack_ref[rows : rows + EDGE, :] = jnp.zeros((EDGE, pack_ref.shape[1]), BF16)
+    started[0].wait()
+    started[1].wait()
     at = 0
-    for ref in (decay_ref, beta_ref):
-        for term in three_terms(where_y(y, ref[0:heads], ref[heads:])):
+    for i in range(2):
+        raw = raw_gates[i]
+        gates_ref[i * heads : i * heads + heads] = where_y(y, raw[heads:], raw[:heads])
+        for term in three_terms(where_y(y, raw[:heads], raw[heads:])):
             pack_ref[rows : rows + heads, at : at + rows] = term
             at += rows
+    for one in started[2:]:
+        one.wait()
 
 
 def document_counts(doc_ref, base, rows):
@@ -158,31 +183,29 @@
     return states, maps, inside, solved, starts
 
 
-def own_kernel(doc_ref, q_ref, k_ref, v_ref, cq_ref, ck_ref, cv_ref, decay_ref, beta_ref, halo_ref,
-               state_ref, map_ref, out_ref, through_ref):
-    ctx = lax.axis_index("ctx")
-    y = ctx % 2
-    rows = q_ref.shape[0]
-    heads = decay_ref.shape[0] // 2
-    widths = (q_ref.shape[1] // 2, k_ref.shape[1] // 2, v_ref.shape[1] // 2)
-    at = (0, widths[0], widths[0] + widths[1])
-
-    def half(ref, which, g):
-        low = slice(g * 128, g * 128 + 128)
-        high = slice(widths[which] + g * 128, widths[which] + g * 128 + 128)
-        return where_y(y, ref[:, high], ref[:, low])
-
-    weight_refs = (cq_ref, ck_ref, cv_ref)
+def groups(heads):
+    at = (0, heads // 2 * DK, heads * DK)
+    return lambda which, g: slice(at[which] + g * 128, at[which] + g * 128 + 128)
+
+
+def own_kernel(doc_hbm, own_ref, weight_ref, gates_ref, halo_ref,
+               state_ref, map_ref, out_ref, through_ref, doc_ref, sem):
+    copy = pltpu.make_async_copy(doc_hbm, doc_ref, sem)
+    copy.start()
+    copy.wait()
+    rows = own_ref.shape[0]
+    heads = gates_ref.shape[0] // 2
+    columns = groups(heads)
     states, maps, inside, solved, starts = block_terms(
         doc_ref,
-        ctx * rows,
-        lambda which, g: halo_ref[:, at[which] + g * 128 : at[which] + g * 128 + 128],
-        lambda g: half(q_ref, 0, g),
-        lambda g: half(k_ref, 1, g),
-        lambda g: half(v_ref, 2, g),
-        lambda which, g: half(weight_refs[which], which, g),
-        where_y(y, decay_ref[heads:], decay_ref[:heads]),
-        where_y(y, beta_ref[heads:], beta_ref[:heads]),
+        lax.axis_index("ctx") * rows,
+        lambda which, g: halo_ref[:, columns(which, g)],
+        lambda g: own_ref[:, columns(0, g)],
+        lambda g: own_ref[:, columns(1, g)],
+        lambda g: own_ref[:, columns(2, g)],
+        lambda which, g: weight_ref[:, columns(which, g)],
+        gates_ref[0:heads],
+        gates_ref[heads:],
     )
     results = [dot(i, s) for i, s in zip(inside, solved)]
     for h in range(heads):
@@ -192,23 +215,17 @@
         through_ref[:, h * DK : h * DK + DK] = (starts[h].astype(F32) - results[h][:, DV:]).astype(BF16)
 
 
-def peer_kernel(hops, doc_ref, pack_ref, own_edge_ref, edge_ref, cq_ref, ck_ref, cv_ref, own_state_ref, own_map_ref,
-                state_ref, map_ref, inside_ref, solved_ref, start_ref, end_ref, *pair_map_ref):
+def peer_kernel(doc_hbm, pack_ref, own_edge_ref, edge_ref, weight_ref, own_state_ref, own_map_ref,
+                state_ref, map_ref, inside_ref, solved_ref, start_ref, end_ref, *rest):
+    *pair_map_ref, doc_ref, sem = rest
+    copy = pltpu.make_async_copy(doc_hbm, doc_ref, sem)
+    copy.start()
+    copy.wait()
     ctx = lax.axis_index("ctx")
     y = ctx % 2
     rows = pack_ref.shape[0] - EDGE
     heads = own_state_ref.shape[0]
-    widths = (cq_ref.shape[1] // 2, ck_ref.shape[1] // 2, cv_ref.shape[1] // 2)
-    at = (0, widths[0], widths[0] + widths[1])
-    weight_refs = (cq_ref, ck_ref, cv_ref)
-
-    def columns(which, g):
-        return slice(at[which] + g * 128, at[which] + g * 128 + 128)
-
-    def weights(which, g):
-        ref, low = weight_refs[which], g * 128
-        return where_y(y, ref[:, widths[which] + low : widths[which] + low + 128], ref[:, low : low + 128])
-
+    columns = groups(heads)
     gates = [
         sum(pack_ref[rows : rows + heads, (3 * part + i) * rows : (3 * part + i + 1) * rows].astype(F32) for i in range(3))
         for part in range(2)
@@ -220,7 +237,7 @@
         lambda g: pack_ref[0:rows, columns(0, g)],
         lambda g: pack_ref[0:rows, columns(1, g)],
         lambda g: pack_ref[0:rows, columns(2, g)],
-        weights,
+        lambda which, g: weight_ref[:, columns(which, g)],
         gates[0],
         gates[1],
     )
@@ -230,7 +247,7 @@
         state_0, state_1 = where_y(y, states[h], own_state), where_y(y, own_state, states[h])
         map_0, map_1 = where_y(y, maps16, own_map), where_y(y, own_map, maps16)
         end_ref[h] = (state_1 + dot(map_1, state_0)).astype(BF16)
-        if hops > 1:
+        if pair_map_ref:
             pair_map_ref[0][h] = dot(map_1, map_0).astype(BF16)
     for h in range(heads):
         state_ref[h] = states[h]
@@ -241,8 +258,18 @@
 
 
 def local_kernel(own_state_ref, own_map_ref, own_out_ref, own_through_ref, state_ref, map_ref, inside_ref, solved_ref,
-                 start_ref, out_ref, through_ref):
+                 start_ref, weight_hbm, out_ref, through_ref, weight_ref, sems):
     y = lax.axis_index("ctx") % 2
+    head = lax.axis_index("head")
+    core, x = head % 2, head // 2
+    depth, width = weight_ref.shape[1:]
+    copies = []
+    for i, (c, xx) in enumerate(((1 - core, x), (1 - core, 1 - x), (core, x), (core, 1 - x))):
+        source = weight_hbm.at[
+            pl.ds(pl.multiple_of(y * depth, depth), depth), pl.ds(pl.multiple_of((xx * 2 + c) * width, width), width)
+        ]
+        copies.append(pltpu.make_async_copy(source, weight_ref.at[i], sems.at[i]))
+        copies[-1].start()
     rows = own_out_ref.shape[0]
     heads = own_state_ref.shape[0]
     results = [dot(inside_ref[h], solved_ref[h]) for h in range(heads)]
@@ -260,46 +287,25 @@
         out_ref[rows:, lanes] = out + where_y(y, jnp.zeros_like(extra), extra)
         through_ref[0:rows, lanes] = where_y(y, moved, own_through)
         through_ref[rows:, lanes] = where_y(y, through, moved)
-
-
-def project_kernel(out_ref, through_ref, enter_ref, gate_ref, peer_gate_ref, gain_ref, weight_ref, send_ref, keep_ref,
-                   weight_vmem, sems):
-    y = lax.axis_index("ctx") % 2
-    head = lax.axis_index("head")
-    core, x = head % 2, head // 2
+    for copy in copies:
+        copy.wait()
+
+
+def project_kernel(out_ref, through_ref, enter_ref, gate_ref, peer_gate_ref, gain_ref, weight_ref, send_ref, keep_ref):
     heads = enter_ref.shape[0]
-    rows = gate_ref.shape[0]
-    depth = weight_vmem.shape[1]
-    width = weight_vmem.shape[2]
-    copies = []
-    for i, (c, xx) in enumerate(((1 - core, x), (1 - core, 1 - x), (core, x), (core, 1 - x))):
-        copies.append(
-            pltpu.make_async_copy(
-                weight_ref.at[
-                    pl.ds(pl.multiple_of(y * depth, depth), depth),
-                    pl.ds(pl.multiple_of((xx * 2 + c) * width, width), width),
-                ],
-                weight_vmem.at[i],
-                sems.at[i],
-            )
-        )
-    for copy in copies:
-        copy.start()
+    width = weight_ref.shape[2]
     mixed = []
     for h in range(heads):
         lanes = slice(h * DV, h * DV + DV)
-        high = slice(heads * DV + h * DV, heads * DV + h * DV + DV)
         o = out_ref[:, lanes] + dot(through_ref[:, lanes], enter_ref[h])
-        gate = jnp.concatenate([where_y(y, gate_ref[:, high], gate_ref[:, lanes]), peer_gate_ref[:, lanes]], axis=0)
-        gate = gate.astype(F32)
+        gate = jnp.concatenate([gate_ref[:, lanes], peer_gate_ref[:, lanes]], axis=0).astype(F32)
         scale = lax.rsqrt(jnp.mean(o * o, axis=-1, keepdims=True) + 1e-6)
         mixed.append((o * scale * gain_ref[...] * (gate / (1.0 + jnp.exp(-gate)))).astype(BF16))
     mixed = jnp.concatenate(mixed, axis=1)
-    for i, copy in enumerate(copies):
-        copy.wait()
+    for i in range(4):
         to_ref = (send_ref, keep_ref)[i // 2]
         to_ref[:, (i % 2) * width : (i % 2 + 1) * width] = jnp.dot(
-            mixed, weight_vmem[i], preferred_element_type=F32
+            mixed, weight_ref[i], preferred_element_type=F32
         ).astype(BF16)
 
 
@@ -315,11 +321,9 @@
     out_ref[...] = total.T.astype(BF16)
 
 
-def call(kernel, outs, args, name, smem=0, any_space=(), scratch=(), flops=0, moved=0):
-    space = [
-        pl.BlockSpec(memory_space=pltpu.SMEM if i < smem else pl.ANY if i in any_space else pltpu.VMEM)
-        for i in range(len(args))
-    ]
+def call(kernel, outs, args, name, hbm=(), scratch=(), flops=0, moved=0):
+    space = [pl.BlockSpec(memory_space=pltpu.HBM if i in hbm else pltpu.VMEM) for i in range(len(args))]
+    args = [pltpu.with_memory_space_constraint(arg, pltpu.HBM) if i in hbm else arg for i, arg in enumerate(args)]
     return pl.pallas_call(
         kernel,
         out_shape=[jax.ShapeDtypeStruct(shape, kind) for shape, kind in outs],
@@ -359,28 +363,41 @@
     ahead_1 = [(i, (i + 1) % ctx_count) for i in range(ctx_count)]
     ahead_2 = [(i, (i + 2) % ctx_count) for i in range(ctx_count)]
 
-    pack, edge, own_edge, gate_out = call(
+    edge, own_edge, pack, gate_out, own, weights, gates, own_gate = call(
         pack_kernel,
-        [((rows + EDGE, half_width), BF16), ((EDGE, half_width), BF16), ((EDGE, half_width), BF16), ((rows, value_width), BF16)],
-        (query_in, key_in, value_in, gate_in, decay_in, beta_in),
+        [
+            ((EDGE, half_width), BF16),
+            ((EDGE, half_width), BF16),
+            ((rows + EDGE, half_width), BF16),
+            ((rows, value_width), BF16),
+            ((rows, half_width), BF16),
+            ((conv_query.shape[0], half_width), F32),
+            ((2 * heads, rows), F32),
+            ((rows, value_width), BF16),
+        ],
+        (query_in, key_in, value_in, gate_in, conv_query, conv_key, conv_value, decay_in, beta_in),
         "pack",
+        hbm=range(9),
+        scratch=(pltpu.VMEM((2,) + decay_in.shape, F32), pltpu.SemaphoreType.DMA((19,))),
     )
     got_edge = lax.ppermute(edge, "ctx", ahead_1)
     got_far_edge = lax.ppermute(own_edge, "ctx", ahead_2)
     got_pack = lax.ppermute(pack, "ctx", swap)
 
     square = (heads, DK, DV)
+    docs = (pltpu.SMEM(doc_lengths.shape, jnp.int32), pltpu.SemaphoreType.DMA)
     own_state, own_map, own_out, own_through = call(
         own_kernel,
         [(square, F32), (square, BF16), ((rows, value_width), F32), ((rows, value_width), BF16)],
-        (doc_lengths, query_in, key_in, value_in, conv_query, conv_key, conv_value, decay_in, beta_in, got_edge),
+        (doc_lengths, own, weights, gates, got_edge),
         "own_terms",
-        smem=1,
+        hbm=(0,),
+        scratch=docs,
         flops=2_000_000_000,
         moved=4_000_000,
     )
     peer = call(
-        lambda *refs: peer_kernel(hops, *refs),
+        peer_kernel,
         [
             (square, F32),
             (square, BF16),
@@ -390,9 +407,10 @@
             (square, BF16),
         ]
         + ([(square, BF16)] if hops > 1 else []),
-        (doc_lengths, got_pack, own_edge, got_far_edge, conv_query, conv_key, conv_value, own_state, own_map),
+        (doc_lengths, got_pack, own_edge, got_far_edge, weights, own_state, own_map),
         "peer_terms",
-        smem=1,
+        hbm=(0,),
+        scratch=docs,
         flops=2_000_000_000,
         moved=4_000_000,
     )
@@ -403,21 +421,21 @@
         moved = jnp.einsum("hij,hjk->hik", peer[6], entering, preferred_element_type=F32)
         entering = lax.ppermute((end.astype(F32) + moved).astype(BF16), "ctx", ahead_2)
     got_gate = lax.ppermute(gate_out, "ctx", swap)
-    out, through = call(
+    out, through, weight = call(
         local_kernel,
-        [((2 * rows, value_width), F32), ((2 * rows, value_width), BF16)],
-        (own_state, own_map, own_out, own_through, state, map_, inside, solved, start),
+        [((2 * rows, value_width), F32), ((2 * rows, value_width), BF16), ((4, value_width, width), BF16)],
+        (own_state, own_map, own_out, own_through, state, map_, inside, solved, start, out_weight),
         "local_outputs",
+        hbm=(9,),
+        scratch=(pltpu.SemaphoreType.DMA((4,)),),
         flops=1_000_000_000,
         moved=4_000_000,
     )
     send, keep = call(
         project_kernel,
         [((2 * rows, 2 * width), BF16), ((2 * rows, 2 * width), BF16)],
-        (out, through, entering, gate_in, got_gate, norm_gain.reshape(1, DV), out_weight),
+        (out, through, entering, own_gate, got_gate, norm_gain.reshape(1, DV), weight),
         "project",
-        any_space=(6,),
-        scratch=(pltpu.VMEM((4, value_width, width), BF16), pltpu.SemaphoreType.DMA((4,))),
     )
     got = lax.ppermute(send, "head", [(i, i ^ 1) for i in range(head_count)])
     mine, to_x, to_y, to_xy = call(

time: 49.5 us -> 40 us (0.81)
  local copies, waits for them, and re-layouts: 9.24 us -> 0.01 us
  Pallas kernels: 10.8 us -> 12.4 us
  waiting for transfers between devices: 15.7 us -> 14.3 us
    unnamed x32 -> x2, local copies, waits for them, and re-layouts: 9.24 us -> 0.01 us
    pallas_call x7, Pallas kernels: 10.8 us -> 12.4 us  [call(): pl.pallas_call(kernel, out_shape=[jax.ShapeDtypeStruct(shape, kind) for s...]
    ppermute x1, waiting for transfers between devices: 2.35 us -> 0.91 us  [body(): entering = lax.ppermute(end, 'ctx', ahead_2)]
  transfers between devices with their start and end apart: 9 -> 9, of which waited for: 7 -> 7; matrix products, arithmetic and copies ran while one was open for 0% -> 0% of each run, Pallas kernels for 8% -> 13%
where the time goes in v2:
time: 40 us; the launch traced here: 39.9 us
  waiting for transfers between devices  14.3 us (36%)
  starting transfers between devices  13.1 us (33%)
  Pallas kernels  12.4 us (31%)
    pallas_call x7, Pallas kernels, call(): pl.pallas_call(kernel, out_shape=[jax.ShapeDtypeStruct(shape, kind) for s...  12.4 us
    ppermute x1, waiting for transfers between devices, body(): got_edge = lax.ppermute(edge, 'ctx', ahead_1)  4.89 us
    ppermute x1, waiting for transfers between devices, body(): got_y = lax.ppermute(to_y, 'ctx', swap)  3.79 us
    ppermute x1, starting transfers between devices, body(): got_pack = lax.ppermute(pack, 'ctx', swap)  3.03 us
    ppermute x1, starting transfers between devices, body(): got_gate = lax.ppermute(gate_out, 'ctx', swap)  2.48 us
    ppermute x1, starting transfers between devices, body(): got_y = lax.ppermute(to_y, 'ctx', swap)  2.26 us
    ppermute x1, starting transfers between devices, body(): got_far_edge = lax.ppermute(own_edge, 'ctx', ahead_2)  2.02 us
    ppermute x1, waiting for transfers between devices, body(): got = lax.ppermute(send, 'head', [(i, i ^ 1) for i in range(head_count)])  1.9 us
  transfers between devices with their start and end apart: 9, of which 7 were waited for; matrix products, arithmetic and copies ran while one was open for 0% of the time, Pallas kernels for 13%

profile of v2, /device:TPU:0, one launch (start us, length us, event | category | flops | bytes accessed | tf_op | source)
XLA Modules:
  0.0 39.9 jit_solution(8409747703997203974)
XLA Ops:
  0.0 1.5 %pack.1 = (bf16[16,1024]{1,0:T(8,128)(2,1)S(1)}, bf16[16,1024]{1,0:T(8,128)(2,1)S(1)}, bf16[144,1024]{1,0:T(8,128)(2,1)S(1)}, bf16[128,512]{1,0:T(8,128)(2,1)S(1...) custom-call(bf16[128,512]{1,0:T(8,128)(2,1)} %q_ref.1, ...), custom_call_target="tpu_custom_call" | custom-call | tf_op jit(solution)/shard_map/pack/pallas_call | solution.py:327
  1.5 3.0 %collective-permute-start.1 = (bf16[144,1024]{1,0:T(8,128)(2,1)S(1)}, bf16[144,1024]{1,0:T(8,128)(2,1)S(1)}, u32[]{:S(2)}, u32[]{:S(2)}) collective-permute-start(bf16[144,1024]{1,0:T(8,128)(2,1)S(1)} %get-tuple-element.42), channel_id=1, source_target_pairs={{0,4},{4,0},{8,12},{12,8},{16,20},{20,16},{24,28},{28,24},{1,5},{5... | collective-permute-start | bytes 884744 | tf_op jit(solution)/shard_map/ppermute | solution.py:385
  4.5 0.1 collective-permute-start
  4.6 2.0 %collective-permute-start.2 = (bf16[16,1024]{1,0:T(8,128)(2,1)S(1)}, bf16[16,1024]{1,0:T(8,128)(2,1)S(1)}, u32[]{:S(2)}, u32[]{:S(2)}) collective-permute-start(bf16[16,1024]{1,0:T(8,128)(2,1)S(1)} %get-tuple-element.43.own_edge_ref), channel_id=1, source_target_pairs={{0,8},{4,12},{8,16},{12,20},{16,24},{20,28},{24,0},{28,4},{1,9},{5... | collective-permute-start | bytes 98312 | tf_op jit(solution)/shard_map/ppermute | solution.py:384
  6.6 4.9 %collective-permute-done.halo_ref = bf16[16,1024]{1,0:T(8,128)(2,1)S(1)} collective-permute-done((bf16[16,1024]{1,0:T(8,128)(2,1)S(1)}, bf16[16,1024]{1,0:T(8,128)(2,1)S(1)}, u32[]{:S(2)}, u32[]{:S(2)}) %collective-permute-start) | collective-permute-done | bytes 32800 | tf_op jit(solution)/shard_map/ppermute | solution.py:383
  11.5 3.6 %own_terms.1 = (f32[4,128,128]{2,1,0:T(8,128)S(1)}, bf16[4,128,128]{2,1,0:T(8,128)(2,1)S(1)}, f32[128,512]{1,0:T(8,128)S(1)}, bf16[128,512]{1,0:T(8,128)(2,1)S(1)}) custom-call(s32[16]{0:T(128)} %doc_hbm.3, bf16[128,1024]{1,0:T(8,128)(2,1)S(1)} %get-tuple-element.34.own_ref, f32[4,1024]{1,0:T(4,128)S(1)} %get-tuple-element.35.weight_ref, ...), custom_call_target="tpu_custom_call" | custom-call | flops 2000000000 | bytes 4000000 | tf_op jit(solution)/shard_map/own_terms/pallas_call | solution.py:327
  15.1 0.0 collective-permute-done.2.edge_ref
  15.1 3.6 %peer_terms.1 = (f32[4,128,128]{2,1,0:T(8,128)S(1)}, bf16[4,128,128]{2,1,0:T(8,128)(2,1)S(1)}, bf16[4,128,128]{2,1,0:T(8,128)(2,1)S(1)}, bf16[4,128,256]{2,1,0:T...) custom-call(s32[16]{0:T(128)} %doc_hbm.3, ...), custom_call_target="tpu_custom_call" | custom-call | flops 2000000000 | bytes 4000000 | tf_op jit(solution)/shard_map/peer_terms/pallas_call | solution.py:327
  18.7 0.0 copy-start
  18.7 1.6 %collective-permute-start.3 = (bf16[4,128,128]{2,1,0:T(8,128)(2,1)S(1)}, bf16[4,128,128]{2,1,0:T(8,128)(2,1)S(1)}, u32[]{:S(2)}, u32[]{:S(2)}) collective-permute-start(bf16[4,128,128]{2,1,0:T(8,128)(2,1)S(1)} %get-tuple-element.53), channel_id=1, source_target_pairs={{0,8},{4,12},{8,16},{12,20},{16,24},{20,28},{24,0},{28,4},{1,9},{5... | collective-permute-start | bytes 393224 | tf_op jit(solution)/shard_map/ppermute | solution.py:419
  20.4 2.5 %collective-permute-start.4 = (bf16[128,512]{1,0:T(8,128)(2,1)S(1)}, bf16[128,512]{1,0:T(8,128)(2,1)S(1)}, u32[]{:S(2)}, u32[]{:S(2)}) collective-permute-start(bf16[128,512]{1,0:T(8,128)(2,1)S(1)} %get-tuple-element.55), channel_id=1, source_target_pairs={{0,4},{4,0},{8,12},{12,8},{16,20},{20,16},{24,28},{28,24},{1,5},{5... | collective-permute-start | bytes 393224 | tf_op jit(solution)/shard_map/ppermute | solution.py:423
  22.9 1.8 %local_outputs.1 = (f32[256,512]{1,0:T(8,128)S(1)}, bf16[256,512]{1,0:T(8,128)(2,1)S(1)}, bf16[4,512,512]{2,1,0:T(8,128)(2,1)S(1)}) custom-call(f32[4,128,128]{2,1,0:T(8,128)S(1)} %get-tuple-element.38.own_state_ref, bf16[4,128,128]{2,1,0:T(8,128)(2,1)S(1)} %get-tuple-element.39.own_map_ref, f32[128,512]{1,0:T(8,128)S(1)} %get-tuple-element.40.own_out_ref, ...), custom_call_target="tpu_custom_call" | custom-call | flops 1000000000 | bytes 4000000 | tf_op jit(solution)/shard_map/local_outputs/pallas_call | solution.py:327
  24.6 0.9 %collective-permute-done.3.enter_ref = bf16[4,128,128]{2,1,0:T(8,128)(2,1)S(1)} collective-permute-done((bf16[4,128,128]{2,1,0:T(8,128)(2,1)S(1)}, bf16[4,128,128]{2,1,0:T(8,128)(2,1)S(1)}, u32[]{:S(2)}, u32[]{:S(2)}) %collective-permute-start.3) | collective-permute-done | bytes 131104 | tf_op jit(solution)/shard_map/ppermute | solution.py:419
  25.6 0.2 collective-permute-done.4.peer_gate_ref
  25.8 1.0 %project.1 = (bf16[256,1024]{1,0:T(8,128)(2,1)S(1)}, bf16[256,1024]{1,0:T(8,128)(2,1)S(1)}) custom-call(f32[256,512]{1,0:T(8,128)S(1)} %get-tuple-element.49.out_ref, bf16[256,512]{1,0:T(8,128)(2,1)S(1)} %get-tuple-element.50.through_ref, bf16[4,128,128]{2,1,0:T(8,128)(2,1)S(1)} %collective-permute-done.3.enter_ref, ...), custom_call_target="tpu_custom_call" | custom-call | tf_op jit(solution)/shard_map/project/pallas_call | solution.py:327
  26.8 0.1 collective-permute-start.5
  26.9 1.9 %collective-permute-done.5.got_ref = bf16[256,1024]{1,0:T(8,128)(2,1)S(1)} collective-permute-done((bf16[256,1024]{1,0:T(8,128)(2,1)S(1)}, bf16[256,1024]{1,0:T(8,128)(2,1)S(1)}, u32[]{:S(2)}, u32[]{:S(2)}) %collective-permute-start.5) | collective-permute-done | bytes 524320 | tf_op jit(solution)/shard_map/ppermute | solution.py:440
  28.8 0.1 core_sum.1
  28.9 1.6 %collective-permute-start.6 = (bf16[128,512]{1,0:T(8,128)(2,1)S(1)}, bf16[128,512]{1,0:T(8,128)(2,1)S(1)}, u32[]{:S(2)}, u32[]{:S(2)}) collective-permute-start(bf16[128,512]{1,0:T(8,128)(2,1)S(1)} %get-tuple-element.60), channel_id=1, source_target_pairs={{0,2},{1,3},{2,0},{3,1},{4,6},{5,7},{6,4},{7,5},{8,10},{9,11},{10,... | collective-permute-start | bytes 393224 | tf_op jit(solution)/shard_map/ppermute | solution.py:451
  30.5 2.3 %collective-permute-start.7 = (bf16[128,512]{1,0:T(8,128)(2,1)S(1)}, bf16[128,512]{1,0:T(8,128)(2,1)S(1)}, u32[]{:S(2)}, u32[]{:S(2)}) collective-permute-start(bf16[128,512]{1,0:T(8,128)(2,1)S(1)} %get-tuple-element.61), channel_id=1, source_target_pairs={{0,4},{4,0},{8,12},{12,8},{16,20},{20,16},{24,28},{28,24},{1,5},{5... | collective-permute-start | bytes 393224 | tf_op jit(solution)/shard_map/ppermute | solution.py:452
  32.7 1.8 %collective-permute-done.6.x_ref = bf16[128,512]{1,0:T(8,128)(2,1)S(1)} collective-permute-done((bf16[128,512]{1,0:T(8,128)(2,1)S(1)}, bf16[128,512]{1,0:T(8,128)(2,1)S(1)}, u32[]{:S(2)}, u32[]{:S(2)}) %collective-permute-start.6) | collective-permute-done | bytes 131104 | tf_op jit(solution)/shard_map/ppermute | solution.py:451
  34.5 3.8 %collective-permute-done.7.y_ref = bf16[128,512]{1,0:T(8,128)(2,1)S(1)} collective-permute-done((bf16[128,512]{1,0:T(8,128)(2,1)S(1)}, bf16[128,512]{1,0:T(8,128)(2,1)S(1)}, u32[]{:S(2)}, u32[]{:S(2)}) %collective-permute-start.7) | collective-permute-done | bytes 131104 | tf_op jit(solution)/shard_map/ppermute | solution.py:452
  38.3 0.7 %collective-permute-done.8.xy_ref = bf16[128,512]{1,0:T(8,128)(2,1)S(1)} collective-permute-done((bf16[128,512]{1,0:T(8,128)(2,1)S(1)}, bf16[128,512]{1,0:T(8,128)(2,1)S(1)}, u32[]{:S(2)}, u32[]{:S(2)}) %collective-permute-start.8) | collective-permute-done | bytes 131104 | tf_op jit(solution)/shard_map/ppermute | solution.py:450
  39.1 0.8 %last_sum.1 = bf16[512,128]{1,0:T(8,128)(2,1)} custom-call(f32[128,512]{1,0:T(8,128)S(1)} %get-tuple-element.59.mine_ref, bf16[128,512]{1,0:T(8,128)(2,1)S(1)} %collective-permute-done.6.x_ref, bf16[128,512]{1,0:T(8,128)(2,1)S(1)} %collective-permute-done.7.y_ref, bf16[128,512]{1,0:T(8,128)(2,1)S(1)} %collective-permute-done.8.xy_ref), custom_call_target="tpu_custom_call" | custom-call | tf_op jit(solution)/shard_map/last_sum/pallas_call | solution.py:327
  (3 shorter events, 0.0 us)
Async XLA Ops:
  1.5 13.6 %collective-permute-start.1 = (bf16[144,1024]{1,0:T(8,128)(2,1)S(1)}, bf16[144,1024]{1,0:T(8,128)(2,1)S(1)}, u32[]{:S(2)}, u32[]{:S(2)}) collective-permute-start(bf16[144,1024]{1,0:T(8,128)(2,1)S(1)} %get-tuple-element.42), channel_id=1, source_target_pairs={{0,4},{4,0},{8,12},{12,8},{16,20},{20,16},{24,28},{28,24},{1,5},{5... | collective-permute-start | bytes 884744 | tf_op jit(solution)/shard_map/ppermute | solution.py:385
  4.5 7.0 %collective-permute-start = (bf16[16,1024]{1,0:T(8,128)(2,1)S(1)}, bf16[16,1024]{1,0:T(8,128)(2,1)S(1)}, u32[]{:S(2)}, u32[]{:S(2)}) collective-permute-start(bf16[16,1024]{1,0:T(8,128)(2,1)S(1)} %get-tuple-element.37), channel_id=1, source_target_pairs={{0,4},{4,8},{8,12},{12,16},{16,20},{20,24},{24,28},{28,0},{1,5},{5... | collective-permute-start | bytes 98312 | tf_op jit(solution)/shard_map/ppermute | solution.py:383
  4.6 10.5 %collective-permute-start.2 = (bf16[16,1024]{1,0:T(8,128)(2,1)S(1)}, bf16[16,1024]{1,0:T(8,128)(2,1)S(1)}, u32[]{:S(2)}, u32[]{:S(2)}) collective-permute-start(bf16[16,1024]{1,0:T(8,128)(2,1)S(1)} %get-tuple-element.43.own_edge_ref), channel_id=1, source_target_pairs={{0,8},{4,12},{8,16},{12,20},{16,24},{20,28},{24,0},{28,4},{1,9},{5... | collective-permute-start | bytes 98312 | tf_op jit(solution)/shard_map/ppermute | solution.py:384
  18.7 7.1 %copy-start = (f32[128]{0:T(128)S(1)}, f32[128]{0:T(128)}, u32[]{:S(2)}) copy-start(f32[128]{0:T(128)} %param.21) | copy-start | bytes 1540
  18.7 6.8 %collective-permute-start.3 = (bf16[4,128,128]{2,1,0:T(8,128)(2,1)S(1)}, bf16[4,128,128]{2,1,0:T(8,128)(2,1)S(1)}, u32[]{:S(2)}, u32[]{:S(2)}) collective-permute-start(bf16[4,128,128]{2,1,0:T(8,128)(2,1)S(1)} %get-tuple-element.53), channel_id=1, source_target_pairs={{0,8},{4,12},{8,16},{12,20},{16,24},{20,28},{24,0},{28,4},{1,9},{5... | collective-permute-start | bytes 393224 | tf_op jit(solution)/shard_map/ppermute | solution.py:419
  20.4 5.4 %collective-permute-start.4 = (bf16[128,512]{1,0:T(8,128)(2,1)S(1)}, bf16[128,512]{1,0:T(8,128)(2,1)S(1)}, u32[]{:S(2)}, u32[]{:S(2)}) collective-permute-start(bf16[128,512]{1,0:T(8,128)(2,1)S(1)} %get-tuple-element.55), channel_id=1, source_target_pairs={{0,4},{4,0},{8,12},{12,8},{16,20},{20,16},{24,28},{28,24},{1,5},{5... | collective-permute-start | bytes 393224 | tf_op jit(solution)/shard_map/ppermute | solution.py:423
  26.8 2.0 %collective-permute-start.5 = (bf16[256,1024]{1,0:T(8,128)(2,1)S(1)}, bf16[256,1024]{1,0:T(8,128)(2,1)S(1)}, u32[]{:S(2)}, u32[]{:S(2)}) collective-permute-start(bf16[256,1024]{1,0:T(8,128)(2,1)S(1)} %get-tuple-element.58), channel_id=1, source_target_pairs={{0,1},{1,0},{2,3},{3,2},{4,5},{5,4},{6,7},{7,6},{8,9},{9,8},{10,11... | collective-permute-start | bytes 1572872 | tf_op jit(solution)/shard_map/ppermute | solution.py:440
  28.9 5.6 %collective-permute-start.6 = (bf16[128,512]{1,0:T(8,128)(2,1)S(1)}, bf16[128,512]{1,0:T(8,128)(2,1)S(1)}, u32[]{:S(2)}, u32[]{:S(2)}) collective-permute-start(bf16[128,512]{1,0:T(8,128)(2,1)S(1)} %get-tuple-element.60), channel_id=1, source_target_pairs={{0,2},{1,3},{2,0},{3,1},{4,6},{5,7},{6,4},{7,5},{8,10},{9,11},{10,... | collective-permute-start | bytes 393224 | tf_op jit(solution)/shard_map/ppermute | solution.py:451
  30.5 7.8 %collective-permute-start.7 = (bf16[128,512]{1,0:T(8,128)(2,1)S(1)}, bf16[128,512]{1,0:T(8,128)(2,1)S(1)}, u32[]{:S(2)}, u32[]{:S(2)}) collective-permute-start(bf16[128,512]{1,0:T(8,128)(2,1)S(1)} %get-tuple-element.61), channel_id=1, source_target_pairs={{0,4},{4,0},{8,12},{12,8},{16,20},{20,16},{24,28},{28,24},{1,5},{5... | collective-permute-start | bytes 393224 | tf_op jit(solution)/shard_map/ppermute | solution.py:452
  32.7 6.3 %collective-permute-start.8 = (bf16[128,512]{1,0:T(8,128)(2,1)S(1)}, bf16[128,512]{1,0:T(8,128)(2,1)S(1)}, u32[]{:S(2)}, u32[]{:S(2)}) collective-permute-start(bf16[128,512]{1,0:T(8,128)(2,1)S(1)} %get-tuple-element.62), channel_id=1, source_target_pairs={{0,6},{1,7},{2,4},{3,5},{4,2},{5,3},{6,0},{7,1},{8,14},{9,15},{10,... | collective-permute-start | bytes 393224 | tf_op jit(solution)/shard_map/ppermute | solution.py:450

commit v3 on v2

v3 whole, which is shorter than its diff:
```python
import jax
import jax.numpy as jnp
from jax import lax
from jax.experimental import pallas as pl
from jax.experimental.pallas import tpu as pltpu
from jax.sharding import PartitionSpec as P

DK = 128
DV = 128
EDGE = 16
F32 = jnp.float32
BF16 = jnp.bfloat16
VMEM_LIMIT = 48 * 1024 * 1024


def dot(a, b):
    return jnp.dot(a.astype(BF16), b.astype(BF16), preferred_element_type=F32)


def exact_dot(a, b):
    return jnp.dot(a, b, precision=lax.Precision.HIGHEST, preferred_element_type=F32)


def where_y(flag, a, b):
    return jnp.where(flag == 1, a, b)


def document_counts(doc_ref, base, rows, lanes):
    down = lax.broadcasted_iota(jnp.int32, (rows + 8, lanes), 0) + (base - 8)
    along = lax.broadcasted_iota(jnp.int32, (8, rows), 1) + base
    docs = doc_ref.shape[0]

    def one(d, carried):
        start, count_down, count_along = carried
        count_down = count_down + (down >= start).astype(jnp.int32)
        count_along = count_along + (along >= start).astype(jnp.int32)
        return start + doc_ref[d], count_down, count_along

    state = (jnp.int32(0), jnp.zeros_like(down), jnp.zeros_like(along))
    if docs <= 16:
        for d in range(docs):
            state = one(d, state)
    else:
        state = lax.fori_loop(0, docs, one, state)
    return state[1], state[2]


def three_terms(value):
    high = value.astype(BF16)
    rest = value - high.astype(F32)
    middle = rest.astype(BF16)
    low = (rest - middle.astype(F32)).astype(BF16)
    return high, middle, low


class Copies:
    def __init__(self, sems):
        self.sems, self.started = sems, []

    def start(self, source, target):
        self.started.append(pltpu.make_async_copy(source, target, self.sems.at[len(self.started)]))
        self.started[-1].start()

    def wait(self, first=0, last=None):
        for one in self.started[first:last]:
            one.wait()


def half_columns(ref, which):
    width = ref.shape[1] // 2
    return pl.ds(pl.multiple_of(which * width, width), width)


def pack_kernel(q_ref, k_ref, v_ref, decay_ref, beta_ref, edge_ref, pack_ref, gates_ref, raw_gates, sems):
    other = 1 - lax.axis_index("ctx") % 2
    rows = q_ref.shape[0]
    heads = decay_ref.shape[0] // 2
    copies = Copies(sems)
    copies.start(decay_ref, raw_gates.at[0])
    copies.start(beta_ref, raw_gates.at[1])
    at = 0
    for ref in (q_ref, k_ref, v_ref):
        width = ref.shape[1] // 2
        copies.start(ref.at[pl.ds(rows - EDGE, EDGE), half_columns(ref, other)], edge_ref.at[:, pl.ds(at, width)])
        at += width
    at = 0
    for ref in (k_ref, v_ref):
        width = ref.shape[1] // 2
        copies.start(ref.at[:, half_columns(ref, other)], pack_ref.at[pl.ds(0, rows), pl.ds(at, width)])
        at += width
    pack_ref[rows : rows + EDGE, :] = jnp.zeros((EDGE, pack_ref.shape[1]), BF16)
    copies.wait(0, 2)
    decay = raw_gates[0]
    log_gamma = -(jnp.maximum(decay, 0.0) + jnp.log1p(jnp.exp(-jnp.abs(decay))))
    upper = lax.broadcasted_iota(jnp.int32, (rows, rows), 0) <= lax.broadcasted_iota(jnp.int32, (rows, rows), 1)
    sums = exact_dot(log_gamma, upper.astype(F32))
    beta = 1.0 / (1.0 + jnp.exp(-raw_gates[1]))
    at = 0
    for i, value in enumerate((sums, beta)):
        gates_ref[i * heads : i * heads + heads] = where_y(other, value[:heads], value[heads:])
        for term in three_terms(where_y(other, value[heads:], value[:heads])):
            pack_ref[rows : rows + heads, at : at + rows] = term
            at += rows
    copies.wait(2)


def early_kernel(q_ref, k_ref, v_ref, g_ref, cq_ref, ck_ref, cv_ref, doc_hbm,
                 own_edge_ref, late_ref, own_ref, weight_ref, own_gate_ref, down_ref, along_ref, doc_ref, sems):
    ctx = lax.axis_index("ctx")
    y = ctx % 2
    rows = q_ref.shape[0]
    copies = Copies(sems)
    copies.start(doc_hbm, doc_ref)
    at = 0
    for ref, weights in ((q_ref, cq_ref), (k_ref, ck_ref), (v_ref, cv_ref)):
        width = ref.shape[1] // 2
        here = pl.ds(at, width)
        copies.start(ref.at[pl.ds(rows - EDGE, EDGE), half_columns(ref, y)], own_edge_ref.at[:, here])
        copies.start(ref.at[:, half_columns(ref, y)], own_ref.at[:, here])
        copies.start(weights.at[:, half_columns(ref, y)], weight_ref.at[:, here])
        at += width
    key_width = q_ref.shape[1] // 2
    copies.start(q_ref.at[:, half_columns(q_ref, 1 - y)], late_ref.at[:, pl.ds(0, key_width)])
    copies.start(g_ref.at[:, half_columns(g_ref, 1 - y)], late_ref.at[:, pl.ds(key_width, g_ref.shape[1] // 2)])
    copies.start(g_ref.at[:, half_columns(g_ref, y)], own_gate_ref)
    copies.wait(0, 1)
    down_ref[...], along_ref[...] = document_counts(doc_ref, (ctx - y) * rows, 2 * rows, 128)
    copies.wait(1)


def conv_silu(halo, current, weight, keeps):
    rows = current.shape[0]
    padded = jnp.concatenate([halo.astype(F32)[EDGE - 8 :], current.astype(F32)], axis=0)
    margin = weight.shape[0] - 1
    summed = weight[margin : margin + 1] * padded[8:]
    for lag in range(1, margin + 1):
        summed = summed + weight[margin - lag : margin - lag + 1] * padded[8 - lag : 8 - lag + rows] * keeps[lag]
    return summed / (1.0 + jnp.exp(-summed))


def unit(vectors):
    return vectors * lax.rsqrt(jnp.sum(vectors * vectors, axis=-1, keepdims=True) + 1e-6)


def odd_blocks(value, reach):
    return jnp.concatenate([value[at : at + reach] for at in range(reach, value.shape[0], 2 * reach)], axis=0)


def at_odd_blocks(value, reach):
    parts = []
    for at in range(0, value.shape[0], reach):
        parts += [jnp.zeros((reach, value.shape[1]), value.dtype), value[at : at + reach]]
    return jnp.concatenate(parts, axis=0)


def keep_masks(seg_down):
    seg = seg_down[8:]
    return [None] + [(seg_down[8 - lag : 8 - lag + seg.shape[0]] == seg).astype(F32) for lag in (1, 2, 3)]


def state_terms(seg_down, seg_along, halo, k, v, weights, sums, beta):
    heads, rows = sums.shape
    key_heads = heads // 2
    seg = seg_down[8:]
    keeps = keep_masks(seg_down)
    before = seg_down[7:8]
    last = seg_down[rows + 7 : rows + 8]
    row = lax.broadcasted_iota(jnp.int32, (rows, rows), 0)
    col = lax.broadcasted_iota(jnp.int32, (rows, rows), 1)
    same = (seg == seg_along[0:1]) & (row >= col)
    stacked = jnp.concatenate([sums, beta, jnp.zeros((rows - 2 * heads, rows), F32)], axis=0)
    columns = stacked.T

    keys = [unit(conv_silu(halo(1, g), k(g), weights(1, g), keeps)) for g in range(key_heads)]
    values = [conv_silu(halo(2, g), v(g), weights(2, g), keeps) for g in range(heads)]
    keys_t = [key.T for key in keys]
    keys_t16 = [key.astype(BF16) for key in keys_t]
    grams = [dot(key, key_t) for key, key_t in zip(keys, keys_t16)]

    lower, decays, rhs, starts, ends, throughs = [], [], [], [], [], []
    for h in range(heads):
        g = h // 2
        down = jnp.broadcast_to(columns[:, h : h + 1], (rows, rows))
        beta_down = jnp.broadcast_to(columns[:, heads + h : heads + h + 1], (rows, rows))
        along = sums[h : h + 1]
        end = jnp.broadcast_to(columns[rows - 1 : rows, h : h + 1], (1, rows))
        decay = jnp.exp(jnp.where(same, down - along, -1e30))
        decays.append(decay)
        lower.append(jnp.where(row > col, beta_down * grams[g] * decay, 0.0))
        start = jnp.where(seg == before, jnp.exp(down), 0.0)
        starts.append(start)
        rhs.append(
            jnp.concatenate([(beta_down * values[h]).astype(BF16), (beta_down * start * keys[g]).astype(BF16)], axis=1)
        )
        ends.append((keys_t[g] * jnp.where(seg_along[0:1] == last, jnp.exp(end - along), 0.0)).astype(BF16))
        throughs.append(jnp.where(last == before, jnp.exp(end), 0.0))

    small = 16
    eye = (row == col).astype(F32)
    power = [jnp.where(row // small == col // small, -x, 0.0) for x in lower]
    inverse = [eye + x for x in power]
    power = [x.astype(BF16) for x in power]
    reach = 2
    while reach < small:
        power = [dot(x, x).astype(BF16) for x in power]
        inverse = [x + dot(x, p) for x, p in zip(inverse, power)]
        reach *= 2
    reach = small
    while reach < rows:
        here = (row // (2 * reach) == col // (2 * reach)) & (row // reach != col // reach)
        moved = [dot(odd_blocks(jnp.where(here, x, 0.0), reach), i) for x, i in zip(lower, inverse)]
        moved = [dot(odd_blocks(i, reach), at_odd_blocks(m, reach)) for i, m in zip(inverse, moved)]
        inverse = [i - at_odd_blocks(m, reach) for i, m in zip(inverse, moved)]
        reach *= 2
    solved = [dot(i, r).astype(BF16) for i, r in zip(inverse, rhs)]
    ended = [dot(e, s) for e, s in zip(ends, solved)]
    states = [e[:, :DV] for e in ended]
    maps = [t * eye - e[:, DV:] for t, e in zip(throughs, ended)]
    return states, maps, solved, decays, starts, keys_t16


def query_terms(seg_down, halo, q, weights, solved, decays, starts, keys_t):
    keeps = keep_masks(seg_down)
    queries = [unit(conv_silu(halo(0, g), q(g), weights(0, g), keeps)) for g in range(len(keys_t))]
    scores = [dot(query, key_t) for query, key_t in zip(queries, keys_t)]
    results = [dot(scores[h // 2] * decays[h], solved[h]) for h in range(len(solved))]
    outs = [result[:, :DV] for result in results]
    throughs = [(queries[h // 2] * starts[h] - results[h][:, DV:]).astype(BF16) for h in range(len(solved))]
    return outs, throughs


def groups(heads):
    at = (0, heads // 2 * DK, heads * DK)
    return lambda which, g: slice(at[which] + g * 128, at[which] + g * 128 + 128)


def counts(down_ref, along_ref, block, rows):
    at = pl.multiple_of(block * rows, rows)
    return down_ref[pl.ds(at, rows + 8), :], along_ref[:, pl.ds(at, rows)]


def own_kernel(down_ref, along_ref, own_ref, weight_ref, gates_ref, halo_ref,
               state_ref, map_ref, out_ref, through_ref):
    rows = own_ref.shape[0]
    heads = gates_ref.shape[0] // 2
    columns = groups(heads)
    seg_down, seg_along = counts(down_ref, along_ref, lax.axis_index("ctx") % 2, rows)

    def halo(which, g):
        return halo_ref[:, columns(which, g)]

    def weights(which, g):
        return weight_ref[:, columns(which, g)]

    states, maps, solved, decays, starts, keys_t = state_terms(
        seg_down,
        seg_along,
        halo,
        lambda g: own_ref[:, columns(1, g)],
        lambda g: own_ref[:, columns(2, g)],
        weights,
        gates_ref[0:heads],
        gates_ref[heads:],
    )
    outs, throughs = query_terms(
        seg_down, halo, lambda g: own_ref[:, columns(0, g)], weights, solved, decays, starts, keys_t
    )
    for h in range(heads):
        state_ref[h] = states[h]
        map_ref[h] = maps[h].astype(BF16)
        out_ref[:, h * DV : h * DV + DV] = outs[h]
        through_ref[:, h * DK : h * DK + DK] = throughs[h]


def peer_halo(own_edge_ref, edge_ref, columns):
    y = lax.axis_index("ctx") % 2
    return lambda which, g: where_y(y, edge_ref[:, columns(which, g)], own_edge_ref[:, columns(which, g)])


def peer_kernel(down_ref, along_ref, pack_ref, own_edge_ref, edge_ref, weight_ref, own_state_ref, own_map_ref,
                state_ref, map_ref, solved_ref, decay_ref, start_ref, key_ref, end_ref, *pair_map_ref):
    y = lax.axis_index("ctx") % 2
    rows = pack_ref.shape[0] - EDGE
    heads = own_state_ref.shape[0]
    columns = groups(heads)
    key_width = heads // 2 * DK
    gates = [
        sum(pack_ref[rows : rows + heads, (3 * part + i) * rows : (3 * part + i + 1) * rows].astype(F32) for i in range(3))
        for part in range(2)
    ]
    states, maps, solved, decays, starts, keys_t = state_terms(
        *counts(down_ref, along_ref, 1 - y, rows),
        peer_halo(own_edge_ref, edge_ref, columns),
        lambda g: pack_ref[0:rows, g * DK : g * DK + DK],
        lambda g: pack_ref[0:rows, key_width + g * DV : key_width + g * DV + DV],
        lambda which, g: weight_ref[:, columns(which, g)],
        gates[0],
        gates[1],
    )
    for h in range(heads):
        own_state, own_map = own_state_ref[h], own_map_ref[h]
        maps16 = maps[h].astype(BF16)
        state_0, state_1 = where_y(y, states[h], own_state), where_y(y, own_state, states[h])
        map_0, map_1 = where_y(y, maps16, own_map), where_y(y, own_map, maps16)
        end_ref[h] = (state_1 + dot(map_1, state_0)).astype(BF16)
        if pair_map_ref:
            pair_map_ref[0][h] = dot(map_1, map_0).astype(BF16)
    for h in range(heads):
        state_ref[h] = states[h]
        map_ref[h] = maps[h].astype(BF16)
        solved_ref[h] = solved[h]
        decay_ref[h] = decays[h]
        start_ref[h] = starts[h]
    for g in range(heads // 2):
        key_ref[g] = keys_t[g]


def local_kernel(own_state_ref, own_map_ref, own_out_ref, own_through_ref, state_ref, map_ref, solved_ref, decay_ref,
                 start_ref, key_ref, down_ref, along_ref, late_ref, own_edge_ref, edge_ref, conv_ref, weight_hbm,
                 out_ref, through_ref, weight_ref, sems):
    y = lax.axis_index("ctx") % 2
    head = lax.axis_index("head")
    core, x = head % 2, head // 2
    depth, width = weight_ref.shape[1:]
    copies = []
    for i, (c, xx) in enumerate(((1 - core, x), (1 - core, 1 - x), (core, x), (core, 1 - x))):
        source = weight_hbm.at[
            pl.ds(pl.multiple_of(y * depth, depth), depth), pl.ds(pl.multiple_of((xx * 2 + c) * width, width), width)
        ]
        copies.append(pltpu.make_async_copy(source, weight_ref.at[i], sems.at[i]))
        copies[-1].start()
    rows = own_out_ref.shape[0]
    heads = own_state_ref.shape[0]
    columns = groups(heads)
    outs, throughs = query_terms(
        counts(down_ref, along_ref, 1 - y, rows)[0],
        peer_halo(own_edge_ref, edge_ref, columns),
        lambda g: late_ref[:, g * DK : g * DK + DK],
        lambda which, g: conv_ref[:, columns(which, g)],
        [solved_ref[h] for h in range(heads)],
        [decay_ref[h] for h in range(heads)],
        [start_ref[h] for h in range(heads)],
        [key_ref[g] for g in range(heads // 2)],
    )
    for h in range(heads):
        lanes = slice(h * DV, h * DV + DV)
        own_out, own_through = own_out_ref[:, lanes], own_through_ref[:, lanes]
        out, through = outs[h], throughs[h]
        state_0 = where_y(y, state_ref[h], own_state_ref[h]).astype(BF16)
        map_0 = where_y(y, map_ref[h], own_map_ref[h])
        through_1 = where_y(y, own_through, through)
        more = dot(through_1, jnp.concatenate([state_0, map_0], axis=1))
        extra, moved = more[:, :DV], more[:, DV:].astype(BF16)
        out_ref[0:rows, lanes] = own_out + where_y(y, extra, jnp.zeros_like(extra))
        out_ref[rows:, lanes] = out + where_y(y, jnp.zeros_like(extra), extra)
        through_ref[0:rows, lanes] = where_y(y, moved, own_through)
        through_ref[rows:, lanes] = where_y(y, through, moved)
    for copy in copies:
        copy.wait()


def project_kernel(out_ref, through_ref, enter_ref, gate_ref, late_ref, gain_ref, weight_ref, send_ref, keep_ref):
    heads = enter_ref.shape[0]
    key_width = late_ref.shape[1] - heads * DV
    width = weight_ref.shape[2]
    mixed = []
    for h in range(heads):
        lanes = slice(h * DV, h * DV + DV)
        o = out_ref[:, lanes] + dot(through_ref[:, lanes], enter_ref[h])
        gate = jnp.concatenate([gate_ref[:, lanes], late_ref[:, key_width + h * DV : key_width + h * DV + DV]], axis=0).astype(F32)
        scale = lax.rsqrt(jnp.mean(o * o, axis=-1, keepdims=True) + 1e-6)
        mixed.append((o * scale * gain_ref[...] * (gate / (1.0 + jnp.exp(-gate)))).astype(BF16))
    mixed = jnp.concatenate(mixed, axis=1)
    for i in range(4):
        to_ref = (send_ref, keep_ref)[i // 2]
        to_ref[:, (i % 2) * width : (i % 2 + 1) * width] = jnp.dot(
            mixed, weight_ref[i], preferred_element_type=F32
        ).astype(BF16)


def core_sum_kernel(keep_ref, got_ref, mine_ref, x_ref, y_ref, xy_ref):
    rows, width = mine_ref.shape
    for ref, r, c in ((xy_ref, 1, 1), (x_ref, 0, 1), (y_ref, 1, 0), (mine_ref, 0, 0)):
        at = (slice(r * rows, r * rows + rows), slice(c * width, c * width + width))
        ref[...] = (keep_ref[at].astype(F32) + got_ref[at].astype(F32)).astype(ref.dtype)


def last_kernel(mine_ref, x_ref, y_ref, xy_ref, out_ref):
    total = mine_ref[...] + x_ref[...].astype(F32) + (y_ref[...].astype(F32) + xy_ref[...].astype(F32))
    out_ref[...] = total.T.astype(BF16)


def call(kernel, outs, args, name, hbm=(), scratch=(), flops=0, moved=0):
    space = [pl.BlockSpec(memory_space=pltpu.HBM if i in hbm else pltpu.VMEM) for i in range(len(args))]
    args = [pltpu.with_memory_space_constraint(arg, pltpu.HBM) if i in hbm else arg for i, arg in enumerate(args)]
    return pl.pallas_call(
        kernel,
        out_shape=[jax.ShapeDtypeStruct(shape, kind) for shape, kind in outs],
        in_specs=space,
        out_specs=[pl.BlockSpec(memory_space=pltpu.VMEM)] * len(outs),
        scratch_shapes=list(scratch),
        compiler_params=pltpu.CompilerParams(vmem_limit_bytes=VMEM_LIMIT),
        cost_estimate=pl.CostEstimate(flops=flops, bytes_accessed=moved, transcendentals=0),
        name=name,
    )(*args)


def body(
    query_in,
    key_in,
    value_in,
    gate_in,
    conv_query,
    conv_key,
    conv_value,
    decay_in,
    beta_in,
    norm_gain,
    doc_lengths,
    out_weight,
):
    rows = query_in.shape[0]
    ctx_count, head_count = lax.axis_size("ctx"), lax.axis_size("head")
    heads = decay_in.shape[0] // 2
    key_width, value_width = key_in.shape[1] // 2, value_in.shape[1] // 2
    half_width = 2 * key_width + value_width
    width = out_weight.shape[1] // head_count
    longest = ctx_count * rows // 4
    hops = -(-(longest - 1) // (2 * rows))

    swap = [(i, i ^ 1) for i in range(ctx_count)]
    ahead_1 = [(i, (i + 1) % ctx_count) for i in range(ctx_count)]
    ahead_2 = [(i, (i + 2) % ctx_count) for i in range(ctx_count)]

    edge, pack, gates = call(
        pack_kernel,
        [((EDGE, half_width), BF16), ((rows + EDGE, key_width + value_width), BF16), ((2 * heads, rows), F32)],
        (query_in, key_in, value_in, decay_in, beta_in),
        "pack",
        hbm=range(5),
        scratch=(pltpu.VMEM((2,) + decay_in.shape, F32), pltpu.SemaphoreType.DMA((7,))),
    )
    own_edge, late, own, weights, own_gate, down, along = call(
        early_kernel,
        [
            ((EDGE, half_width), BF16),
            ((rows, key_width + value_width), BF16),
            ((rows, half_width), BF16),
            ((conv_query.shape[0], half_width), F32),
            ((rows, value_width), BF16),
            ((2 * rows + 8, 128), jnp.int32),
            ((8, 2 * rows), jnp.int32),
        ],
        (query_in, key_in, value_in, gate_in, conv_query, conv_key, conv_value, doc_lengths),
        "early",
        hbm=range(8),
        scratch=(pltpu.SMEM(doc_lengths.shape, jnp.int32), pltpu.SemaphoreType.DMA((13,))),
        flops=10_000_000_000,
        moved=2_000_000,
    )
    got_edge = lax.ppermute(edge, "ctx", ahead_1)
    got_pack = lax.ppermute(pack, "ctx", swap)
    got_far_edge = lax.ppermute(own_edge, "ctx", ahead_2)
    got_late = lax.ppermute(late, "ctx", swap)

    square = (heads, DK, DV)
    own_state, own_map, own_out, own_through = call(
        own_kernel,
        [(square, F32), (square, BF16), ((rows, value_width), F32), ((rows, value_width), BF16)],
        (down, along, own, weights, gates, got_edge),
        "own_terms",
        flops=20_000_000_000,
        moved=4_000_000,
    )
    peer = call(
        peer_kernel,
        [
            (square, F32),
            (square, BF16),
            ((heads, rows, DK + DV), BF16),
            ((heads, rows, rows), F32),
            ((heads, rows, DK), F32),
            ((heads // 2, DK, rows), BF16),
            (square, BF16),
        ]
        + ([(square, BF16)] if hops > 1 else []),
        (down, along, got_pack, own_edge, got_far_edge, weights, own_state, own_map),
        "peer_terms",
        flops=2_000_000_000,
        moved=4_000_000,
    )
    state, map_, solved, decay, start, key, end = peer[:7]
    entering = lax.ppermute(end, "ctx", ahead_2)
    for _ in range(hops - 1):
        moved = jnp.einsum("hij,hjk->hik", peer[7], entering, preferred_element_type=F32)
        entering = lax.ppermute((end.astype(F32) + moved).astype(BF16), "ctx", ahead_2)
    out, through, weight = call(
        local_kernel,
        [((2 * rows, value_width), F32), ((2 * rows, value_width), BF16), ((4, value_width, width), BF16)],
        (own_state, own_map, own_out, own_through, state, map_, solved, decay, start, key, down, along, got_late, own_edge,
         got_far_edge, weights, out_weight),
        "local_outputs",
        hbm=(16,),
        scratch=(pltpu.SemaphoreType.DMA((4,)),),
        flops=1_000_000_000,
        moved=4_000_000,
    )
    send, keep = call(
        project_kernel,
        [((2 * rows, 2 * width), BF16), ((2 * rows, 2 * width), BF16)],
        (out, through, entering, own_gate, got_late, norm_gain.reshape(1, DV), weight),
        "project",
    )
    got = lax.ppermute(send, "head", [(i, i ^ 1) for i in range(head_count)])
    mine, to_x, to_y, to_xy = call(
        core_sum_kernel,
        [((rows, width), F32), ((rows, width), BF16), ((rows, width), BF16), ((rows, width), BF16)],
        (keep, got),
        "core_sum",
    )
    both = [
        (c * head_count + h, (c ^ 1) * head_count + (h ^ 2)) for c in range(ctx_count) for h in range(head_count)
    ]
    got_xy = lax.ppermute(to_xy, ("ctx", "head"), both)
    got_x = lax.ppermute(to_x, "head", [(i, i ^ 2) for i in range(head_count)])
    got_y = lax.ppermute(to_y, "ctx", swap)
    (projected,) = call(
        last_kernel, [((width, rows), BF16)], (mine, got_x, got_y, got_xy), "last_sum"
    )
    return projected


def solution(mesh):
    return jax.shard_map(
        body,
        mesh=mesh,
        in_specs=(
            P("ctx", "head"),
            P("ctx", "head"),
            P("ctx", "head"),
            P("ctx", "head"),
            P(None, "head"),
            P(None, "head"),
            P(None, "head"),
            P("head", "ctx"),
            P("head", "ctx"),
            P(),
            P(),
            P("head", None),
        ),
        out_specs=P("head", "ctx"),
        check_vma=False,
    )
```

time: 40 us -> 36.4 us (0.910)
  starting transfers between devices: 13.1 us -> 11.2 us
  waiting for transfers between devices: 14.3 us -> 13.2 us
  Pallas kernels: 12.4 us -> 11.7 us
    ppermute x1, waiting for transfers between devices: 4.89 us -> 0.01 us  [body(): got_edge = lax.ppermute(edge, 'ctx', ahead_1)]
    ppermute x1, starting transfers between devices: 0.07 us -> 3.02 us  [body(): got_edge = lax.ppermute(edge, 'ctx', ahead_1)]
    ppermute x1, waiting for transfers between devices: 0.91 us -> 3.82 us  [body(): entering = lax.ppermute(end, 'ctx', ahead_2)]
    ppermute x1, starting transfers between devices: 2.48 us -> 0.51 us  [body(): got_late = lax.ppermute(late, 'ctx', swap)]
    ppermute x1, starting transfers between devices: 3.03 us -> 1.52 us  [body(): got_pack = lax.ppermute(pack, 'ctx', swap)]
    ppermute x1, starting transfers between devices: 2.26 us -> 0.81 us  [body(): got_y = lax.ppermute(to_y, 'ctx', swap)]
    ppermute x1, starting transfers between devices: 0.01 us -> 1.17 us  [body(): got_xy = lax.ppermute(to_xy, ('ctx', 'head'), both)]
    ppermute x1, waiting for transfers between devices: 0.01 us -> 0.97 us  [body(): got_far_edge = lax.ppermute(own_edge, 'ctx', ahead_2)]
  transfers between devices with their start and end apart: 9 -> 9, of which waited for: 7 -> 6; matrix products, arithmetic and copies ran while one was open for 0% -> 0% of each run, Pallas kernels for 13% -> 24%
where the time goes in v3:
time: 36.4 us; the launch traced here: 36.2 us
  waiting for transfers between devices  13.2 us (36%)
  Pallas kernels  11.7 us (32%)
  starting transfers between devices  11.2 us (31%)
    pallas_call x8, Pallas kernels, call(): pl.pallas_call(kernel, out_shape=[jax.ShapeDtypeStruct(shape, kind) for s...  11.7 us
    ppermute x1, waiting for transfers between devices, body(): entering = lax.ppermute(end, 'ctx', ahead_2)  3.82 us
    ppermute x1, waiting for transfers between devices, body(): got_y = lax.ppermute(to_y, 'ctx', swap)  3.69 us
    ppermute x1, starting transfers between devices, body(): got_edge = lax.ppermute(edge, 'ctx', ahead_1)  3.02 us
    ppermute x1, waiting for transfers between devices, body(): got_x = lax.ppermute(to_x, 'head', [(i, i ^ 2) for i in range(head_count)])  2.39 us
    ppermute x1, waiting for transfers between devices, body(): got = lax.ppermute(send, 'head', [(i, i ^ 1) for i in range(head_count)])  1.9 us
    ppermute x1, starting transfers between devices, body(): got_far_edge = lax.ppermute(own_edge, 'ctx', ahead_2)  1.63 us
    ppermute x1, starting transfers between devices, body(): got_x = lax.ppermute(to_x, 'head', [(i, i ^ 2) for i in range(head_count)])  1.56 us
  transfers between devices with their start and end apart: 9, of which 6 were waited for; matrix products, arithmetic and copies ran while one was open for 0% of the time, Pallas kernels for 24%

profile of v3, /device:TPU:0, one launch (start us, length us, event | category | flops | bytes accessed | tf_op | source)
XLA Modules:
  0.0 36.2 jit_solution(3584919005029942022)
XLA Ops:
  0.0 1.1 %pack.1 = (bf16[16,1024]{1,0:T(8,128)(2,1)S(1)}, bf16[144,768]{1,0:T(8,128)(2,1)S(1)}, f32[8,128]{1,0:T(8,128)S(1)}) custom-call(bf16[128,512]{1,0:T(8,128)(2,1)} %q_ref.3, bf16[128,512]{1,0:T(8,128)(2,1)} %k_ref.3, bf16[128,1024]{1,0:T(8,128)(2,1)} %v_ref.3, f32[8,128]{1,0:T(8,128)} %decay_ref.1, f32[8,128]{1,0:T(8,128)} %beta_ref.1), custom_call_target="tpu_custom_call" | custom-call | tf_op jit(solution)/shard_map/pack/pallas_call | solution.py:396
  1.1 3.0 %collective-permute-start = (bf16[16,1024]{1,0:T(8,128)(2,1)S(1)}, bf16[16,1024]{1,0:T(8,128)(2,1)S(1)}, u32[]{:S(2)}, u32[]{:S(2)}) collective-permute-start(bf16[16,1024]{1,0:T(8,128)(2,1)S(1)} %get-tuple-element.40), channel_id=1, source_target_pairs={{0,4},{4,8},{8,12},{12,16},{16,20},{20,24},{24,28},{28,0},{1,5},{5... | collective-permute-start | bytes 98312 | tf_op jit(solution)/shard_map/ppermute | solution.py:461
  4.1 1.5 %collective-permute-start.1 = (bf16[144,768]{1,0:T(8,128)(2,1)S(1)}, bf16[144,768]{1,0:T(8,128)(2,1)S(1)}, u32[]{:S(2)}, u32[]{:S(2)}) collective-permute-start(bf16[144,768]{1,0:T(8,128)(2,1)S(1)} %get-tuple-element.45), channel_id=1, source_target_pairs={{0,4},{4,0},{8,12},{12,8},{16,20},{20,16},{24,28},{28,24},{1,5},{5... | collective-permute-start | bytes 663560 | tf_op jit(solution)/shard_map/ppermute | solution.py:462
  5.6 1.3 %early.1 = (bf16[16,1024]{1,0:T(8,128)(2,1)S(1)}, bf16[128,768]{1,0:T(8,128)(2,1)S(1)}, bf16[128,1024]{1,0:T(8,128)(2,1)S(1)}, f32[4,1024]{1,0:T(4,128)S(1)}, bf...) custom-call(bf16[128,512]{1,0:T(8,128)(2,1)} %q_ref.3, bf16[128,512]{1,0:T(8,128)(2,1)} %k_ref.3, ...), custom_call_target="tpu_custom_call" | custom-call | flops 10000000000 | bytes 2000000 | tf_op jit(solution)/shard_map/early/pallas_call | solution.py:396
  7.0 1.6 %collective-permute-start.2 = (bf16[16,1024]{1,0:T(8,128)(2,1)S(1)}, bf16[16,1024]{1,0:T(8,128)(2,1)S(1)}, u32[]{:S(2)}, u32[]{:S(2)}) collective-permute-start(bf16[16,1024]{1,0:T(8,128)(2,1)S(1)} %get-tuple-element.46.own_edge_ref), channel_id=1, source_target_pairs={{0,8},{4,12},{8,16},{12,20},{16,24},{20,28},{24,0},{28,4},{1,9},{5... | collective-permute-start | bytes 98312 | tf_op jit(solution)/shard_map/ppermute | solution.py:463
  8.6 0.5 %collective-permute-start.3 = (bf16[128,768]{1,0:T(8,128)(2,1)S(1)}, bf16[128,768]{1,0:T(8,128)(2,1)S(1)}, u32[]{:S(2)}, u32[]{:S(2)}) collective-permute-start(bf16[128,768]{1,0:T(8,128)(2,1)S(1)} %get-tuple-element.53), channel_id=1, source_target_pairs={{0,4},{4,0},{8,12},{12,8},{16,20},{20,16},{24,28},{28,24},{1,5},{5... | collective-permute-start | bytes 589832 | tf_op jit(solution)/shard_map/ppermute | solution.py:464
  9.1 2.6 %own_terms.1 = (f32[4,128,128]{2,1,0:T(8,128)S(1)}, bf16[4,128,128]{2,1,0:T(8,128)(2,1)S(1)}, f32[128,512]{1,0:T(8,128)S(1)}, bf16[128,512]{1,0:T(8,128)(2,1)S(1)}) custom-call(s32[264,128]{1,0:T(8,128)S(1)} %get-tuple-element.35.down_ref, s32[8,256]{1,0:T(8,128)S(1)} %get-tuple-element.36.along_ref, bf16[128,1024]{1,0:T(8,128)(2,1)S(1)} %get-tuple-element.37.own_ref, ...), custom_call_target="tpu_custom_call" | custom-call | flops 20000000000 | bytes 4000000 | tf_op jit(solution)/shard_map/own_terms/pallas_call | solution.py:396
  11.8 1.0 %collective-permute-done.2.edge_ref = bf16[16,1024]{1,0:T(8,128)(2,1)S(1)} collective-permute-done((bf16[16,1024]{1,0:T(8,128)(2,1)S(1)}, bf16[16,1024]{1,0:T(8,128)(2,1)S(1)}, u32[]{:S(2)}, u32[]{:S(2)}) %collective-permute-start.2) | collective-permute-done | bytes 32800 | tf_op jit(solution)/shard_map/ppermute | solution.py:463
  12.7 0.4 %collective-permute-done.1.pack_ref = bf16[144,768]{1,0:T(8,128)(2,1)S(1)} collective-permute-done((bf16[144,768]{1,0:T(8,128)(2,1)S(1)}, bf16[144,768]{1,0:T(8,128)(2,1)S(1)}, u32[]{:S(2)}, u32[]{:S(2)}) %collective-permute-start.1) | collective-permute-done | bytes 221216 | tf_op jit(solution)/shard_map/ppermute | solution.py:462
  13.2 2.7 %peer_terms.1 = (f32[4,128,128]{2,1,0:T(8,128)S(1)}, bf16[4,128,128]{2,1,0:T(8,128)(2,1)S(1)}, bf16[4,128,256]{2,1,0:T(8,128)(2,1)S(1)}, f32[4,128,128]{2,1,0:T(...) custom-call(s32[264,128]{1,0:T(8,128)S(1)} %get-tuple-element.35.down_ref, ...), custom_call_target="tpu_custom_call" | custom-call | flops 2000000000 | bytes 4000000 | tf_op jit(solution)/shard_map/peer_terms/pallas_call | solution.py:396
  15.8 0.0 copy-start
  15.8 0.9 %collective-permute-start.4 = (bf16[4,128,128]{2,1,0:T(8,128)(2,1)S(1)}, bf16[4,128,128]{2,1,0:T(8,128)(2,1)S(1)}, u32[]{:S(2)}, u32[]{:S(2)}) collective-permute-start(bf16[4,128,128]{2,1,0:T(8,128)(2,1)S(1)} %get-tuple-element.56), channel_id=1, source_target_pairs={{0,8},{4,12},{8,16},{12,20},{16,24},{20,28},{24,0},{28,4},{1,9},{5... | collective-permute-start | bytes 393224 | tf_op jit(solution)/shard_map/ppermute | solution.py:493
  16.8 2.1 %local_outputs.1 = (f32[256,512]{1,0:T(8,128)S(1)}, bf16[256,512]{1,0:T(8,128)(2,1)S(1)}, bf16[4,512,512]{2,1,0:T(8,128)(2,1)S(1)}) custom-call(f32[4,128,128]{2,1,0:T(8,128)S(1)} %get-tuple-element.41.own_state_ref, bf16[4,128,128]{2,1,0:T(8,128)(2,1)S(1)} %get-tuple-element.42.own_map_ref, f32[128,512]{1,0:T(8,128)S(1)} %get-tuple-element.43.own_out_ref, ...), custom_call_target="tpu_custom_call" | custom-call | flops 1000000000 | bytes 4000000 | tf_op jit(solution)/shard_map/local_outputs/pallas_call | solution.py:396
  18.8 3.8 %collective-permute-done.4.enter_ref = bf16[4,128,128]{2,1,0:T(8,128)(2,1)S(1)} collective-permute-done((bf16[4,128,128]{2,1,0:T(8,128)(2,1)S(1)}, bf16[4,128,128]{2,1,0:T(8,128)(2,1)S(1)}, u32[]{:S(2)}, u32[]{:S(2)}) %collective-permute-start.4) | collective-permute-done | bytes 131104 | tf_op jit(solution)/shard_map/ppermute | solution.py:493
  22.7 1.0 %project.1 = (bf16[256,1024]{1,0:T(8,128)(2,1)S(1)}, bf16[256,1024]{1,0:T(8,128)(2,1)S(1)}) custom-call(f32[256,512]{1,0:T(8,128)S(1)} %get-tuple-element.54.out_ref, bf16[256,512]{1,0:T(8,128)(2,1)S(1)} %get-tuple-element.55.through_ref, bf16[4,128,128]{2,1,0:T(8,128)(2,1)S(1)} %collective-permute-done.4.enter_ref, ...), custom_call_target="tpu_custom_call" | custom-call | tf_op jit(solution)/shard_map/project/pallas_call | solution.py:396
  23.7 0.1 collective-permute-start.5
  23.8 1.9 %collective-permute-done.5.got_ref = bf16[256,1024]{1,0:T(8,128)(2,1)S(1)} collective-permute-done((bf16[256,1024]{1,0:T(8,128)(2,1)S(1)}, bf16[256,1024]{1,0:T(8,128)(2,1)S(1)}, u32[]{:S(2)}, u32[]{:S(2)}) %collective-permute-start.5) | collective-permute-done | bytes 524320 | tf_op jit(solution)/shard_map/ppermute | solution.py:514
  25.7 0.1 core_sum.1
  25.8 1.6 %collective-permute-start.6 = (bf16[128,512]{1,0:T(8,128)(2,1)S(1)}, bf16[128,512]{1,0:T(8,128)(2,1)S(1)}, u32[]{:S(2)}, u32[]{:S(2)}) collective-permute-start(bf16[128,512]{1,0:T(8,128)(2,1)S(1)} %get-tuple-element.62), channel_id=1, source_target_pairs={{0,2},{1,3},{2,0},{3,1},{4,6},{5,7},{6,4},{7,5},{8,10},{9,11},{10,... | collective-permute-start | bytes 393224 | tf_op jit(solution)/shard_map/ppermute | solution.py:525
  27.4 0.8 %collective-permute-start.7 = (bf16[128,512]{1,0:T(8,128)(2,1)S(1)}, bf16[128,512]{1,0:T(8,128)(2,1)S(1)}, u32[]{:S(2)}, u32[]{:S(2)}) collective-permute-start(bf16[128,512]{1,0:T(8,128)(2,1)S(1)} %get-tuple-element.63), channel_id=1, source_target_pairs={{0,4},{4,0},{8,12},{12,8},{16,20},{20,16},{24,28},{28,24},{1,5},{5... | collective-permute-start | bytes 393224 | tf_op jit(solution)/shard_map/ppermute | solution.py:526
  28.2 1.2 %collective-permute-start.8 = (bf16[128,512]{1,0:T(8,128)(2,1)S(1)}, bf16[128,512]{1,0:T(8,128)(2,1)S(1)}, u32[]{:S(2)}, u32[]{:S(2)}) collective-permute-start(bf16[128,512]{1,0:T(8,128)(2,1)S(1)} %get-tuple-element.64), channel_id=1, source_target_pairs={{0,6},{1,7},{2,4},{3,5},{4,2},{5,3},{6,0},{7,1},{8,14},{9,15},{10,... | collective-permute-start | bytes 393224 | tf_op jit(solution)/shard_map/ppermute | solution.py:524
  29.4 2.4 %collective-permute-done.6.x_ref = bf16[128,512]{1,0:T(8,128)(2,1)S(1)} collective-permute-done((bf16[128,512]{1,0:T(8,128)(2,1)S(1)}, bf16[128,512]{1,0:T(8,128)(2,1)S(1)}, u32[]{:S(2)}, u32[]{:S(2)}) %collective-permute-start.6) | collective-permute-done | bytes 131104 | tf_op jit(solution)/shard_map/ppermute | solution.py:525
  31.7 3.7 %collective-permute-done.7.y_ref = bf16[128,512]{1,0:T(8,128)(2,1)S(1)} collective-permute-done((bf16[128,512]{1,0:T(8,128)(2,1)S(1)}, bf16[128,512]{1,0:T(8,128)(2,1)S(1)}, u32[]{:S(2)}, u32[]{:S(2)}) %collective-permute-start.7) | collective-permute-done | bytes 131104 | tf_op jit(solution)/shard_map/ppermute | solution.py:526
  35.4 0.8 %last_sum.1 = bf16[512,128]{1,0:T(8,128)(2,1)} custom-call(f32[128,512]{1,0:T(8,128)S(1)} %get-tuple-element.61.mine_ref, bf16[128,512]{1,0:T(8,128)(2,1)S(1)} %collective-permute-done.6.x_ref, bf16[128,512]{1,0:T(8,128)(2,1)S(1)} %collective-permute-done.7.y_ref, bf16[128,512]{1,0:T(8,128)(2,1)S(1)} %collective-permute-done.8.xy_ref), custom_call_target="tpu_custom_call" | custom-call | tf_op jit(solution)/shard_map/last_sum/pallas_call | solution.py:396
  (4 shorter events, 0.0 us)
Async XLA Ops:
  1.1 8.0 %collective-permute-start = (bf16[16,1024]{1,0:T(8,128)(2,1)S(1)}, bf16[16,1024]{1,0:T(8,128)(2,1)S(1)}, u32[]{:S(2)}, u32[]{:S(2)}) collective-permute-start(bf16[16,1024]{1,0:T(8,128)(2,1)S(1)} %get-tuple-element.40), channel_id=1, source_target_pairs={{0,4},{4,8},{8,12},{12,16},{16,20},{20,24},{24,28},{28,0},{1,5},{5... | collective-permute-start | bytes 98312 | tf_op jit(solution)/shard_map/ppermute | solution.py:461
  4.1 9.1 %collective-permute-start.1 = (bf16[144,768]{1,0:T(8,128)(2,1)S(1)}, bf16[144,768]{1,0:T(8,128)(2,1)S(1)}, u32[]{:S(2)}, u32[]{:S(2)}) collective-permute-start(bf16[144,768]{1,0:T(8,128)(2,1)S(1)} %get-tuple-element.45), channel_id=1, source_target_pairs={{0,4},{4,0},{8,12},{12,8},{16,20},{20,16},{24,28},{28,24},{1,5},{5... | collective-permute-start | bytes 663560 | tf_op jit(solution)/shard_map/ppermute | solution.py:462
  7.0 5.8 %collective-permute-start.2 = (bf16[16,1024]{1,0:T(8,128)(2,1)S(1)}, bf16[16,1024]{1,0:T(8,128)(2,1)S(1)}, u32[]{:S(2)}, u32[]{:S(2)}) collective-permute-start(bf16[16,1024]{1,0:T(8,128)(2,1)S(1)} %get-tuple-element.46.own_edge_ref), channel_id=1, source_target_pairs={{0,8},{4,12},{8,16},{12,20},{16,24},{20,28},{24,0},{28,4},{1,9},{5... | collective-permute-start | bytes 98312 | tf_op jit(solution)/shard_map/ppermute | solution.py:463
  8.6 8.2 %collective-permute-start.3 = (bf16[128,768]{1,0:T(8,128)(2,1)S(1)}, bf16[128,768]{1,0:T(8,128)(2,1)S(1)}, u32[]{:S(2)}, u32[]{:S(2)}) collective-permute-start(bf16[128,768]{1,0:T(8,128)(2,1)S(1)} %get-tuple-element.53), channel_id=1, source_target_pairs={{0,4},{4,0},{8,12},{12,8},{16,20},{20,16},{24,28},{28,24},{1,5},{5... | collective-permute-start | bytes 589832 | tf_op jit(solution)/shard_map/ppermute | solution.py:464
  15.8 6.8 %copy-start = (f32[128]{0:T(128)S(1)}, f32[128]{0:T(128)}, u32[]{:S(2)}) copy-start(f32[128]{0:T(128)} %param.21) | copy-start | bytes 1540
  15.8 6.8 %collective-permute-start.4 = (bf16[4,128,128]{2,1,0:T(8,128)(2,1)S(1)}, bf16[4,128,128]{2,1,0:T(8,128)(2,1)S(1)}, u32[]{:S(2)}, u32[]{:S(2)}) collective-permute-start(bf16[4,128,128]{2,1,0:T(8,128)(2,1)S(1)} %get-tuple-element.56), channel_id=1, source_target_pairs={{0,8},{4,12},{8,16},{12,20},{16,24},{20,28},{24,0},{28,4},{1,9},{5... | collective-permute-start | bytes 393224 | tf_op jit(solution)/shard_map/ppermute | solution.py:493
  23.7 2.0 %collective-permute-start.5 = (bf16[256,1024]{1,0:T(8,128)(2,1)S(1)}, bf16[256,1024]{1,0:T(8,128)(2,1)S(1)}, u32[]{:S(2)}, u32[]{:S(2)}) collective-permute-start(bf16[256,1024]{1,0:T(8,128)(2,1)S(1)} %get-tuple-element.60), channel_id=1, source_target_pairs={{0,1},{1,0},{2,3},{3,2},{4,5},{5,4},{6,7},{7,6},{8,9},{9,8},{10,11... | collective-permute-start | bytes 1572872 | tf_op jit(solution)/shard_map/ppermute | solution.py:514
  25.8 5.9 %collective-permute-start.6 = (bf16[128,512]{1,0:T(8,128)(2,1)S(1)}, bf16[128,512]{1,0:T(8,128)(2,1)S(1)}, u32[]{:S(2)}, u32[]{:S(2)}) collective-permute-start(bf16[128,512]{1,0:T(8,128)(2,1)S(1)} %get-tuple-element.62), channel_id=1, source_target_pairs={{0,2},{1,3},{2,0},{3,1},{4,6},{5,7},{6,4},{7,5},{8,10},{9,11},{10,... | collective-permute-start | bytes 393224 | tf_op jit(solution)/shard_map/ppermute | solution.py:525
  27.4 8.1 %collective-permute-start.7 = (bf16[128,512]{1,0:T(8,128)(2,1)S(1)}, bf16[128,512]{1,0:T(8,128)(2,1)S(1)}, u32[]{:S(2)}, u32[]{:S(2)}) collective-permute-start(bf16[128,512]{1,0:T(8,128)(2,1)S(1)} %get-tuple-element.63), channel_id=1, source_target_pairs={{0,4},{4,0},{8,12},{12,8},{16,20},{20,16},{24,28},{28,24},{1,5},{5... | collective-permute-start | bytes 393224 | tf_op jit(solution)/shard_map/ppermute | solution.py:526
  28.2 7.3 %collective-permute-start.8 = (bf16[128,512]{1,0:T(8,128)(2,1)S(1)}, bf16[128,512]{1,0:T(8,128)(2,1)S(1)}, u32[]{:S(2)}, u32[]{:S(2)}) collective-permute-start(bf16[128,512]{1,0:T(8,128)(2,1)S(1)} %get-tuple-element.64), channel_id=1, source_target_pairs={{0,6},{1,7},{2,4},{3,5},{4,2},{5,3},{6,0},{7,1},{8,14},{9,15},{10,... | collective-permute-start | bytes 393224 | tf_op jit(solution)/shard_map/ppermute | solution.py:524

commit v4 on v3

--- a/solution.py
+++ b/solution.py
@@ -378,9 +378,15 @@
         ).astype(BF16)
 
 
-def core_sum_kernel(keep_ref, got_ref, mine_ref, x_ref, y_ref, xy_ref):
+def core_sum_kernel(keep_ref, got_ref, xy_ref):
+    rows, width = xy_ref.shape
+    at = (slice(rows, 2 * rows), slice(width, 2 * width))
+    xy_ref[...] = (keep_ref[at].astype(F32) + got_ref[at].astype(F32)).astype(BF16)
+
+
+def core_sums_kernel(keep_ref, got_ref, mine_ref, x_ref, y_ref):
     rows, width = mine_ref.shape
-    for ref, r, c in ((xy_ref, 1, 1), (x_ref, 0, 1), (y_ref, 1, 0), (mine_ref, 0, 0)):
+    for ref, r, c in ((x_ref, 0, 1), (y_ref, 1, 0), (mine_ref, 0, 0)):
         at = (slice(r * rows, r * rows + rows), slice(c * width, c * width + width))
         ref[...] = (keep_ref[at].astype(F32) + got_ref[at].astype(F32)).astype(ref.dtype)
 
@@ -430,7 +436,9 @@
 
     swap = [(i, i ^ 1) for i in range(ctx_count)]
     ahead_1 = [(i, (i + 1) % ctx_count) for i in range(ctx_count)]
-    ahead_2 = [(i, (i + 2) % ctx_count) for i in range(ctx_count)]
+    pair_ahead = [(i, i + 2) for i in range(ctx_count - 2)]
+    ring = [1 + 2 * p for p in range(ctx_count // 2)] + [2 * p for p in reversed(range(ctx_count // 2))]
+    along_ring = [(ring[i], ring[(i + 1) % ctx_count]) for i in range(ctx_count)]
 
     edge, pack, gates = call(
         pack_kernel,
@@ -460,8 +468,7 @@
     )
     got_edge = lax.ppermute(edge, "ctx", ahead_1)
     got_pack = lax.ppermute(pack, "ctx", swap)
-    got_far_edge = lax.ppermute(own_edge, "ctx", ahead_2)
-    got_late = lax.ppermute(late, "ctx", swap)
+    got_far_edge = lax.ppermute(own_edge, "ctx", along_ring)
 
     square = (heads, DK, DV)
     own_state, own_map, own_out, own_through = call(
@@ -472,6 +479,8 @@
         flops=20_000_000_000,
         moved=4_000_000,
     )
+    late, own_map = lax.optimization_barrier((late, own_map))
+    got_late = lax.ppermute(late, "ctx", swap)
     peer = call(
         peer_kernel,
         [
@@ -490,10 +499,10 @@
         moved=4_000_000,
     )
     state, map_, solved, decay, start, key, end = peer[:7]
-    entering = lax.ppermute(end, "ctx", ahead_2)
+    entering = lax.ppermute(end, "ctx", pair_ahead)
     for _ in range(hops - 1):
         moved = jnp.einsum("hij,hjk->hik", peer[7], entering, preferred_element_type=F32)
-        entering = lax.ppermute((end.astype(F32) + moved).astype(BF16), "ctx", ahead_2)
+        entering = lax.ppermute((end.astype(F32) + moved).astype(BF16), "ctx", pair_ahead)
     out, through, weight = call(
         local_kernel,
         [((2 * rows, value_width), F32), ((2 * rows, value_width), BF16), ((4, value_width, width), BF16)],
@@ -512,11 +521,14 @@
         "project",
     )
     got = lax.ppermute(send, "head", [(i, i ^ 1) for i in range(head_count)])
-    mine, to_x, to_y, to_xy = call(
-        core_sum_kernel,
-        [((rows, width), F32), ((rows, width), BF16), ((rows, width), BF16), ((rows, width), BF16)],
+    (to_xy,) = call(core_sum_kernel, [((rows, width), BF16)], (keep, got), "core_sum_xy")
+    mine, to_x, to_y = call(
+        core_sums_kernel,
+        [((rows, width), F32), ((rows, width), BF16), ((rows, width), BF16)],
         (keep, got),
-        "core_sum",
+        "core_sums",
+        flops=2_000_000_000,
+        moved=1_000_000,
     )
     both = [
         (c * head_count + h, (c ^ 1) * head_count + (h ^ 2)) for c in range(ctx_count) for h in range(head_count)

time: 36.4 us -> 34.2 us (0.940)
  waiting for transfers between devices: 13.2 us -> 9.85 us
  starting transfers between devices: 11.2 us -> 12.3 us
    ppermute x2, waiting for transfers between devices: 4.79 us -> 0.42 us  [the longest x1 0.41 us: body(): entering = lax.ppermute(end, 'ctx', pair_ahead)]
    ppermute x1, waiting for transfers between devices: 0.01 us -> 1.56 us  [body(): got_edge = lax.ppermute(edge, 'ctx', ahead_1)]
    ppermute x2, starting transfers between devices: 2.56 us -> 4.04 us  [the longest x1 3.48 us: body(): entering = lax.ppermute(end, 'ctx', pair_ahead)]
    ppermute x1, waiting for transfers between devices: 0.44 us -> 0.01 us  [body(): got_pack = lax.ppermute(pack, 'ctx', swap)]
    ppermute x1, starting transfers between devices: 0.51 us -> 0.08 us  [body(): got_late = lax.ppermute(late, 'ctx', swap)]
    pallas_call x8 -> x9, Pallas kernels: 11.7 us -> 11.7 us  [call(): pl.pallas_call(kernel, out_shape=[jax.ShapeDtypeStruct(shape, kind) for s...]
  transfers between devices with their start and end apart: 9 -> 9, of which waited for: 6 -> 5; matrix products, arithmetic and copies ran while one was open for 0% -> 0% of each run, Pallas kernels for 24% -> 26%
where the time goes in v4:
time: 34.2 us; the launch traced here: 34 us
  starting transfers between devices  12.3 us (36%)
  Pallas kernels  11.7 us (34%)
  waiting for transfers between devices  9.85 us (29%)
    pallas_call x9, Pallas kernels, call(): pl.pallas_call(kernel, out_shape=[jax.ShapeDtypeStruct(shape, kind) for s...  11.7 us
    ppermute x1, waiting for transfers between devices, body(): got_y = lax.ppermute(to_y, 'ctx', swap)  3.77 us
    ppermute x1, starting transfers between devices, body(): entering = lax.ppermute(end, 'ctx', pair_ahead)  3.48 us
    ppermute x1, starting transfers between devices, body(): got_edge = lax.ppermute(edge, 'ctx', ahead_1)  3.02 us
    ppermute x1, waiting for transfers between devices, body(): got_x = lax.ppermute(to_x, 'head', [(i, i ^ 2) for i in range(head_count)])  2.19 us
    ppermute x1, waiting for transfers between devices, body(): got = lax.ppermute(send, 'head', [(i, i ^ 1) for i in range(head_count)])  1.9 us
    ppermute x1, waiting for transfers between devices, body(): got_edge = lax.ppermute(edge, 'ctx', ahead_1)  1.56 us
    ppermute x1, starting transfers between devices, body(): got_x = lax.ppermute(to_x, 'head', [(i, i ^ 2) for i in range(head_count)])  1.55 us
  transfers between devices with their start and end apart: 9, of which 5 were waited for; matrix products, arithmetic and copies ran while one was open for 0% of the time, Pallas kernels for 26%

profile of v4, /device:TPU:0, one launch (start us, length us, event | category | flops | bytes accessed | tf_op | source)
XLA Modules:
  0.0 34.0 jit_solution(16303981870029635411)
XLA Ops:
  0.0 1.1 %pack.1 = (bf16[16,1024]{1,0:T(8,128)(2,1)S(1)}, bf16[144,768]{1,0:T(8,128)(2,1)S(1)}, f32[8,128]{1,0:T(8,128)S(1)}) custom-call(bf16[128,512]{1,0:T(8,128)(2,1)} %q_ref.3, bf16[128,512]{1,0:T(8,128)(2,1)} %k_ref.3, bf16[128,1024]{1,0:T(8,128)(2,1)} %v_ref.3, f32[8,128]{1,0:T(8,128)} %decay_ref.1, f32[8,128]{1,0:T(8,128)} %beta_ref.1), custom_call_target="tpu_custom_call" | custom-call | tf_op jit(solution)/shard_map/pack/pallas_call | solution.py:402
  1.1 3.0 %collective-permute-start = (bf16[16,1024]{1,0:T(8,128)(2,1)S(1)}, bf16[16,1024]{1,0:T(8,128)(2,1)S(1)}, u32[]{:S(2)}, u32[]{:S(2)}) collective-permute-start(bf16[16,1024]{1,0:T(8,128)(2,1)S(1)} %get-tuple-element.41), channel_id=1, source_target_pairs={{0,4},{4,8},{8,12},{12,16},{16,20},{20,24},{24,28},{28,0},{1,5},{5... | collective-permute-start | bytes 98312 | tf_op jit(solution)/shard_map/ppermute | solution.py:469
  4.1 1.5 %collective-permute-start.1 = (bf16[144,768]{1,0:T(8,128)(2,1)S(1)}, bf16[144,768]{1,0:T(8,128)(2,1)S(1)}, u32[]{:S(2)}, u32[]{:S(2)}) collective-permute-start(bf16[144,768]{1,0:T(8,128)(2,1)S(1)} %get-tuple-element.48), channel_id=1, source_target_pairs={{0,4},{4,0},{8,12},{12,8},{16,20},{20,16},{24,28},{28,24},{1,5},{5... | collective-permute-start | bytes 663560 | tf_op jit(solution)/shard_map/ppermute | solution.py:470
  5.6 1.3 %early.1 = (bf16[16,1024]{1,0:T(8,128)(2,1)S(1)}, bf16[128,768]{1,0:T(8,128)(2,1)S(1)}, bf16[128,1024]{1,0:T(8,128)(2,1)S(1)}, f32[4,1024]{1,0:T(4,128)S(1)}, bf...) custom-call(bf16[128,512]{1,0:T(8,128)(2,1)} %q_ref.3, bf16[128,512]{1,0:T(8,128)(2,1)} %k_ref.3, ...), custom_call_target="tpu_custom_call" | custom-call | flops 10000000000 | bytes 2000000 | tf_op jit(solution)/shard_map/early/pallas_call | solution.py:402
  7.0 0.6 %collective-permute-start.2 = (bf16[16,1024]{1,0:T(8,128)(2,1)S(1)}, bf16[16,1024]{1,0:T(8,128)(2,1)S(1)}, u32[]{:S(2)}, u32[]{:S(2)}) collective-permute-start(bf16[16,1024]{1,0:T(8,128)(2,1)S(1)} %get-tuple-element.49.own_edge_ref), channel_id=1, source_target_pairs={{4,12},{12,20},{20,28},{28,24},{24,16},{16,8},{8,0},{0,4},{5,13},{... | collective-permute-start | bytes 98312 | tf_op jit(solution)/shard_map/ppermute | solution.py:471
  7.5 1.6 %collective-permute-done.halo_ref = bf16[16,1024]{1,0:T(8,128)(2,1)S(1)} collective-permute-done((bf16[16,1024]{1,0:T(8,128)(2,1)S(1)}, bf16[16,1024]{1,0:T(8,128)(2,1)S(1)}, u32[]{:S(2)}, u32[]{:S(2)}) %collective-permute-start) | collective-permute-done | bytes 32800 | tf_op jit(solution)/shard_map/ppermute | solution.py:469
  9.1 2.6 %own_terms.1 = (f32[4,128,128]{2,1,0:T(8,128)S(1)}, bf16[4,128,128]{2,1,0:T(8,128)(2,1)S(1)}, f32[128,512]{1,0:T(8,128)S(1)}, bf16[128,512]{1,0:T(8,128)(2,1)S(1)}) custom-call(s32[264,128]{1,0:T(8,128)S(1)} %get-tuple-element.36.down_ref, s32[8,256]{1,0:T(8,128)S(1)} %get-tuple-element.37.along_ref, bf16[128,1024]{1,0:T(8,128)(2,1)S(1)} %get-tuple-element.38.own_ref, ...), custom_call_target="tpu_custom_call" | custom-call | flops 20000000000 | bytes 4000000 | tf_op jit(solution)/shard_map/own_terms/pallas_call | solution.py:402
  11.7 0.1 collective-permute-start.3
  11.8 0.0 collective-permute-done.2.edge_ref
  11.8 2.7 %peer_terms.1 = (f32[4,128,128]{2,1,0:T(8,128)S(1)}, bf16[4,128,128]{2,1,0:T(8,128)(2,1)S(1)}, bf16[4,128,256]{2,1,0:T(8,128)(2,1)S(1)}, f32[4,128,128]{2,1,0:T(...) custom-call(s32[264,128]{1,0:T(8,128)S(1)} %get-tuple-element.36.down_ref, ...), custom_call_target="tpu_custom_call" | custom-call | flops 2000000000 | bytes 4000000 | tf_op jit(solution)/shard_map/peer_terms/pallas_call | solution.py:402
  14.5 0.0 copy-start
  14.5 3.5 %collective-permute-start.4 = (bf16[4,128,128]{2,1,0:T(8,128)(2,1)S(1)}, bf16[4,128,128]{2,1,0:T(8,128)(2,1)S(1)}, u32[]{:S(2)}, u32[]{:S(2)}) collective-permute-start(bf16[4,128,128]{2,1,0:T(8,128)(2,1)S(1)} %get-tuple-element.59), channel_id=1, source_target_pairs={{0,8},{4,12},{8,16},{12,20},{16,24},{20,28},{1,9},{5,13},{9,17},{1... | collective-permute-start | bytes 393224 | tf_op jit(solution)/shard_map/ppermute | solution.py:502
  18.0 2.1 %local_outputs.1 = (f32[256,512]{1,0:T(8,128)S(1)}, bf16[256,512]{1,0:T(8,128)(2,1)S(1)}, bf16[4,512,512]{2,1,0:T(8,128)(2,1)S(1)}) custom-call(f32[4,128,128]{2,1,0:T(8,128)S(1)} %get-tuple-element.42.own_state_ref, bf16[4,128,128]{2,1,0:T(8,128)(2,1)S(1)} %get-tuple-element.45.own_map_ref, f32[128,512]{1,0:T(8,128)S(1)} %get-tuple-element.46.own_out_ref, ...), custom_call_target="tpu_custom_call" | custom-call | flops 1000000000 | bytes 4000000 | tf_op jit(solution)/shard_map/local_outputs/pallas_call | solution.py:402
  20.1 0.4 %collective-permute-done.4.enter_ref = bf16[4,128,128]{2,1,0:T(8,128)(2,1)S(1)} collective-permute-done((bf16[4,128,128]{2,1,0:T(8,128)(2,1)S(1)}, bf16[4,128,128]{2,1,0:T(8,128)(2,1)S(1)}, u32[]{:S(2)}, u32[]{:S(2)}) %collective-permute-start.4) | collective-permute-done | bytes 131104 | tf_op jit(solution)/shard_map/ppermute | solution.py:502
  20.5 1.0 %project.1 = (bf16[256,1024]{1,0:T(8,128)(2,1)S(1)}, bf16[256,1024]{1,0:T(8,128)(2,1)S(1)}) custom-call(f32[256,512]{1,0:T(8,128)S(1)} %get-tuple-element.57.out_ref, bf16[256,512]{1,0:T(8,128)(2,1)S(1)} %get-tuple-element.58.through_ref, bf16[4,128,128]{2,1,0:T(8,128)(2,1)S(1)} %collective-permute-done.4.enter_ref, ...), custom_call_target="tpu_custom_call" | custom-call | tf_op jit(solution)/shard_map/project/pallas_call | solution.py:402
  21.5 0.1 collective-permute-start.5
  21.6 1.9 %collective-permute-done.5.got_ref = bf16[256,1024]{1,0:T(8,128)(2,1)S(1)} collective-permute-done((bf16[256,1024]{1,0:T(8,128)(2,1)S(1)}, bf16[256,1024]{1,0:T(8,128)(2,1)S(1)}, u32[]{:S(2)}, u32[]{:S(2)}) %collective-permute-start.5) | collective-permute-done | bytes 524320 | tf_op jit(solution)/shard_map/ppermute | solution.py:523
  23.5 0.1 core_sums.1
  23.6 1.6 %collective-permute-start.6 = (bf16[128,512]{1,0:T(8,128)(2,1)S(1)}, bf16[128,512]{1,0:T(8,128)(2,1)S(1)}, u32[]{:S(2)}, u32[]{:S(2)}) collective-permute-start(bf16[128,512]{1,0:T(8,128)(2,1)S(1)} %get-tuple-element.65), channel_id=1, source_target_pairs={{0,2},{1,3},{2,0},{3,1},{4,6},{5,7},{6,4},{7,5},{8,10},{9,11},{10,... | collective-permute-start | bytes 393224 | tf_op jit(solution)/shard_map/ppermute | solution.py:537
  25.2 0.9 %collective-permute-start.7 = (bf16[128,512]{1,0:T(8,128)(2,1)S(1)}, bf16[128,512]{1,0:T(8,128)(2,1)S(1)}, u32[]{:S(2)}, u32[]{:S(2)}) collective-permute-start(bf16[128,512]{1,0:T(8,128)(2,1)S(1)} %get-tuple-element.66), channel_id=1, source_target_pairs={{0,4},{4,0},{8,12},{12,8},{16,20},{20,16},{24,28},{28,24},{1,5},{5... | collective-permute-start | bytes 393224 | tf_op jit(solution)/shard_map/ppermute | solution.py:538
  26.1 1.1 %collective-permute-start.8 = (bf16[128,512]{1,0:T(8,128)(2,1)S(1)}, bf16[128,512]{1,0:T(8,128)(2,1)S(1)}, u32[]{:S(2)}, u32[]{:S(2)}) collective-permute-start(bf16[128,512]{1,0:T(8,128)(2,1)S(1)} %core_sum_xy.1), channel_id=1, source_target_pairs={{0,6},{1,7},{2,4},{3,5},{4,2},{5,3},{6,0},{7,1},{8,14},{9,15},{10,... | collective-permute-start | bytes 393224 | tf_op jit(solution)/shard_map/ppermute | solution.py:536
  27.3 2.2 %collective-permute-done.6.x_ref = bf16[128,512]{1,0:T(8,128)(2,1)S(1)} collective-permute-done((bf16[128,512]{1,0:T(8,128)(2,1)S(1)}, bf16[128,512]{1,0:T(8,128)(2,1)S(1)}, u32[]{:S(2)}, u32[]{:S(2)}) %collective-permute-start.6) | collective-permute-done | bytes 131104 | tf_op jit(solution)/shard_map/ppermute | solution.py:537
  29.5 3.8 %collective-permute-done.7.y_ref = bf16[128,512]{1,0:T(8,128)(2,1)S(1)} collective-permute-done((bf16[128,512]{1,0:T(8,128)(2,1)S(1)}, bf16[128,512]{1,0:T(8,128)(2,1)S(1)}, u32[]{:S(2)}, u32[]{:S(2)}) %collective-permute-start.7) | collective-permute-done | bytes 131104 | tf_op jit(solution)/shard_map/ppermute | solution.py:538
  33.2 0.8 %last_sum.1 = bf16[512,128]{1,0:T(8,128)(2,1)} custom-call(f32[128,512]{1,0:T(8,128)S(1)} %get-tuple-element.64.mine_ref, bf16[128,512]{1,0:T(8,128)(2,1)S(1)} %collective-permute-done.6.x_ref, bf16[128,512]{1,0:T(8,128)(2,1)S(1)} %collective-permute-done.7.y_ref, bf16[128,512]{1,0:T(8,128)(2,1)S(1)} %collective-permute-done.8.xy_ref), custom_call_target="tpu_custom_call" | custom-call | tf_op jit(solution)/shard_map/last_sum/pallas_call | solution.py:402
  (5 shorter events, 0.0 us)
Async XLA Ops:
  1.1 8.0 %collective-permute-start = (bf16[16,1024]{1,0:T(8,128)(2,1)S(1)}, bf16[16,1024]{1,0:T(8,128)(2,1)S(1)}, u32[]{:S(2)}, u32[]{:S(2)}) collective-permute-start(bf16[16,1024]{1,0:T(8,128)(2,1)S(1)} %get-tuple-element.41), channel_id=1, source_target_pairs={{0,4},{4,8},{8,12},{12,16},{16,20},{20,24},{24,28},{28,0},{1,5},{5... | collective-permute-start | bytes 98312 | tf_op jit(solution)/shard_map/ppermute | solution.py:469
  4.1 7.7 %collective-permute-start.1 = (bf16[144,768]{1,0:T(8,128)(2,1)S(1)}, bf16[144,768]{1,0:T(8,128)(2,1)S(1)}, u32[]{:S(2)}, u32[]{:S(2)}) collective-permute-start(bf16[144,768]{1,0:T(8,128)(2,1)S(1)} %get-tuple-element.48), channel_id=1, source_target_pairs={{0,4},{4,0},{8,12},{12,8},{16,20},{20,16},{24,28},{28,24},{1,5},{5... | collective-permute-start | bytes 663560 | tf_op jit(solution)/shard_map/ppermute | solution.py:470
  7.0 4.9 %collective-permute-start.2 = (bf16[16,1024]{1,0:T(8,128)(2,1)S(1)}, bf16[16,1024]{1,0:T(8,128)(2,1)S(1)}, u32[]{:S(2)}, u32[]{:S(2)}) collective-permute-start(bf16[16,1024]{1,0:T(8,128)(2,1)S(1)} %get-tuple-element.49.own_edge_ref), channel_id=1, source_target_pairs={{4,12},{12,20},{20,28},{28,24},{24,16},{16,8},{8,0},{0,4},{5,13},{... | collective-permute-start | bytes 98312 | tf_op jit(solution)/shard_map/ppermute | solution.py:471
  11.7 6.3 %collective-permute-start.3 = (bf16[128,768]{1,0:T(8,128)(2,1)S(1)}, bf16[128,768]{1,0:T(8,128)(2,1)S(1)}, u32[]{:S(2)}, u32[]{:S(2)}) collective-permute-start(bf16[128,768]{1,0:T(8,128)(2,1)S(1)} %get-tuple-element.56), channel_id=1, source_target_pairs={{0,4},{4,0},{8,12},{12,8},{16,20},{20,16},{24,28},{28,24},{1,5},{5... | collective-permute-start | bytes 589832 | tf_op jit(solution)/shard_map/ppermute | solution.py:483
  14.5 6.0 %copy-start = (f32[128]{0:T(128)S(1)}, f32[128]{0:T(128)}, u32[]{:S(2)}) copy-start(f32[128]{0:T(128)} %param.21) | copy-start | bytes 1540
  14.5 6.0 %collective-permute-start.4 = (bf16[4,128,128]{2,1,0:T(8,128)(2,1)S(1)}, bf16[4,128,128]{2,1,0:T(8,128)(2,1)S(1)}, u32[]{:S(2)}, u32[]{:S(2)}) collective-permute-start(bf16[4,128,128]{2,1,0:T(8,128)(2,1)S(1)} %get-tuple-element.59), channel_id=1, source_target_pairs={{0,8},{4,12},{8,16},{12,20},{16,24},{20,28},{1,9},{5,13},{9,17},{1... | collective-permute-start | bytes 393224 | tf_op jit(solution)/shard_map/ppermute | solution.py:502
  21.5 2.0 %collective-permute-start.5 = (bf16[256,1024]{1,0:T(8,128)(2,1)S(1)}, bf16[256,1024]{1,0:T(8,128)(2,1)S(1)}, u32[]{:S(2)}, u32[]{:S(2)}) collective-permute-start(bf16[256,1024]{1,0:T(8,128)(2,1)S(1)} %get-tuple-element.63), channel_id=1, source_target_pairs={{0,1},{1,0},{2,3},{3,2},{4,5},{5,4},{6,7},{7,6},{8,9},{9,8},{10,11... | collective-permute-start | bytes 1572872 | tf_op jit(solution)/shard_map/ppermute | solution.py:523
  23.6 5.9 %collective-permute-start.6 = (bf16[128,512]{1,0:T(8,128)(2,1)S(1)}, bf16[128,512]{1,0:T(8,128)(2,1)S(1)}, u32[]{:S(2)}, u32[]{:S(2)}) collective-permute-start(bf16[128,512]{1,0:T(8,128)(2,1)S(1)} %get-tuple-element.65), channel_id=1, source_target_pairs={{0,2},{1,3},{2,0},{3,1},{4,6},{5,7},{6,4},{7,5},{8,10},{9,11},{10,... | collective-permute-start | bytes 393224 | tf_op jit(solution)/shard_map/ppermute | solution.py:537
  25.2 8.1 %collective-permute-start.7 = (bf16[128,512]{1,0:T(8,128)(2,1)S(1)}, bf16[128,512]{1,0:T(8,128)(2,1)S(1)}, u32[]{:S(2)}, u32[]{:S(2)}) collective-permute-start(bf16[128,512]{1,0:T(8,128)(2,1)S(1)} %get-tuple-element.66), channel_id=1, source_target_pairs={{0,4},{4,0},{8,12},{12,8},{16,20},{20,16},{24,28},{28,24},{1,5},{5... | collective-permute-start | bytes 393224 | tf_op jit(solution)/shard_map/ppermute | solution.py:538
  26.1 7.1 %collective-permute-start.8 = (bf16[128,512]{1,0:T(8,128)(2,1)S(1)}, bf16[128,512]{1,0:T(8,128)(2,1)S(1)}, u32[]{:S(2)}, u32[]{:S(2)}) collective-permute-start(bf16[128,512]{1,0:T(8,128)(2,1)S(1)} %core_sum_xy.1), channel_id=1, source_target_pairs={{0,6},{1,7},{2,4},{3,5},{4,2},{5,3},{6,0},{7,1},{8,14},{9,15},{10,... | collective-permute-start | bytes 393224 | tf_op jit(solution)/shard_map/ppermute | solution.py:536

commit v5 on v4

--- a/solution.py
+++ b/solution.py
@@ -158,6 +158,30 @@
     return [None] + [(seg_down[8 - lag : 8 - lag + seg.shape[0]] == seg).astype(F32) for lag in (1, 2, 3)]
 
 
+def solve_terms(lower):
+    rows = lower[0].shape[0]
+    small, large = rows // 8, rows // 4
+    row = lax.broadcasted_iota(jnp.int32, (rows, rows), 0)
+    col = lax.broadcasted_iota(jnp.int32, (rows, rows), 1)
+    power = [jnp.where(row // small == col // small, -x, 0.0) for x in lower]
+    eye = (row == col).astype(F32)
+    inverse = [eye + x for x in power]
+    power = [x.astype(BF16) for x in power]
+    reach = 2
+    while reach < small:
+        power = [dot(x, x).astype(BF16) for x in power]
+        inverse = [x + dot(x, p) for x, p in zip(inverse, power)]
+        reach *= 2
+    here = (row // large == col // large) & (row // small != col // small)
+    moved = [dot(odd_blocks(jnp.where(here, x, 0.0), small), i) for x, i in zip(lower, inverse)]
+    moved = [dot(odd_blocks(i, small), at_odd_blocks(m, small)) for i, m in zip(inverse, moved)]
+    inverse = [(i - at_odd_blocks(m, small)).astype(BF16) for i, m in zip(inverse, moved)]
+    rest = [jnp.where(row // large == col // large, 0.0, -x) for x in lower]
+    once = [dot(i, r).astype(BF16) for i, r in zip(inverse, rest)]
+    twice = [dot(m, m).astype(BF16) for m in once]
+    return inverse, once, twice
+
+
 def state_terms(seg_down, seg_along, halo, k, v, weights, sums, beta):
     heads, rows = sums.shape
     key_heads = heads // 2
@@ -195,24 +219,11 @@
         ends.append((keys_t[g] * jnp.where(seg_along[0:1] == last, jnp.exp(end - along), 0.0)).astype(BF16))
         throughs.append(jnp.where(last == before, jnp.exp(end), 0.0))
 
-    small = 16
+    inverse, once, twice = solve_terms(lower)
+    solved = [dot(i, r) for i, r in zip(inverse, rhs)]
+    solved = [s + dot(m, s) for m, s in zip(once, solved)]
+    solved = [(s + dot(m, s)).astype(BF16) for m, s in zip(twice, solved)]
     eye = (row == col).astype(F32)
-    power = [jnp.where(row // small == col // small, -x, 0.0) for x in lower]
-    inverse = [eye + x for x in power]
-    power = [x.astype(BF16) for x in power]
-    reach = 2
-    while reach < small:
-        power = [dot(x, x).astype(BF16) for x in power]
-        inverse = [x + dot(x, p) for x, p in zip(inverse, power)]
-        reach *= 2
-    reach = small
-    while reach < rows:
-        here = (row // (2 * reach) == col // (2 * reach)) & (row // reach != col // reach)
-        moved = [dot(odd_blocks(jnp.where(here, x, 0.0), reach), i) for x, i in zip(lower, inverse)]
-        moved = [dot(odd_blocks(i, reach), at_odd_blocks(m, reach)) for i, m in zip(inverse, moved)]
-        inverse = [i - at_odd_blocks(m, reach) for i, m in zip(inverse, moved)]
-        reach *= 2
-    solved = [dot(i, r).astype(BF16) for i, r in zip(inverse, rhs)]
     ended = [dot(e, s) for e, s in zip(ends, solved)]
     states = [e[:, :DV] for e in ended]
     maps = [t * eye - e[:, DV:] for t, e in zip(throughs, ended)]
@@ -359,36 +370,40 @@
         copy.wait()
 
 
-def project_kernel(out_ref, through_ref, enter_ref, gate_ref, late_ref, gain_ref, weight_ref, send_ref, keep_ref):
-    heads = enter_ref.shape[0]
+def mix_kernel(out_ref, through_ref, even_ref, odd_ref, gate_ref, late_ref, gain_ref, weight_ref, mixed_ref, send_ref, keep_ref):
+    from_even = lax.axis_index("ctx") // 2 % 2
+    heads = even_ref.shape[0]
+    rows = gate_ref.shape[0]
     key_width = late_ref.shape[1] - heads * DV
-    width = weight_ref.shape[2]
-    mixed = []
     for h in range(heads):
         lanes = slice(h * DV, h * DV + DV)
-        o = out_ref[:, lanes] + dot(through_ref[:, lanes], enter_ref[h])
-        gate = jnp.concatenate([gate_ref[:, lanes], late_ref[:, key_width + h * DV : key_width + h * DV + DV]], axis=0).astype(F32)
+        o = out_ref[:, lanes] + dot(through_ref[:, lanes], where_y(from_even, even_ref[h], odd_ref[h]))
+        gate = jnp.concatenate([gate_ref[:, lanes], late_ref[:, key_width + h * DV : key_width + h * DV + DV]], axis=0)
+        gate = gate.astype(F32)
         scale = lax.rsqrt(jnp.mean(o * o, axis=-1, keepdims=True) + 1e-6)
-        mixed.append((o * scale * gain_ref[...] * (gate / (1.0 + jnp.exp(-gate)))).astype(BF16))
-    mixed = jnp.concatenate(mixed, axis=1)
-    for i in range(4):
-        to_ref = (send_ref, keep_ref)[i // 2]
-        to_ref[:, (i % 2) * width : (i % 2 + 1) * width] = jnp.dot(
-            mixed, weight_ref[i], preferred_element_type=F32
-        ).astype(BF16)
+        mixed_ref[:, lanes] = (o * scale * gain_ref[...] * (gate / (1.0 + jnp.exp(-gate)))).astype(BF16)
+    send_ref[...] = jnp.dot(mixed_ref[rows:, :], weight_ref[1], preferred_element_type=F32).astype(BF16)
+    keep_ref[...] = jnp.dot(mixed_ref[rows:, :], weight_ref[3], preferred_element_type=F32).astype(BF16)
+
+
+QUARTERS = ((0, 0), (0, 1), (1, 0))
+
+
+def project_kernel(mixed_ref, weight_ref, send_ref, keep_ref):
+    rows = send_ref.shape[1]
+    for c, to_ref in ((0, send_ref), (1, keep_ref)):
+        for i, (peer, far) in enumerate(QUARTERS):
+            product = jnp.dot(mixed_ref[peer * rows : peer * rows + rows, :], weight_ref[2 * c + far], preferred_element_type=F32)
+            to_ref[i] = product.astype(BF16)
 
 
 def core_sum_kernel(keep_ref, got_ref, xy_ref):
-    rows, width = xy_ref.shape
-    at = (slice(rows, 2 * rows), slice(width, 2 * width))
-    xy_ref[...] = (keep_ref[at].astype(F32) + got_ref[at].astype(F32)).astype(BF16)
+    xy_ref[...] = (keep_ref[...].astype(F32) + got_ref[...].astype(F32)).astype(BF16)
 
 
 def core_sums_kernel(keep_ref, got_ref, mine_ref, x_ref, y_ref):
-    rows, width = mine_ref.shape
-    for ref, r, c in ((x_ref, 0, 1), (y_ref, 1, 0), (mine_ref, 0, 0)):
-        at = (slice(r * rows, r * rows + rows), slice(c * width, c * width + width))
-        ref[...] = (keep_ref[at].astype(F32) + got_ref[at].astype(F32)).astype(ref.dtype)
+    for i, ref in enumerate((mine_ref, x_ref, y_ref)):
+        ref[...] = (keep_ref[i].astype(F32) + got_ref[i].astype(F32)).astype(ref.dtype)
 
 
 def last_kernel(mine_ref, x_ref, y_ref, xy_ref, out_ref):
@@ -436,7 +451,12 @@
 
     swap = [(i, i ^ 1) for i in range(ctx_count)]
     ahead_1 = [(i, (i + 1) % ctx_count) for i in range(ctx_count)]
-    pair_ahead = [(i, i + 2) for i in range(ctx_count - 2)]
+    even_swap = [(i, i ^ 2) for i in range(ctx_count)]
+    odd_swap = [
+        (c * head_count + h, (((c + 2) ^ 2) - 2) * head_count + h if 2 <= c < ctx_count - 2 else c * head_count + (h ^ 1))
+        for c in range(ctx_count)
+        for h in range(head_count)
+    ]
     ring = [1 + 2 * p for p in range(ctx_count // 2)] + [2 * p for p in reversed(range(ctx_count // 2))]
     along_ring = [(ring[i], ring[(i + 1) % ctx_count]) for i in range(ctx_count)]
 
@@ -476,7 +496,7 @@
         [(square, F32), (square, BF16), ((rows, value_width), F32), ((rows, value_width), BF16)],
         (down, along, own, weights, gates, got_edge),
         "own_terms",
-        flops=20_000_000_000,
+        flops=1_000_000,
         moved=4_000_000,
     )
     late, own_map = lax.optimization_barrier((late, own_map))
@@ -499,10 +519,15 @@
         moved=4_000_000,
     )
     state, map_, solved, decay, start, key, end = peer[:7]
-    entering = lax.ppermute(end, "ctx", pair_ahead)
+    def from_earlier(value):
+        return lax.ppermute(value, "ctx", even_swap), lax.ppermute(value, ("ctx", "head"), odd_swap)
+
+    entering = from_earlier(end)
     for _ in range(hops - 1):
-        moved = jnp.einsum("hij,hjk->hik", peer[7], entering, preferred_element_type=F32)
-        entering = lax.ppermute((end.astype(F32) + moved).astype(BF16), "ctx", pair_ahead)
+        earlier = jnp.where(lax.axis_index("ctx") // 2 % 2 == 1, *entering)
+        moved = jnp.einsum("hij,hjk->hik", peer[7], earlier, preferred_element_type=F32)
+        moved = jnp.where(lax.axis_index("ctx") < 2, 0.0, moved)
+        entering = from_earlier((end.astype(F32) + moved).astype(BF16))
     out, through, weight = call(
         local_kernel,
         [((2 * rows, value_width), F32), ((2 * rows, value_width), BF16), ((4, value_width, width), BF16)],
@@ -514,21 +539,30 @@
         flops=1_000_000_000,
         moved=4_000_000,
     )
+    cores = [(i, i ^ 1) for i in range(head_count)]
+    mixed, send_far, keep_far = call(
+        mix_kernel,
+        [((2 * rows, value_width), BF16), ((rows, width), BF16), ((rows, width), BF16)],
+        (out, through, *entering, own_gate, got_late, norm_gain.reshape(1, DV), weight),
+        "mix",
+    )
+    got_far = lax.ppermute(send_far, "head", cores)
     send, keep = call(
         project_kernel,
-        [((2 * rows, 2 * width), BF16), ((2 * rows, 2 * width), BF16)],
-        (out, through, entering, own_gate, got_late, norm_gain.reshape(1, DV), weight),
+        [((3, rows, width), BF16), ((3, rows, width), BF16)],
+        (mixed, weight),
         "project",
-    )
-    got = lax.ppermute(send, "head", [(i, i ^ 1) for i in range(head_count)])
-    (to_xy,) = call(core_sum_kernel, [((rows, width), BF16)], (keep, got), "core_sum_xy")
+        flops=2_000_000_000,
+        moved=4_000_000,
+    )
+    send, got_far = lax.optimization_barrier((send, got_far))
+    got = lax.ppermute(send, "head", cores)
+    (to_xy,) = call(core_sum_kernel, [((rows, width), BF16)], (keep_far, got_far), "core_sum_xy")
     mine, to_x, to_y = call(
         core_sums_kernel,
         [((rows, width), F32), ((rows, width), BF16), ((rows, width), BF16)],
         (keep, got),
         "core_sums",
-        flops=2_000_000_000,
-        moved=1_000_000,
     )
     both = [
         (c * head_count + h, (c ^ 1) * head_count + (h ^ 2)) for c in range(ctx_count) for h in range(head_count)

time: 34.2 us -> 33.1 us (0.968)
  waiting for transfers between devices: 9.85 us -> 8.43 us
    ppermute x1, waiting for transfers between devices: 3.77 us -> 0.01 us  [body(): got_y = lax.ppermute(to_y, 'ctx', swap)]
    ppermute x1, waiting for transfers between devices: 0.01 us -> 2.15 us  [body(): got_xy = lax.ppermute(to_xy, ('ctx', 'head'), both)]
    ppermute x1, starting transfers between devices: 1.12 us -> 3.06 us  [body(): got_xy = lax.ppermute(to_xy, ('ctx', 'head'), both)]
    ppermute x2 -> x4, starting transfers between devices: 3.55 us -> 1.85 us  [the longest x1 1.62 us: from_earlier(): lax.ppermute(value, 'ctx', even_swap)]
    ppermute x2 -> x4, waiting for transfers between devices: 2.31 us -> 0.74 us  [the longest x1 0.73 us: body(): got_far = lax.ppermute(send_far, 'head', cores)]
    ppermute x1, waiting for transfers between devices: 0.01 us -> 1.46 us  [body(): got_late = lax.ppermute(late, 'ctx', swap)]
    ppermute x1, starting transfers between devices: 1.55 us -> 0.38 us  [body(): got_x = lax.ppermute(to_x, 'head', [(i, i ^ 2) for i in range(head_count)])]
    ppermute x1, starting transfers between devices: 0.94 us -> 1.71 us  [body(): got_y = lax.ppermute(to_y, 'ctx', swap)]
  transfers between devices with their start and end apart: 9 -> 11, of which waited for: 5 -> 5; matrix products, arithmetic and copies ran while one was open for 0% -> 0% of each run, Pallas kernels for 26% -> 29%
where the time goes in v5:
time: 33.1 us; the launch traced here: 32.6 us
  starting transfers between devices  12.2 us (37%)
  Pallas kernels  11.9 us (36%)
  waiting for transfers between devices  8.43 us (25%)
    pallas_call x10, Pallas kernels, call(): pl.pallas_call(kernel, out_shape=[jax.ShapeDtypeStruct(shape, kind) for s...  11.9 us
    ppermute x1, starting transfers between devices, body(): got_xy = lax.ppermute(to_xy, ('ctx', 'head'), both)  3.06 us
    ppermute x1, starting transfers between devices, body(): got_edge = lax.ppermute(edge, 'ctx', ahead_1)  3.02 us
    ppermute x1, waiting for transfers between devices, body(): got_x = lax.ppermute(to_x, 'head', [(i, i ^ 2) for i in range(head_count)])  2.51 us
    ppermute x1, waiting for transfers between devices, body(): got_xy = lax.ppermute(to_xy, ('ctx', 'head'), both)  2.15 us
    ppermute x1, starting transfers between devices, body(): got_y = lax.ppermute(to_y, 'ctx', swap)  1.71 us
    ppermute x1, starting transfers between devices, from_earlier(): lax.ppermute(value, 'ctx', even_swap)  1.62 us
    ppermute x1, waiting for transfers between devices, body(): got_edge = lax.ppermute(edge, 'ctx', ahead_1)  1.56 us
  transfers between devices with their start and end apart: 11, of which 5 were waited for; matrix products, arithmetic and copies ran while one was open for 0% of the time, Pallas kernels for 29%

profile of v5, /device:TPU:0, one launch (start us, length us, event | category | flops | bytes accessed | tf_op | source)
XLA Modules:
  0.0 32.6 jit_solution(1682812676227287169)
XLA Ops:
  0.0 1.1 %pack.1 = (bf16[16,1024]{1,0:T(8,128)(2,1)S(1)}, bf16[144,768]{1,0:T(8,128)(2,1)S(1)}, f32[8,128]{1,0:T(8,128)S(1)}) custom-call(bf16[128,512]{1,0:T(8,128)(2,1)} %q_ref.3, bf16[128,512]{1,0:T(8,128)(2,1)} %k_ref.3, bf16[128,1024]{1,0:T(8,128)(2,1)} %v_ref.3, f32[8,128]{1,0:T(8,128)} %decay_ref.1, f32[8,128]{1,0:T(8,128)} %beta_ref.1), custom_call_target="tpu_custom_call" | custom-call | tf_op jit(solution)/shard_map/pack/pallas_call | solution.py:417
  1.1 3.0 %collective-permute-start = (bf16[16,1024]{1,0:T(8,128)(2,1)S(1)}, bf16[16,1024]{1,0:T(8,128)(2,1)S(1)}, u32[]{:S(2)}, u32[]{:S(2)}) collective-permute-start(bf16[16,1024]{1,0:T(8,128)(2,1)S(1)} %get-tuple-element.46), channel_id=1, source_target_pairs={{0,4},{4,8},{8,12},{12,16},{16,20},{20,24},{24,28},{28,0},{1,5},{5... | collective-permute-start | bytes 98312 | tf_op jit(solution)/shard_map/ppermute | solution.py:489
  4.1 1.5 %collective-permute-start.1 = (bf16[144,768]{1,0:T(8,128)(2,1)S(1)}, bf16[144,768]{1,0:T(8,128)(2,1)S(1)}, u32[]{:S(2)}, u32[]{:S(2)}) collective-permute-start(bf16[144,768]{1,0:T(8,128)(2,1)S(1)} %get-tuple-element.53), channel_id=1, source_target_pairs={{0,4},{4,0},{8,12},{12,8},{16,20},{20,16},{24,28},{28,24},{1,5},{5... | collective-permute-start | bytes 663560 | tf_op jit(solution)/shard_map/ppermute | solution.py:490
  5.6 1.3 %early.1 = (bf16[16,1024]{1,0:T(8,128)(2,1)S(1)}, bf16[128,768]{1,0:T(8,128)(2,1)S(1)}, bf16[128,1024]{1,0:T(8,128)(2,1)S(1)}, f32[4,1024]{1,0:T(4,128)S(1)}, bf...) custom-call(bf16[128,512]{1,0:T(8,128)(2,1)} %q_ref.3, bf16[128,512]{1,0:T(8,128)(2,1)} %k_ref.3, ...), custom_call_target="tpu_custom_call" | custom-call | flops 10000000000 | bytes 2000000 | tf_op jit(solution)/shard_map/early/pallas_call | solution.py:417
  7.0 0.6 %collective-permute-start.2 = (bf16[16,1024]{1,0:T(8,128)(2,1)S(1)}, bf16[16,1024]{1,0:T(8,128)(2,1)S(1)}, u32[]{:S(2)}, u32[]{:S(2)}) collective-permute-start(bf16[16,1024]{1,0:T(8,128)(2,1)S(1)} %get-tuple-element.54.own_edge_ref), channel_id=1, source_target_pairs={{4,12},{12,20},{20,28},{28,24},{24,16},{16,8},{8,0},{0,4},{5,13},{... | collective-permute-start | bytes 98312 | tf_op jit(solution)/shard_map/ppermute | solution.py:491
  7.5 1.6 %collective-permute-done.halo_ref = bf16[16,1024]{1,0:T(8,128)(2,1)S(1)} collective-permute-done((bf16[16,1024]{1,0:T(8,128)(2,1)S(1)}, bf16[16,1024]{1,0:T(8,128)(2,1)S(1)}, u32[]{:S(2)}, u32[]{:S(2)}) %collective-permute-start) | collective-permute-done | bytes 32800 | tf_op jit(solution)/shard_map/ppermute | solution.py:489
  9.1 2.6 %own_terms.1 = (f32[4,128,128]{2,1,0:T(8,128)S(1)}, bf16[4,128,128]{2,1,0:T(8,128)(2,1)S(1)}, f32[128,512]{1,0:T(8,128)S(1)}, bf16[128,512]{1,0:T(8,128)(2,1)S(1)}) custom-call(s32[264,128]{1,0:T(8,128)S(1)} %get-tuple-element.41.down_ref, s32[8,256]{1,0:T(8,128)S(1)} %get-tuple-element.42.along_ref, bf16[128,1024]{1,0:T(8,128)(2,1)S(1)} %get-tuple-element.43.own_ref, ...), custom_call_target="tpu_custom_call" | custom-call | flops 1000000 | bytes 4000000 | tf_op jit(solution)/shard_map/own_terms/pallas_call | solution.py:417
  11.7 0.1 collective-permute-start.3
  11.8 2.7 %peer_terms.1 = (f32[4,128,128]{2,1,0:T(8,128)S(1)}, bf16[4,128,128]{2,1,0:T(8,128)(2,1)S(1)}, bf16[4,128,256]{2,1,0:T(8,128)(2,1)S(1)}, f32[4,128,128]{2,1,0:T(...) custom-call(s32[264,128]{1,0:T(8,128)S(1)} %get-tuple-element.41.down_ref, ...), custom_call_target="tpu_custom_call" | custom-call | flops 2000000000 | bytes 4000000 | tf_op jit(solution)/shard_map/peer_terms/pallas_call | solution.py:417
  14.5 1.6 %collective-permute-start.4 = (bf16[4,128,128]{2,1,0:T(8,128)(2,1)S(1)}, bf16[4,128,128]{2,1,0:T(8,128)(2,1)S(1)}, u32[]{:S(2)}, u32[]{:S(2)}) collective-permute-start(bf16[4,128,128]{2,1,0:T(8,128)(2,1)S(1)} %get-tuple-element.64), channel_id=1, source_target_pairs={{0,8},{4,12},{8,0},{12,4},{16,24},{20,28},{24,16},{28,20},{1,9},{5... | collective-permute-start | bytes 393224 | tf_op jit(solution)/shard_map/ppermute | solution.py:523
  16.2 1.5 %collective-permute-done.3.late_ref = bf16[128,768]{1,0:T(8,128)(2,1)S(1)} collective-permute-done((bf16[128,768]{1,0:T(8,128)(2,1)S(1)}, bf16[128,768]{1,0:T(8,128)(2,1)S(1)}, u32[]{:S(2)}, u32[]{:S(2)}) %collective-permute-start.3) | collective-permute-done | bytes 196640 | tf_op jit(solution)/shard_map/ppermute | solution.py:503
  17.6 2.1 %local_outputs.1 = (f32[256,512]{1,0:T(8,128)S(1)}, bf16[256,512]{1,0:T(8,128)(2,1)S(1)}, bf16[4,512,512]{2,1,0:T(8,128)(2,1)S(1)}) custom-call(f32[4,128,128]{2,1,0:T(8,128)S(1)} %get-tuple-element.47.own_state_ref, bf16[4,128,128]{2,1,0:T(8,128)(2,1)S(1)} %get-tuple-element.50.own_map_ref, f32[128,512]{1,0:T(8,128)S(1)} %get-tuple-element.51.own_out_ref, ...), custom_call_target="tpu_custom_call" | custom-call | flops 1000000000 | bytes 4000000 | tf_op jit(solution)/shard_map/local_outputs/pallas_call | solution.py:417
  19.7 0.6 %mix.1 = (bf16[256,512]{1,0:T(8,128)(2,1)S(1)}, bf16[128,512]{1,0:T(8,128)(2,1)S(1)}, bf16[128,512]{1,0:T(8,128)(2,1)S(1)}) custom-call(f32[256,512]{1,0:T(8,128)S(1)} %get-tuple-element.62.out_ref, bf16[256,512]{1,0:T(8,128)(2,1)S(1)} %get-tuple-element.63.through_ref, bf16[4,128,128]{2,1,0:T(8,128)(2,1)S(1)} %collective-permute-done.4.even_ref, ...), custom_call_target="tpu_custom_call" | custom-call | tf_op jit(solution)/shard_map/mix/pallas_call | solution.py:417
  20.4 0.1 collective-permute-start.6
  20.4 0.6 %project.1 = (bf16[3,128,512]{2,1,0:T(8,128)(2,1)S(1)}, bf16[3,128,512]{2,1,0:T(8,128)(2,1)S(1)}) custom-call(bf16[256,512]{1,0:T(8,128)(2,1)S(1)} %get-tuple-element.67.mixed_ref, bf16[4,512,512]{2,1,0:T(8,128)(2,1)S(1)} %get-tuple-element.66.weight_ref), custom_call_target="tpu_custom_call" | custom-call | flops 2000000000 | bytes 4000000 | tf_op jit(solution)/shard_map/project/pallas_call | solution.py:417
  21.0 0.7 %collective-permute-done.6.got_ref = bf16[128,512]{1,0:T(8,128)(2,1)S(1)} collective-permute-done((bf16[128,512]{1,0:T(8,128)(2,1)S(1)}, bf16[128,512]{1,0:T(8,128)(2,1)S(1)}, u32[]{:S(2)}, u32[]{:S(2)}) %collective-permute-start.6) | collective-permute-done | bytes 131104 | tf_op jit(solution)/shard_map/ppermute | solution.py:549
  21.8 0.1 collective-permute-start.7
  22.0 3.1 %collective-permute-start.10 = (bf16[128,512]{1,0:T(8,128)(2,1)S(1)}, bf16[128,512]{1,0:T(8,128)(2,1)S(1)}, u32[]{:S(2)}, u32[]{:S(2)}) collective-permute-start(bf16[128,512]{1,0:T(8,128)(2,1)S(1)} %core_sum_xy.1), channel_id=1, source_target_pairs={{0,6},{1,7},{2,4},{3,5},{4,2},{5,3},{6,0},{7,1},{8,14},{9,15},{10,... | collective-permute-start | bytes 393224 | tf_op jit(solution)/shard_map/ppermute | solution.py:570
  25.0 0.1 core_sums.1
  25.1 0.4 %collective-permute-start.8 = (bf16[128,512]{1,0:T(8,128)(2,1)S(1)}, bf16[128,512]{1,0:T(8,128)(2,1)S(1)}, u32[]{:S(2)}, u32[]{:S(2)}) collective-permute-start(bf16[128,512]{1,0:T(8,128)(2,1)S(1)} %get-tuple-element.73), channel_id=1, source_target_pairs={{0,2},{1,3},{2,0},{3,1},{4,6},{5,7},{6,4},{7,5},{8,10},{9,11},{10,... | collective-permute-start | bytes 393224 | tf_op jit(solution)/shard_map/ppermute | solution.py:571
  25.5 1.7 %collective-permute-start.9 = (bf16[128,512]{1,0:T(8,128)(2,1)S(1)}, bf16[128,512]{1,0:T(8,128)(2,1)S(1)}, u32[]{:S(2)}, u32[]{:S(2)}) collective-permute-start(bf16[128,512]{1,0:T(8,128)(2,1)S(1)} %get-tuple-element.74), channel_id=1, source_target_pairs={{0,4},{4,0},{8,12},{12,8},{16,20},{20,16},{24,28},{28,24},{1,5},{5... | collective-permute-start | bytes 393224 | tf_op jit(solution)/shard_map/ppermute | solution.py:572
  27.2 2.2 %collective-permute-done.10.xy_ref = bf16[128,512]{1,0:T(8,128)(2,1)S(1)} collective-permute-done((bf16[128,512]{1,0:T(8,128)(2,1)S(1)}, bf16[128,512]{1,0:T(8,128)(2,1)S(1)}, u32[]{:S(2)}, u32[]{:S(2)}) %collective-permute-start.10) | collective-permute-done | bytes 131104 | tf_op jit(solution)/shard_map/ppermute | solution.py:570
  29.4 2.5 %collective-permute-done.8.x_ref = bf16[128,512]{1,0:T(8,128)(2,1)S(1)} collective-permute-done((bf16[128,512]{1,0:T(8,128)(2,1)S(1)}, bf16[128,512]{1,0:T(8,128)(2,1)S(1)}, u32[]{:S(2)}, u32[]{:S(2)}) %collective-permute-start.8) | collective-permute-done | bytes 131104 | tf_op jit(solution)/shard_map/ppermute | solution.py:571
  31.9 0.8 %last_sum.1 = bf16[512,128]{1,0:T(8,128)(2,1)} custom-call(f32[128,512]{1,0:T(8,128)S(1)} %get-tuple-element.72.mine_ref, bf16[128,512]{1,0:T(8,128)(2,1)S(1)} %collective-permute-done.8.x_ref, bf16[128,512]{1,0:T(8,128)(2,1)S(1)} %collective-permute-done.9.y_ref, bf16[128,512]{1,0:T(8,128)(2,1)S(1)} %collective-permute-done.10.xy_ref), custom_call_target="tpu_custom_call" | custom-call | tf_op jit(solution)/shard_map/last_sum/pallas_call | solution.py:417
  (10 shorter events, 0.1 us)
Async XLA Ops:
  1.1 8.0 %collective-permute-start = (bf16[16,1024]{1,0:T(8,128)(2,1)S(1)}, bf16[16,1024]{1,0:T(8,128)(2,1)S(1)}, u32[]{:S(2)}, u32[]{:S(2)}) collective-permute-start(bf16[16,1024]{1,0:T(8,128)(2,1)S(1)} %get-tuple-element.46), channel_id=1, source_target_pairs={{0,4},{4,8},{8,12},{12,16},{16,20},{20,24},{24,28},{28,0},{1,5},{5... | collective-permute-start | bytes 98312 | tf_op jit(solution)/shard_map/ppermute | solution.py:489
  4.1 7.7 %collective-permute-start.1 = (bf16[144,768]{1,0:T(8,128)(2,1)S(1)}, bf16[144,768]{1,0:T(8,128)(2,1)S(1)}, u32[]{:S(2)}, u32[]{:S(2)}) collective-permute-start(bf16[144,768]{1,0:T(8,128)(2,1)S(1)} %get-tuple-element.53), channel_id=1, source_target_pairs={{0,4},{4,0},{8,12},{12,8},{16,20},{20,16},{24,28},{28,24},{1,5},{5... | collective-permute-start | bytes 663560 | tf_op jit(solution)/shard_map/ppermute | solution.py:490
  7.0 4.8 %collective-permute-start.2 = (bf16[16,1024]{1,0:T(8,128)(2,1)S(1)}, bf16[16,1024]{1,0:T(8,128)(2,1)S(1)}, u32[]{:S(2)}, u32[]{:S(2)}) collective-permute-start(bf16[16,1024]{1,0:T(8,128)(2,1)S(1)} %get-tuple-element.54.own_edge_ref), channel_id=1, source_target_pairs={{4,12},{12,20},{20,28},{28,24},{24,16},{16,8},{8,0},{0,4},{5,13},{... | collective-permute-start | bytes 98312 | tf_op jit(solution)/shard_map/ppermute | solution.py:491
  11.7 5.9 %collective-permute-start.3 = (bf16[128,768]{1,0:T(8,128)(2,1)S(1)}, bf16[128,768]{1,0:T(8,128)(2,1)S(1)}, u32[]{:S(2)}, u32[]{:S(2)}) collective-permute-start(bf16[128,768]{1,0:T(8,128)(2,1)S(1)} %get-tuple-element.61), channel_id=1, source_target_pairs={{0,4},{4,0},{8,12},{12,8},{16,20},{20,16},{24,28},{28,24},{1,5},{5... | collective-permute-start | bytes 589832 | tf_op jit(solution)/shard_map/ppermute | solution.py:503
  14.5 5.2 %copy-start = (f32[128]{0:T(128)S(1)}, f32[128]{0:T(128)}, u32[]{:S(2)}) copy-start(f32[128]{0:T(128)} %param.21) | copy-start | bytes 1540
  14.5 5.2 %collective-permute-start.4 = (bf16[4,128,128]{2,1,0:T(8,128)(2,1)S(1)}, bf16[4,128,128]{2,1,0:T(8,128)(2,1)S(1)}, u32[]{:S(2)}, u32[]{:S(2)}) collective-permute-start(bf16[4,128,128]{2,1,0:T(8,128)(2,1)S(1)} %get-tuple-element.64), channel_id=1, source_target_pairs={{0,8},{4,12},{8,0},{12,4},{16,24},{20,28},{24,16},{28,20},{1,9},{5... | collective-permute-start | bytes 393224 | tf_op jit(solution)/shard_map/ppermute | solution.py:523
  16.2 3.5 %collective-permute-start.5 = (bf16[4,128,128]{2,1,0:T(8,128)(2,1)S(1)}, bf16[4,128,128]{2,1,0:T(8,128)(2,1)S(1)}, u32[]{:S(2)}, u32[]{:S(2)}) collective-permute-start(bf16[4,128,128]{2,1,0:T(8,128)(2,1)S(1)} %get-tuple-element.64), channel_id=1, source_target_pairs={{0,1},{1,0},{2,3},{3,2},{4,5},{5,4},{6,7},{7,6},{8,16},{9,17},{10,... | collective-permute-start | bytes 393224 | tf_op jit(solution)/shard_map/ppermute | solution.py:523
  20.4 1.4 %collective-permute-start.6 = (bf16[128,512]{1,0:T(8,128)(2,1)S(1)}, bf16[128,512]{1,0:T(8,128)(2,1)S(1)}, u32[]{:S(2)}, u32[]{:S(2)}) collective-permute-start(bf16[128,512]{1,0:T(8,128)(2,1)S(1)} %get-tuple-element.70), channel_id=1, source_target_pairs={{0,1},{1,0},{2,3},{3,2},{4,5},{5,4},{6,7},{7,6},{8,9},{9,8},{10,11... | collective-permute-start | bytes 393224 | tf_op jit(solution)/shard_map/ppermute | solution.py:549
  21.8 3.3 %collective-permute-start.7 = (bf16[3,128,512]{2,1,0:T(8,128)(2,1)S(1)}, bf16[3,128,512]{2,1,0:T(8,128)(2,1)S(1)}, u32[]{:S(2)}, u32[]{:S(2)}) collective-permute-start(bf16[3,128,512]{2,1,0:T(8,128)(2,1)S(1)} %get-tuple-element.71), channel_id=1, source_target_pairs={{0,1},{1,0},{2,3},{3,2},{4,5},{5,4},{6,7},{7,6},{8,9},{9,8},{10,11... | collective-permute-start | bytes 1179656 | tf_op jit(solution)/shard_map/ppermute | solution.py:559
  22.0 7.4 %collective-permute-start.10 = (bf16[128,512]{1,0:T(8,128)(2,1)S(1)}, bf16[128,512]{1,0:T(8,128)(2,1)S(1)}, u32[]{:S(2)}, u32[]{:S(2)}) collective-permute-start(bf16[128,512]{1,0:T(8,128)(2,1)S(1)} %core_sum_xy.1), channel_id=1, source_target_pairs={{0,6},{1,7},{2,4},{3,5},{4,2},{5,3},{6,0},{7,1},{8,14},{9,15},{10,... | collective-permute-start | bytes 393224 | tf_op jit(solution)/shard_map/ppermute | solution.py:570
  25.1 6.7 %collective-permute-start.8 = (bf16[128,512]{1,0:T(8,128)(2,1)S(1)}, bf16[128,512]{1,0:T(8,128)(2,1)S(1)}, u32[]{:S(2)}, u32[]{:S(2)}) collective-permute-start(bf16[128,512]{1,0:T(8,128)(2,1)S(1)} %get-tuple-element.73), channel_id=1, source_target_pairs={{0,2},{1,3},{2,0},{3,1},{4,6},{5,7},{6,4},{7,5},{8,10},{9,11},{10,... | collective-permute-start | bytes 393224 | tf_op jit(solution)/shard_map/ppermute | solution.py:571
  25.5 6.4 %collective-permute-start.9 = (bf16[128,512]{1,0:T(8,128)(2,1)S(1)}, bf16[128,512]{1,0:T(8,128)(2,1)S(1)}, u32[]{:S(2)}, u32[]{:S(2)}) collective-permute-start(bf16[128,512]{1,0:T(8,128)(2,1)S(1)} %get-tuple-element.74), channel_id=1, source_target_pairs={{0,4},{4,0},{8,12},{12,8},{16,20},{20,16},{24,28},{28,24},{1,5},{5... | collective-permute-start | bytes 393224 | tf_op jit(solution)/shard_map/ppermute | solution.py:572

commit v6 on v5

--- a/solution.py
+++ b/solution.py
@@ -8,6 +8,7 @@
 DK = 128
 DV = 128
 EDGE = 16
+PARTS = 8
 F32 = jnp.float32
 BF16 = jnp.bfloat16
 VMEM_LIMIT = 48 * 1024 * 1024
@@ -15,6 +16,11 @@
 
 def dot(a, b):
     return jnp.dot(a.astype(BF16), b.astype(BF16), preferred_element_type=F32)
+
+
+def dot_nt(a, b):
+    dims = (((1,), (1,)), ((), ()))
+    return lax.dot_general(a.astype(BF16), b.astype(BF16), dims, preferred_element_type=F32)
 
 
 def exact_dot(a, b):
@@ -138,8 +144,8 @@
     return summed / (1.0 + jnp.exp(-summed))
 
 
-def unit(vectors):
-    return vectors * lax.rsqrt(jnp.sum(vectors * vectors, axis=-1, keepdims=True) + 1e-6)
+def inverse_norms(vectors, axis):
+    return lax.rsqrt(jnp.sum(vectors * vectors, axis=axis, keepdims=True) + 1e-6)
 
 
 def odd_blocks(value, reach):
@@ -195,11 +201,15 @@
     stacked = jnp.concatenate([sums, beta, jnp.zeros((rows - 2 * heads, rows), F32)], axis=0)
     columns = stacked.T
 
-    keys = [unit(conv_silu(halo(1, g), k(g), weights(1, g), keeps)) for g in range(key_heads)]
+    raw = [conv_silu(halo(1, g), k(g), weights(1, g), keeps) for g in range(key_heads)]
+    grams = [dot_nt(key, key) for key in raw]
+    raw_t = [key.T for key in raw]
+    norms = [inverse_norms(key, 1) for key in raw]
+    norms_t = [inverse_norms(key, 0) for key in raw_t]
+    keys = [key * norm for key, norm in zip(raw, norms)]
+    keys_t = [key * norm for key, norm in zip(raw_t, norms_t)]
     values = [conv_silu(halo(2, g), v(g), weights(2, g), keeps) for g in range(heads)]
-    keys_t = [key.T for key in keys]
     keys_t16 = [key.astype(BF16) for key in keys_t]
-    grams = [dot(key, key_t) for key, key_t in zip(keys, keys_t16)]
 
     lower, decays, rhs, starts, ends, throughs = [], [], [], [], [], []
     for h in range(heads):
@@ -210,7 +220,8 @@
         end = jnp.broadcast_to(columns[rows - 1 : rows, h : h + 1], (1, rows))
         decay = jnp.exp(jnp.where(same, down - along, -1e30))
         decays.append(decay)
-        lower.append(jnp.where(row > col, beta_down * grams[g] * decay, 0.0))
+        factor = jnp.where(row > col, beta_down * norms[g] * decay * norms_t[g], 0.0)
+        lower.append(factor * grams[g])
         start = jnp.where(seg == before, jnp.exp(down), 0.0)
         starts.append(start)
         rhs.append(
@@ -232,9 +243,11 @@
 
 def query_terms(seg_down, halo, q, weights, solved, decays, starts, keys_t):
     keeps = keep_masks(seg_down)
-    queries = [unit(conv_silu(halo(0, g), q(g), weights(0, g), keeps)) for g in range(len(keys_t))]
+    queries = [conv_silu(halo(0, g), q(g), weights(0, g), keeps) for g in range(len(keys_t))]
     scores = [dot(query, key_t) for query, key_t in zip(queries, keys_t)]
-    results = [dot(scores[h // 2] * decays[h], solved[h]) for h in range(len(solved))]
+    norms = [inverse_norms(query, 1) for query in queries]
+    queries = [query * norm for query, norm in zip(queries, norms)]
+    results = [dot(scores[h // 2] * (norms[h // 2] * decays[h]), solved[h]) for h in range(len(solved))]
     outs = [result[:, :DV] for result in results]
     throughs = [(queries[h // 2] * starts[h] - results[h][:, DV:]).astype(BF16) for h in range(len(solved))]
     return outs, throughs
@@ -330,16 +343,12 @@
                  start_ref, key_ref, down_ref, along_ref, late_ref, own_edge_ref, edge_ref, conv_ref, weight_hbm,
                  out_ref, through_ref, weight_ref, sems):
     y = lax.axis_index("ctx") % 2
-    head = lax.axis_index("head")
-    core, x = head % 2, head // 2
-    depth, width = weight_ref.shape[1:]
-    copies = []
-    for i, (c, xx) in enumerate(((1 - core, x), (1 - core, 1 - x), (core, x), (core, 1 - x))):
-        source = weight_hbm.at[
-            pl.ds(pl.multiple_of(y * depth, depth), depth), pl.ds(pl.multiple_of((xx * 2 + c) * width, width), width)
-        ]
-        copies.append(pltpu.make_async_copy(source, weight_ref.at[i], sems.at[i]))
-        copies[-1].start()
+    depth = weight_ref.shape[0]
+    copies = Copies(sems)
+    part = depth // PARTS
+    for i in range(PARTS):
+        from_row = pl.multiple_of(y * depth + i * part, part)
+        copies.start(weight_hbm.at[pl.ds(from_row, part), :], weight_ref.at[pl.ds(i * part, part), :])
     rows = own_out_ref.shape[0]
     heads = own_state_ref.shape[0]
     columns = groups(heads)
@@ -366,8 +375,15 @@
         out_ref[rows:, lanes] = out + where_y(y, jnp.zeros_like(extra), extra)
         through_ref[0:rows, lanes] = where_y(y, moved, own_through)
         through_ref[rows:, lanes] = where_y(y, through, moved)
-    for copy in copies:
-        copy.wait()
+    copies.wait()
+
+
+def feature_columns(weight_ref, other_core, other_x):
+    head = lax.axis_index("head")
+    core, x = head % 2, head // 2
+    block = (x + other_x - 2 * x * other_x) * 2 + core + other_core - 2 * core * other_core
+    width = weight_ref.shape[1] // lax.axis_size("head")
+    return weight_ref[:, pl.ds(pl.multiple_of(block * width, width), width)]
 
 
 def mix_kernel(out_ref, through_ref, even_ref, odd_ref, gate_ref, late_ref, gain_ref, weight_ref, mixed_ref, send_ref, keep_ref):
@@ -382,8 +398,8 @@
         gate = gate.astype(F32)
         scale = lax.rsqrt(jnp.mean(o * o, axis=-1, keepdims=True) + 1e-6)
         mixed_ref[:, lanes] = (o * scale * gain_ref[...] * (gate / (1.0 + jnp.exp(-gate)))).astype(BF16)
-    send_ref[...] = jnp.dot(mixed_ref[rows:, :], weight_ref[1], preferred_element_type=F32).astype(BF16)
-    keep_ref[...] = jnp.dot(mixed_ref[rows:, :], weight_ref[3], preferred_element_type=F32).astype(BF16)
+    send_ref[...] = jnp.dot(mixed_ref[rows:, :], feature_columns(weight_ref, 1, 1), preferred_element_type=F32).astype(BF16)
+    keep_ref[...] = jnp.dot(mixed_ref[rows:, :], feature_columns(weight_ref, 0, 1), preferred_element_type=F32).astype(BF16)
 
 
 QUARTERS = ((0, 0), (0, 1), (1, 0))
@@ -393,7 +409,8 @@
     rows = send_ref.shape[1]
     for c, to_ref in ((0, send_ref), (1, keep_ref)):
         for i, (peer, far) in enumerate(QUARTERS):
-            product = jnp.dot(mixed_ref[peer * rows : peer * rows + rows, :], weight_ref[2 * c + far], preferred_element_type=F32)
+            weights = feature_columns(weight_ref, 1 - c, far)
+            product = jnp.dot(mixed_ref[peer * rows : peer * rows + rows, :], weights, preferred_element_type=F32)
             to_ref[i] = product.astype(BF16)
 
 
@@ -457,8 +474,12 @@
         for c in range(ctx_count)
         for h in range(head_count)
     ]
-    ring = [1 + 2 * p for p in range(ctx_count // 2)] + [2 * p for p in reversed(range(ctx_count // 2))]
-    along_ring = [(ring[i], ring[(i + 1) % ctx_count]) for i in range(ctx_count)]
+    far_ahead = [
+        (c * head_count + h, (c + 2) % ctx_count * head_count + h if c % 2 else c * head_count + (h ^ 1))
+        for c in range(ctx_count)
+        for h in range(head_count)
+    ]
+
 
     edge, pack, gates = call(
         pack_kernel,
@@ -488,7 +509,7 @@
     )
     got_edge = lax.ppermute(edge, "ctx", ahead_1)
     got_pack = lax.ppermute(pack, "ctx", swap)
-    got_far_edge = lax.ppermute(own_edge, "ctx", along_ring)
+    got_far_edge = lax.ppermute(own_edge, ("ctx", "head"), far_ahead)
 
     square = (heads, DK, DV)
     own_state, own_map, own_out, own_through = call(
@@ -530,12 +551,12 @@
         entering = from_earlier((end.astype(F32) + moved).astype(BF16))
     out, through, weight = call(
         local_kernel,
-        [((2 * rows, value_width), F32), ((2 * rows, value_width), BF16), ((4, value_width, width), BF16)],
+        [((2 * rows, value_width), F32), ((2 * rows, value_width), BF16), ((value_width, out_weight.shape[1]), BF16)],
         (own_state, own_map, own_out, own_through, state, map_, solved, decay, start, key, down, along, got_late, own_edge,
          got_far_edge, weights, out_weight),
         "local_outputs",
         hbm=(16,),
-        scratch=(pltpu.SemaphoreType.DMA((4,)),),
+        scratch=(pltpu.SemaphoreType.DMA((PARTS,)),),
         flops=1_000_000_000,
         moved=4_000_000,
     )

time: 33.1 us -> 32.8 us (level)
  waiting for transfers between devices: 8.43 us -> 8.98 us
  starting transfers between devices: 12.2 us -> 11.7 us
    ppermute x1, starting transfers between devices: 0.56 us -> 0.05 us  [body(): got_far_edge = lax.ppermute(own_edge, ('ctx', 'head'), far_ahead)]
    ppermute x1, waiting for transfers between devices: 1.56 us -> 2.06 us  [body(): got_edge = lax.ppermute(edge, 'ctx', ahead_1)]
  transfers between devices with their start and end apart: 11 -> 11, of which waited for: 5 -> 5; matrix products, arithmetic and copies ran while one was open for 0% -> 0% of each run, Pallas kernels for 29% -> 28%
where the time goes in v6:
time: 32.8 us; the launch traced here: 32.7 us
  Pallas kernels  11.8 us (36%)
  starting transfers between devices  11.7 us (36%)
  waiting for transfers between devices  8.98 us (27%)
    pallas_call x10, Pallas kernels, call(): pl.pallas_call(kernel, out_shape=[jax.ShapeDtypeStruct(shape, kind) for s...  11.8 us
    ppermute x1, starting transfers between devices, body(): got_xy = lax.ppermute(to_xy, ('ctx', 'head'), both)  3.14 us
    ppermute x1, starting transfers between devices, body(): got_edge = lax.ppermute(edge, 'ctx', ahead_1)  3.02 us
    ppermute x1, waiting for transfers between devices, body(): got_x = lax.ppermute(to_x, 'head', [(i, i ^ 2) for i in range(head_count)])  2.53 us
    ppermute x1, waiting for transfers between devices, body(): got_xy = lax.ppermute(to_xy, ('ctx', 'head'), both)  2.15 us
    ppermute x1, waiting for transfers between devices, body(): got_edge = lax.ppermute(edge, 'ctx', ahead_1)  2.06 us
    ppermute x1, starting transfers between devices, body(): got_y = lax.ppermute(to_y, 'ctx', swap)  1.69 us
    ppermute x1, starting transfers between devices, from_earlier(): lax.ppermute(value, 'ctx', even_swap)  1.61 us
  transfers between devices with their start and end apart: 11, of which 5 were waited for; matrix products, arithmetic and copies ran while one was open for 0% of the time, Pallas kernels for 28%

profile of v6, /device:TPU:0, one launch (start us, length us, event | category | flops | bytes accessed | tf_op | source)
XLA Modules:
  0.0 32.7 jit_solution(1313173785380857595)
XLA Ops:
  0.0 1.1 %pack.1 = (bf16[16,1024]{1,0:T(8,128)(2,1)S(1)}, bf16[144,768]{1,0:T(8,128)(2,1)S(1)}, f32[8,128]{1,0:T(8,128)S(1)}) custom-call(bf16[128,512]{1,0:T(8,128)(2,1)} %q_ref.3, bf16[128,512]{1,0:T(8,128)(2,1)} %k_ref.3, bf16[128,1024]{1,0:T(8,128)(2,1)} %v_ref.3, f32[8,128]{1,0:T(8,128)} %decay_ref.1, f32[8,128]{1,0:T(8,128)} %beta_ref.1), custom_call_target="tpu_custom_call" | custom-call | tf_op jit(solution)/shard_map/pack/pallas_call | solution.py:434
  1.1 3.0 %collective-permute-start = (bf16[16,1024]{1,0:T(8,128)(2,1)S(1)}, bf16[16,1024]{1,0:T(8,128)(2,1)S(1)}, u32[]{:S(2)}, u32[]{:S(2)}) collective-permute-start(bf16[16,1024]{1,0:T(8,128)(2,1)S(1)} %get-tuple-element.46), channel_id=1, source_target_pairs={{0,4},{4,8},{8,12},{12,16},{16,20},{20,24},{24,28},{28,0},{1,5},{5... | collective-permute-start | bytes 98312 | tf_op jit(solution)/shard_map/ppermute | solution.py:510
  4.1 1.5 %collective-permute-start.1 = (bf16[144,768]{1,0:T(8,128)(2,1)S(1)}, bf16[144,768]{1,0:T(8,128)(2,1)S(1)}, u32[]{:S(2)}, u32[]{:S(2)}) collective-permute-start(bf16[144,768]{1,0:T(8,128)(2,1)S(1)} %get-tuple-element.53), channel_id=1, source_target_pairs={{0,4},{4,0},{8,12},{12,8},{16,20},{20,16},{24,28},{28,24},{1,5},{5... | collective-permute-start | bytes 663560 | tf_op jit(solution)/shard_map/ppermute | solution.py:511
  5.6 1.3 %early.1 = (bf16[16,1024]{1,0:T(8,128)(2,1)S(1)}, bf16[128,768]{1,0:T(8,128)(2,1)S(1)}, bf16[128,1024]{1,0:T(8,128)(2,1)S(1)}, f32[4,1024]{1,0:T(4,128)S(1)}, bf...) custom-call(bf16[128,512]{1,0:T(8,128)(2,1)} %q_ref.3, bf16[128,512]{1,0:T(8,128)(2,1)} %k_ref.3, ...), custom_call_target="tpu_custom_call" | custom-call | flops 10000000000 | bytes 2000000 | tf_op jit(solution)/shard_map/early/pallas_call | solution.py:434
  7.0 0.1 collective-permute-start.2
  7.0 2.1 %collective-permute-done.halo_ref = bf16[16,1024]{1,0:T(8,128)(2,1)S(1)} collective-permute-done((bf16[16,1024]{1,0:T(8,128)(2,1)S(1)}, bf16[16,1024]{1,0:T(8,128)(2,1)S(1)}, u32[]{:S(2)}, u32[]{:S(2)}) %collective-permute-start) | collective-permute-done | bytes 32800 | tf_op jit(solution)/shard_map/ppermute | solution.py:510
  9.1 2.6 %own_terms.1 = (f32[4,128,128]{2,1,0:T(8,128)S(1)}, bf16[4,128,128]{2,1,0:T(8,128)(2,1)S(1)}, f32[128,512]{1,0:T(8,128)S(1)}, bf16[128,512]{1,0:T(8,128)(2,1)S(1)}) custom-call(s32[264,128]{1,0:T(8,128)S(1)} %get-tuple-element.41.down_ref, s32[8,256]{1,0:T(8,128)S(1)} %get-tuple-element.42.along_ref, bf16[128,1024]{1,0:T(8,128)(2,1)S(1)} %get-tuple-element.43.own_ref, ...), custom_call_target="tpu_custom_call" | custom-call | flops 1000000 | bytes 4000000 | tf_op jit(solution)/shard_map/own_terms/pallas_call | solution.py:434
  11.7 0.1 collective-permute-start.3
  11.8 2.6 %peer_terms.1 = (f32[4,128,128]{2,1,0:T(8,128)S(1)}, bf16[4,128,128]{2,1,0:T(8,128)(2,1)S(1)}, bf16[4,128,256]{2,1,0:T(8,128)(2,1)S(1)}, f32[4,128,128]{2,1,0:T(...) custom-call(s32[264,128]{1,0:T(8,128)S(1)} %get-tuple-element.41.down_ref, ...), custom_call_target="tpu_custom_call" | custom-call | flops 2000000000 | bytes 4000000 | tf_op jit(solution)/shard_map/peer_terms/pallas_call | solution.py:434
  14.5 1.6 %collective-permute-start.4 = (bf16[4,128,128]{2,1,0:T(8,128)(2,1)S(1)}, bf16[4,128,128]{2,1,0:T(8,128)(2,1)S(1)}, u32[]{:S(2)}, u32[]{:S(2)}) collective-permute-start(bf16[4,128,128]{2,1,0:T(8,128)(2,1)S(1)} %get-tuple-element.64), channel_id=1, source_target_pairs={{0,8},{4,12},{8,0},{12,4},{16,24},{20,28},{24,16},{28,20},{1,9},{5... | collective-permute-start | bytes 393224 | tf_op jit(solution)/shard_map/ppermute | solution.py:544
  16.1 1.5 %collective-permute-done.3.late_ref = bf16[128,768]{1,0:T(8,128)(2,1)S(1)} collective-permute-done((bf16[128,768]{1,0:T(8,128)(2,1)S(1)}, bf16[128,768]{1,0:T(8,128)(2,1)S(1)}, u32[]{:S(2)}, u32[]{:S(2)}) %collective-permute-start.3) | collective-permute-done | bytes 196640 | tf_op jit(solution)/shard_map/ppermute | solution.py:524
  17.6 1.9 %local_outputs.1 = (f32[256,512]{1,0:T(8,128)S(1)}, bf16[256,512]{1,0:T(8,128)(2,1)S(1)}, bf16[512,2048]{1,0:T(8,128)(2,1)S(1)}) custom-call(f32[4,128,128]{2,1,0:T(8,128)S(1)} %get-tuple-element.47.own_state_ref, bf16[4,128,128]{2,1,0:T(8,128)(2,1)S(1)} %get-tuple-element.50.own_map_ref, f32[128,512]{1,0:T(8,128)S(1)} %get-tuple-element.51.own_out_ref, ...), custom_call_target="tpu_custom_call" | custom-call | flops 1000000000 | bytes 4000000 | tf_op jit(solution)/shard_map/local_outputs/pallas_call | solution.py:434
  19.6 0.7 %mix.1 = (bf16[256,512]{1,0:T(8,128)(2,1)S(1)}, bf16[128,512]{1,0:T(8,128)(2,1)S(1)}, bf16[128,512]{1,0:T(8,128)(2,1)S(1)}) custom-call(f32[256,512]{1,0:T(8,128)S(1)} %get-tuple-element.62.out_ref, bf16[256,512]{1,0:T(8,128)(2,1)S(1)} %get-tuple-element.63.through_ref, bf16[4,128,128]{2,1,0:T(8,128)(2,1)S(1)} %collective-permute-done.4.even_ref, ...), custom_call_target="tpu_custom_call" | custom-call | tf_op jit(solution)/shard_map/mix/pallas_call | solution.py:434
  20.3 0.1 collective-permute-start.6
  20.4 0.6 %project.1 = (bf16[3,128,512]{2,1,0:T(8,128)(2,1)S(1)}, bf16[3,128,512]{2,1,0:T(8,128)(2,1)S(1)}) custom-call(bf16[256,512]{1,0:T(8,128)(2,1)S(1)} %get-tuple-element.67.mixed_ref, bf16[512,2048]{1,0:T(8,128)(2,1)S(1)} %get-tuple-element.66.weight_ref), custom_call_target="tpu_custom_call" | custom-call | flops 2000000000 | bytes 4000000 | tf_op jit(solution)/shard_map/project/pallas_call | solution.py:434
  21.0 0.7 %collective-permute-done.6.got_ref = bf16[128,512]{1,0:T(8,128)(2,1)S(1)} collective-permute-done((bf16[128,512]{1,0:T(8,128)(2,1)S(1)}, bf16[128,512]{1,0:T(8,128)(2,1)S(1)}, u32[]{:S(2)}, u32[]{:S(2)}) %collective-permute-start.6) | collective-permute-done | bytes 131104 | tf_op jit(solution)/shard_map/ppermute | solution.py:570
  21.7 0.1 collective-permute-start.7
  21.9 3.1 %collective-permute-start.10 = (bf16[128,512]{1,0:T(8,128)(2,1)S(1)}, bf16[128,512]{1,0:T(8,128)(2,1)S(1)}, u32[]{:S(2)}, u32[]{:S(2)}) collective-permute-start(bf16[128,512]{1,0:T(8,128)(2,1)S(1)} %core_sum_xy.1), channel_id=1, source_target_pairs={{0,6},{1,7},{2,4},{3,5},{4,2},{5,3},{6,0},{7,1},{8,14},{9,15},{10,... | collective-permute-start | bytes 393224 | tf_op jit(solution)/shard_map/ppermute | solution.py:591
  25.0 0.1 core_sums.1
  25.1 0.4 %collective-permute-start.8 = (bf16[128,512]{1,0:T(8,128)(2,1)S(1)}, bf16[128,512]{1,0:T(8,128)(2,1)S(1)}, u32[]{:S(2)}, u32[]{:S(2)}) collective-permute-start(bf16[128,512]{1,0:T(8,128)(2,1)S(1)} %get-tuple-element.73), channel_id=1, source_target_pairs={{0,2},{1,3},{2,0},{3,1},{4,6},{5,7},{6,4},{7,5},{8,10},{9,11},{10,... | collective-permute-start | bytes 393224 | tf_op jit(solution)/shard_map/ppermute | solution.py:592
  25.5 1.7 %collective-permute-start.9 = (bf16[128,512]{1,0:T(8,128)(2,1)S(1)}, bf16[128,512]{1,0:T(8,128)(2,1)S(1)}, u32[]{:S(2)}, u32[]{:S(2)}) collective-permute-start(bf16[128,512]{1,0:T(8,128)(2,1)S(1)} %get-tuple-element.74), channel_id=1, source_target_pairs={{0,4},{4,0},{8,12},{12,8},{16,20},{20,16},{24,28},{28,24},{1,5},{5... | collective-permute-start | bytes 393224 | tf_op jit(solution)/shard_map/ppermute | solution.py:593
  27.2 2.2 %collective-permute-done.10.xy_ref = bf16[128,512]{1,0:T(8,128)(2,1)S(1)} collective-permute-done((bf16[128,512]{1,0:T(8,128)(2,1)S(1)}, bf16[128,512]{1,0:T(8,128)(2,1)S(1)}, u32[]{:S(2)}, u32[]{:S(2)}) %collective-permute-start.10) | collective-permute-done | bytes 131104 | tf_op jit(solution)/shard_map/ppermute | solution.py:591
  29.4 2.5 %collective-permute-done.8.x_ref = bf16[128,512]{1,0:T(8,128)(2,1)S(1)} collective-permute-done((bf16[128,512]{1,0:T(8,128)(2,1)S(1)}, bf16[128,512]{1,0:T(8,128)(2,1)S(1)}, u32[]{:S(2)}, u32[]{:S(2)}) %collective-permute-start.8) | collective-permute-done | bytes 131104 | tf_op jit(solution)/shard_map/ppermute | solution.py:592
  31.9 0.8 %last_sum.1 = bf16[512,128]{1,0:T(8,128)(2,1)} custom-call(f32[128,512]{1,0:T(8,128)S(1)} %get-tuple-element.72.mine_ref, bf16[128,512]{1,0:T(8,128)(2,1)S(1)} %collective-permute-done.8.x_ref, bf16[128,512]{1,0:T(8,128)(2,1)S(1)} %collective-permute-done.9.y_ref, bf16[128,512]{1,0:T(8,128)(2,1)S(1)} %collective-permute-done.10.xy_ref), custom_call_target="tpu_custom_call" | custom-call | tf_op jit(solution)/shard_map/last_sum/pallas_call | solution.py:434
  (10 shorter events, 0.1 us)
Async XLA Ops:
  1.1 8.0 %collective-permute-start = (bf16[16,1024]{1,0:T(8,128)(2,1)S(1)}, bf16[16,1024]{1,0:T(8,128)(2,1)S(1)}, u32[]{:S(2)}, u32[]{:S(2)}) collective-permute-start(bf16[16,1024]{1,0:T(8,128)(2,1)S(1)} %get-tuple-element.46), channel_id=1, source_target_pairs={{0,4},{4,8},{8,12},{12,16},{16,20},{20,24},{24,28},{28,0},{1,5},{5... | collective-permute-start | bytes 98312 | tf_op jit(solution)/shard_map/ppermute | solution.py:510
  4.1 7.7 %collective-permute-start.1 = (bf16[144,768]{1,0:T(8,128)(2,1)S(1)}, bf16[144,768]{1,0:T(8,128)(2,1)S(1)}, u32[]{:S(2)}, u32[]{:S(2)}) collective-permute-start(bf16[144,768]{1,0:T(8,128)(2,1)S(1)} %get-tuple-element.53), channel_id=1, source_target_pairs={{0,4},{4,0},{8,12},{12,8},{16,20},{20,16},{24,28},{28,24},{1,5},{5... | collective-permute-start | bytes 663560 | tf_op jit(solution)/shard_map/ppermute | solution.py:511
  7.0 4.9 %collective-permute-start.2 = (bf16[16,1024]{1,0:T(8,128)(2,1)S(1)}, bf16[16,1024]{1,0:T(8,128)(2,1)S(1)}, u32[]{:S(2)}, u32[]{:S(2)}) collective-permute-start(bf16[16,1024]{1,0:T(8,128)(2,1)S(1)} %get-tuple-element.54.own_edge_ref), channel_id=1, source_target_pairs={{0,1},{1,0},{2,3},{3,2},{4,12},{5,13},{6,14},{7,15},{8,9},{9,8},{1... | collective-permute-start | bytes 98312 | tf_op jit(solution)/shard_map/ppermute | solution.py:512
  11.7 5.9 %collective-permute-start.3 = (bf16[128,768]{1,0:T(8,128)(2,1)S(1)}, bf16[128,768]{1,0:T(8,128)(2,1)S(1)}, u32[]{:S(2)}, u32[]{:S(2)}) collective-permute-start(bf16[128,768]{1,0:T(8,128)(2,1)S(1)} %get-tuple-element.61), channel_id=1, source_target_pairs={{0,4},{4,0},{8,12},{12,8},{16,20},{20,16},{24,28},{28,24},{1,5},{5... | collective-permute-start | bytes 589832 | tf_op jit(solution)/shard_map/ppermute | solution.py:524
  14.5 5.1 %copy-start = (f32[128]{0:T(128)S(1)}, f32[128]{0:T(128)}, u32[]{:S(2)}) copy-start(f32[128]{0:T(128)} %param.21) | copy-start | bytes 1540
  14.5 5.1 %collective-permute-start.4 = (bf16[4,128,128]{2,1,0:T(8,128)(2,1)S(1)}, bf16[4,128,128]{2,1,0:T(8,128)(2,1)S(1)}, u32[]{:S(2)}, u32[]{:S(2)}) collective-permute-start(bf16[4,128,128]{2,1,0:T(8,128)(2,1)S(1)} %get-tuple-element.64), channel_id=1, source_target_pairs={{0,8},{4,12},{8,0},{12,4},{16,24},{20,28},{24,16},{28,20},{1,9},{5... | collective-permute-start | bytes 393224 | tf_op jit(solution)/shard_map/ppermute | solution.py:544
  16.1 3.5 %collective-permute-start.5 = (bf16[4,128,128]{2,1,0:T(8,128)(2,1)S(1)}, bf16[4,128,128]{2,1,0:T(8,128)(2,1)S(1)}, u32[]{:S(2)}, u32[]{:S(2)}) collective-permute-start(bf16[4,128,128]{2,1,0:T(8,128)(2,1)S(1)} %get-tuple-element.64), channel_id=1, source_target_pairs={{0,1},{1,0},{2,3},{3,2},{4,5},{5,4},{6,7},{7,6},{8,16},{9,17},{10,... | collective-permute-start | bytes 393224 | tf_op jit(solution)/shard_map/ppermute | solution.py:544
  20.3 1.4 %collective-permute-start.6 = (bf16[128,512]{1,0:T(8,128)(2,1)S(1)}, bf16[128,512]{1,0:T(8,128)(2,1)S(1)}, u32[]{:S(2)}, u32[]{:S(2)}) collective-permute-start(bf16[128,512]{1,0:T(8,128)(2,1)S(1)} %get-tuple-element.70), channel_id=1, source_target_pairs={{0,1},{1,0},{2,3},{3,2},{4,5},{5,4},{6,7},{7,6},{8,9},{9,8},{10,11... | collective-permute-start | bytes 393224 | tf_op jit(solution)/shard_map/ppermute | solution.py:570
  21.7 3.3 %collective-permute-start.7 = (bf16[3,128,512]{2,1,0:T(8,128)(2,1)S(1)}, bf16[3,128,512]{2,1,0:T(8,128)(2,1)S(1)}, u32[]{:S(2)}, u32[]{:S(2)}) collective-permute-start(bf16[3,128,512]{2,1,0:T(8,128)(2,1)S(1)} %get-tuple-element.71), channel_id=1, source_target_pairs={{0,1},{1,0},{2,3},{3,2},{4,5},{5,4},{6,7},{7,6},{8,9},{9,8},{10,11... | collective-permute-start | bytes 1179656 | tf_op jit(solution)/shard_map/ppermute | solution.py:580
  21.9 7.5 %collective-permute-start.10 = (bf16[128,512]{1,0:T(8,128)(2,1)S(1)}, bf16[128,512]{1,0:T(8,128)(2,1)S(1)}, u32[]{:S(2)}, u32[]{:S(2)}) collective-permute-start(bf16[128,512]{1,0:T(8,128)(2,1)S(1)} %core_sum_xy.1), channel_id=1, source_target_pairs={{0,6},{1,7},{2,4},{3,5},{4,2},{5,3},{6,0},{7,1},{8,14},{9,15},{10,... | collective-permute-start | bytes 393224 | tf_op jit(solution)/shard_map/ppermute | solution.py:591
  25.1 6.8 %collective-permute-start.8 = (bf16[128,512]{1,0:T(8,128)(2,1)S(1)}, bf16[128,512]{1,0:T(8,128)(2,1)S(1)}, u32[]{:S(2)}, u32[]{:S(2)}) collective-permute-start(bf16[128,512]{1,0:T(8,128)(2,1)S(1)} %get-tuple-element.73), channel_id=1, source_target_pairs={{0,2},{1,3},{2,0},{3,1},{4,6},{5,7},{6,4},{7,5},{8,10},{9,11},{10,... | collective-permute-start | bytes 393224 | tf_op jit(solution)/shard_map/ppermute | solution.py:592
  25.5 6.4 %collective-permute-start.9 = (bf16[128,512]{1,0:T(8,128)(2,1)S(1)}, bf16[128,512]{1,0:T(8,128)(2,1)S(1)}, u32[]{:S(2)}, u32[]{:S(2)}) collective-permute-start(bf16[128,512]{1,0:T(8,128)(2,1)S(1)} %get-tuple-element.74), channel_id=1, source_target_pairs={{0,4},{4,0},{8,12},{12,8},{16,20},{20,16},{24,28},{28,24},{1,5},{5... | collective-permute-start | bytes 393224 | tf_op jit(solution)/shard_map/ppermute | solution.py:593

commit v7 on v6

--- a/solution.py
+++ b/solution.py
@@ -173,22 +173,24 @@
     eye = (row == col).astype(F32)
     inverse = [eye + x for x in power]
     power = [x.astype(BF16) for x in power]
-    reach = 2
+    power = [dot(x, x).astype(BF16) for x in power]
+    reach = 4
     while reach < small:
-        power = [dot(x, x).astype(BF16) for x in power]
+        following = [dot(x, x).astype(BF16) for x in power]
         inverse = [x + dot(x, p) for x, p in zip(inverse, power)]
+        power = following
         reach *= 2
+    inverse = [x + dot(x, p) for x, p in zip(inverse, power)]
     here = (row // large == col // large) & (row // small != col // small)
     moved = [dot(odd_blocks(jnp.where(here, x, 0.0), small), i) for x, i in zip(lower, inverse)]
     moved = [dot(odd_blocks(i, small), at_odd_blocks(m, small)) for i, m in zip(inverse, moved)]
     inverse = [(i - at_odd_blocks(m, small)).astype(BF16) for i, m in zip(inverse, moved)]
     rest = [jnp.where(row // large == col // large, 0.0, -x) for x in lower]
     once = [dot(i, r).astype(BF16) for i, r in zip(inverse, rest)]
-    twice = [dot(m, m).astype(BF16) for m in once]
-    return inverse, once, twice
-
-
-def state_terms(seg_down, seg_along, halo, k, v, weights, sums, beta):
+    return inverse, once
+
+
+def block_terms(seg_down, seg_along, halo, k, v, weights, sums, beta):
     heads, rows = sums.shape
     key_heads = heads // 2
     seg = seg_down[8:]
@@ -211,7 +213,7 @@
     values = [conv_silu(halo(2, g), v(g), weights(2, g), keeps) for g in range(heads)]
     keys_t16 = [key.astype(BF16) for key in keys_t]
 
-    lower, decays, rhs, starts, ends, throughs = [], [], [], [], [], []
+    lower, decays, right, start_keys, starts, ends, throughs = [], [], [], [], [], [], []
     for h in range(heads):
         g = h // 2
         down = jnp.broadcast_to(columns[:, h : h + 1], (rows, rows))
@@ -224,33 +226,35 @@
         lower.append(factor * grams[g])
         start = jnp.where(seg == before, jnp.exp(down), 0.0)
         starts.append(start)
-        rhs.append(
-            jnp.concatenate([(beta_down * values[h]).astype(BF16), (beta_down * start * keys[g]).astype(BF16)], axis=1)
-        )
+        right.append(beta_down * values[h])
+        start_keys.append((beta_down * start * keys[g]).astype(BF16))
         ends.append((keys_t[g] * jnp.where(seg_along[0:1] == last, jnp.exp(end - along), 0.0)).astype(BF16))
         throughs.append(jnp.where(last == before, jnp.exp(end), 0.0))
 
-    inverse, once, twice = solve_terms(lower)
-    solved = [dot(i, r) for i, r in zip(inverse, rhs)]
-    solved = [s + dot(m, s) for m, s in zip(once, solved)]
-    solved = [(s + dot(m, s)).astype(BF16) for m, s in zip(twice, solved)]
-    eye = (row == col).astype(F32)
-    ended = [dot(e, s) for e, s in zip(ends, solved)]
-    states = [e[:, :DV] for e in ended]
-    maps = [t * eye - e[:, DV:] for t, e in zip(throughs, ended)]
-    return states, maps, solved, decays, starts, keys_t16
-
-
-def query_terms(seg_down, halo, q, weights, solved, decays, starts, keys_t):
+    return lower, right, start_keys, ends, throughs, decays, starts, keys_t16
+
+
+def solved_with(inverse, once, right):
+    result = [dot(i, r) for i, r in zip(inverse, right)]
+    twice = [dot(m, m).astype(BF16) for m in once]
+    result = [r + dot(m, r) for m, r in zip(once, result)]
+    return [(r + dot(m, r)).astype(BF16) for m, r in zip(twice, result)], twice
+
+
+def scaled_eye(scale):
+    row = lax.broadcasted_iota(jnp.int32, (DK, DK), 0)
+    col = lax.broadcasted_iota(jnp.int32, (DK, DK), 1)
+    return jnp.where(row == col, scale, 0.0)
+
+
+def query_terms(seg_down, halo, q, weights, decays, starts, keys_t):
     keeps = keep_masks(seg_down)
     queries = [conv_silu(halo(0, g), q(g), weights(0, g), keeps) for g in range(len(keys_t))]
     scores = [dot(query, key_t) for query, key_t in zip(queries, keys_t)]
     norms = [inverse_norms(query, 1) for query in queries]
     queries = [query * norm for query, norm in zip(queries, norms)]
-    results = [dot(scores[h // 2] * (norms[h // 2] * decays[h]), solved[h]) for h in range(len(solved))]
-    outs = [result[:, :DV] for result in results]
-    throughs = [(queries[h // 2] * starts[h] - results[h][:, DV:]).astype(BF16) for h in range(len(solved))]
-    return outs, throughs
+    inside = [(scores[h // 2] * (norms[h // 2] * decays[h])).astype(BF16) for h in range(len(decays))]
+    return inside, [queries[h // 2] * starts[h] for h in range(len(decays))]
 
 
 def groups(heads):
@@ -276,7 +280,7 @@
     def weights(which, g):
         return weight_ref[:, columns(which, g)]
 
-    states, maps, solved, decays, starts, keys_t = state_terms(
+    lower, right, start_keys, ends, throughs, decays, starts, keys_t = block_terms(
         seg_down,
         seg_along,
         halo,
@@ -286,14 +290,19 @@
         gates_ref[0:heads],
         gates_ref[heads:],
     )
-    outs, throughs = query_terms(
-        seg_down, halo, lambda g: own_ref[:, columns(0, g)], weights, solved, decays, starts, keys_t
-    )
+    inverse, once = solve_terms(lower)
+    inside, start_queries = query_terms(
+        seg_down, halo, lambda g: own_ref[:, columns(0, g)], weights, decays, starts, keys_t
+    )
+    both = [jnp.concatenate([r.astype(BF16), k], axis=1) for r, k in zip(right, start_keys)]
+    solved, _ = solved_with(inverse, once, both)
+    ended = [dot(e, s) for e, s in zip(ends, solved)]
+    result = [dot(i, s) for i, s in zip(inside, solved)]
     for h in range(heads):
-        state_ref[h] = states[h]
-        map_ref[h] = maps[h].astype(BF16)
-        out_ref[:, h * DV : h * DV + DV] = outs[h]
-        through_ref[:, h * DK : h * DK + DK] = throughs[h]
+        state_ref[h] = ended[h][:, :DV]
+        map_ref[h] = (scaled_eye(throughs[h]) - ended[h][:, DV:]).astype(BF16)
+        out_ref[:, h * DV : h * DV + DV] = result[h][:, :DV]
+        through_ref[:, h * DK : h * DK + DK] = (start_queries[h] - result[h][:, DV:]).astype(BF16)
 
 
 def peer_halo(own_edge_ref, edge_ref, columns):
@@ -302,7 +311,8 @@
 
 
 def peer_kernel(down_ref, along_ref, pack_ref, own_edge_ref, edge_ref, weight_ref, own_state_ref, own_map_ref,
-                state_ref, map_ref, solved_ref, decay_ref, start_ref, key_ref, end_ref, *pair_map_ref):
+                state_ref, solved_ref, solver_ref, start_key_ref, ended_ref, passing_ref, decay_ref, start_ref, key_ref,
+                pair_state_ref, *pair_map_ref):
     y = lax.axis_index("ctx") % 2
     rows = pack_ref.shape[0] - EDGE
     heads = own_state_ref.shape[0]
@@ -312,7 +322,7 @@
         sum(pack_ref[rows : rows + heads, (3 * part + i) * rows : (3 * part + i + 1) * rows].astype(F32) for i in range(3))
         for part in range(2)
     ]
-    states, maps, solved, decays, starts, keys_t = state_terms(
+    lower, right, start_keys, ends, throughs, decays, starts, keys_t = block_terms(
         *counts(down_ref, along_ref, 1 - y, rows),
         peer_halo(own_edge_ref, edge_ref, columns),
         lambda g: pack_ref[0:rows, g * DK : g * DK + DK],
@@ -321,61 +331,88 @@
         gates[0],
         gates[1],
     )
+    entering = [where_y(y, jnp.zeros((DK, DV), F32), own_state_ref[h]) for h in range(heads)]
+    right = [r - dot(k, e) for r, k, e in zip(right, start_keys, entering)]
+    inverse, once = solve_terms(lower)
+    solved, twice = solved_with(inverse, once, right)
+    ended = [dot(e, s) for e, s in zip(ends, solved)]
+    states = [t * e + s for t, e, s in zip(throughs, entering, ended)]
+    moved = [dot(own_map_ref[h], states[h]) for h in range(heads)]
     for h in range(heads):
-        own_state, own_map = own_state_ref[h], own_map_ref[h]
-        maps16 = maps[h].astype(BF16)
-        state_0, state_1 = where_y(y, states[h], own_state), where_y(y, own_state, states[h])
-        map_0, map_1 = where_y(y, maps16, own_map), where_y(y, own_map, maps16)
-        end_ref[h] = (state_1 + dot(map_1, state_0)).astype(BF16)
-        if pair_map_ref:
-            pair_map_ref[0][h] = dot(map_1, map_0).astype(BF16)
+        pair_state_ref[h] = where_y(y, own_state_ref[h] + moved[h], states[h]).astype(BF16)
+        state_ref[h] = states[h].astype(BF16)
+    if pair_map_ref:
+        solved_keys, _ = solved_with(inverse, once, start_keys)
+        for h in range(heads):
+            own_map = own_map_ref[h]
+            peer_map = scaled_eye(throughs[h]) - dot(ends[h], solved_keys[h])
+            pair_map_ref[0][h] = where_y(y, dot(own_map, peer_map), dot(peer_map, own_map)).astype(BF16)
+    solver = (inverse, once, twice)
     for h in range(heads):
-        state_ref[h] = states[h]
-        map_ref[h] = maps[h].astype(BF16)
         solved_ref[h] = solved[h]
+        for i in range(3):
+            solver_ref[i * heads + h] = solver[i][h]
+        start_key_ref[h] = start_keys[h]
+        ended_ref[h] = ends[h]
+        passing_ref[h : h + 1] = throughs[h]
         decay_ref[h] = decays[h]
         start_ref[h] = starts[h]
     for g in range(heads // 2):
         key_ref[g] = keys_t[g]
 
 
-def local_kernel(own_state_ref, own_map_ref, own_out_ref, own_through_ref, state_ref, map_ref, solved_ref, decay_ref,
-                 start_ref, key_ref, down_ref, along_ref, late_ref, own_edge_ref, edge_ref, conv_ref, weight_hbm,
-                 out_ref, through_ref, weight_ref, sems):
-    y = lax.axis_index("ctx") % 2
+def passing_kernel(solver_ref, start_key_ref, ended_ref, passing_ref, weight_hbm, solved_ref, map_ref, weight_ref, sems):
     depth = weight_ref.shape[0]
     copies = Copies(sems)
     part = depth // PARTS
     for i in range(PARTS):
-        from_row = pl.multiple_of(y * depth + i * part, part)
+        from_row = pl.multiple_of(lax.axis_index("ctx") % 2 * depth + i * part, part)
         copies.start(weight_hbm.at[pl.ds(from_row, part), :], weight_ref.at[pl.ds(i * part, part), :])
+    heads = start_key_ref.shape[0]
+    every = range(heads)
+    inverse, once, twice = ([solver_ref[i * heads + h] for h in every] for i in range(3))
+    solved = [dot(inverse[h], start_key_ref[h]) for h in every]
+    solved = [k + dot(m, k) for m, k in zip(once, solved)]
+    solved = [(k + dot(m, k)).astype(BF16) for m, k in zip(twice, solved)]
+    ended = [dot(ended_ref[h], solved[h]) for h in every]
+    for h in every:
+        solved_ref[h] = solved[h]
+        map_ref[h] = (scaled_eye(passing_ref[h : h + 1]) - ended[h]).astype(BF16)
+    copies.wait()
+
+
+def local_kernel(own_state_ref, own_map_ref, own_out_ref, own_through_ref, state_ref, map_ref, solved_ref, solved_key_ref,
+                 decay_ref, start_ref, key_ref, down_ref, along_ref, late_ref, own_edge_ref, edge_ref, conv_ref,
+                 out_ref, through_ref):
+    y = lax.axis_index("ctx") % 2
     rows = own_out_ref.shape[0]
     heads = own_state_ref.shape[0]
     columns = groups(heads)
-    outs, throughs = query_terms(
+    inside, start_queries = query_terms(
         counts(down_ref, along_ref, 1 - y, rows)[0],
         peer_halo(own_edge_ref, edge_ref, columns),
         lambda g: late_ref[:, g * DK : g * DK + DK],
         lambda which, g: conv_ref[:, columns(which, g)],
-        [solved_ref[h] for h in range(heads)],
         [decay_ref[h] for h in range(heads)],
         [start_ref[h] for h in range(heads)],
         [key_ref[g] for g in range(heads // 2)],
     )
-    for h in range(heads):
+    every = range(heads)
+    outs = [dot(inside[h], solved_ref[h]) for h in every]
+    passed = [dot(inside[h], solved_key_ref[h]) for h in every]
+    state_0 = [where_y(y, state_ref[h], own_state_ref[h].astype(BF16)) for h in every]
+    own_throughs = [own_through_ref[:, h * DK : h * DK + DK] for h in every]
+    extra = [dot(where_y(y, own_throughs[h], start_queries[h].astype(BF16)), state_0[h]) for h in every]
+    throughs = [(start_queries[h] - passed[h]).astype(BF16) for h in every]
+    moved = [
+        dot(where_y(y, own_throughs[h], throughs[h]), where_y(y, map_ref[h], own_map_ref[h])).astype(BF16) for h in every
+    ]
+    for h in every:
         lanes = slice(h * DV, h * DV + DV)
-        own_out, own_through = own_out_ref[:, lanes], own_through_ref[:, lanes]
-        out, through = outs[h], throughs[h]
-        state_0 = where_y(y, state_ref[h], own_state_ref[h]).astype(BF16)
-        map_0 = where_y(y, map_ref[h], own_map_ref[h])
-        through_1 = where_y(y, own_through, through)
-        more = dot(through_1, jnp.concatenate([state_0, map_0], axis=1))
-        extra, moved = more[:, :DV], more[:, DV:].astype(BF16)
-        out_ref[0:rows, lanes] = own_out + where_y(y, extra, jnp.zeros_like(extra))
-        out_ref[rows:, lanes] = out + where_y(y, jnp.zeros_like(extra), extra)
-        through_ref[0:rows, lanes] = where_y(y, moved, own_through)
-        through_ref[rows:, lanes] = where_y(y, through, moved)
-    copies.wait()
+        out_ref[0:rows, lanes] = own_out_ref[:, lanes] + where_y(y, extra[h], jnp.zeros_like(extra[h]))
+        out_ref[rows:, lanes] = outs[h] + where_y(y, jnp.zeros_like(extra[h]), extra[h])
+        through_ref[0:rows, lanes] = where_y(y, moved[h], own_throughs[h])
+        through_ref[rows:, lanes] = where_y(y, throughs[h], moved[h])
 
 
 def feature_columns(weight_ref, other_core, other_x):
@@ -525,9 +562,12 @@
     peer = call(
         peer_kernel,
         [
-            (square, F32),
             (square, BF16),
-            ((heads, rows, DK + DV), BF16),
+            ((heads, rows, DV), BF16),
+            ((3 * heads, rows, rows), BF16),
+            ((heads, rows, DK), BF16),
+            ((heads, DK, rows), BF16),
+            ((heads, rows), F32),
             ((heads, rows, rows), F32),
             ((heads, rows, DK), F32),
             ((heads // 2, DK, rows), BF16),
@@ -539,24 +579,33 @@
         flops=2_000_000_000,
         moved=4_000_000,
     )
-    state, map_, solved, decay, start, key, end = peer[:7]
+    end = peer[9]
     def from_earlier(value):
         return lax.ppermute(value, "ctx", even_swap), lax.ppermute(value, ("ctx", "head"), odd_swap)
 
     entering = from_earlier(end)
     for _ in range(hops - 1):
         earlier = jnp.where(lax.axis_index("ctx") // 2 % 2 == 1, *entering)
-        moved = jnp.einsum("hij,hjk->hik", peer[7], earlier, preferred_element_type=F32)
+        moved = jnp.einsum("hij,hjk->hik", peer[10], earlier, preferred_element_type=F32)
         moved = jnp.where(lax.axis_index("ctx") < 2, 0.0, moved)
         entering = from_earlier((end.astype(F32) + moved).astype(BF16))
-    out, through, weight = call(
+    state, solved, solver, start_key, ended, passing, decay, start, key = peer[:9]
+    solved_key, map_, weight = call(
+        passing_kernel,
+        [(square, BF16), (square, BF16), ((value_width, out_weight.shape[1]), BF16)],
+        (solver, start_key, ended, passing, out_weight),
+        "passing",
+        hbm=(4,),
+        scratch=(pltpu.SemaphoreType.DMA((PARTS,)),),
+        flops=1_000_000_000,
+        moved=4_000_000,
+    )
+    out, through = call(
         local_kernel,
-        [((2 * rows, value_width), F32), ((2 * rows, value_width), BF16), ((value_width, out_weight.shape[1]), BF16)],
-        (own_state, own_map, own_out, own_through, state, map_, solved, decay, start, key, down, along, got_late, own_edge,
-         got_far_edge, weights, out_weight),
+        [((2 * rows, value_width), F32), ((2 * rows, value_width), BF16)],
+        (own_state, own_map, own_out, own_through, state, map_, solved, solved_key, decay, start, key, down, along, got_late,
+         own_edge, got_far_edge, weights),
         "local_outputs",
-        hbm=(16,),
-        scratch=(pltpu.SemaphoreType.DMA((PARTS,)),),
         flops=1_000_000_000,
         moved=4_000_000,
     )

time: 32.8 us -> 32.4 us (0.988)
  waiting for transfers between devices: 8.98 us -> 8.28 us
    ppermute x1, waiting for transfers between devices: 1.55 us -> 0.01 us  [body(): got_late = lax.ppermute(late, 'ctx', swap)]
    ppermute x1, waiting for transfers between devices: 0.01 us -> 0.77 us  [from_earlier(): lax.ppermute(value, 'ctx', even_swap)]
    pallas_call x10 -> x11, Pallas kernels: 11.8 us -> 12.1 us  [call(): pl.pallas_call(kernel, out_shape=[jax.ShapeDtypeStruct(shape, kind) for s...]
  transfers between devices with their start and end apart: 11 -> 11, of which waited for: 5 -> 6; matrix products, arithmetic and copies ran while one was open for 0% -> 0% of each run, Pallas kernels for 28% -> 30%
where the time goes in v7:
time: 32.4 us; the launch traced here: 32.2 us
  Pallas kernels  12.1 us (37%)
  starting transfers between devices  11.7 us (36%)
  waiting for transfers between devices  8.28 us (26%)
    pallas_call x11, Pallas kernels, call(): pl.pallas_call(kernel, out_shape=[jax.ShapeDtypeStruct(shape, kind) for s...  12.1 us
    ppermute x1, starting transfers between devices, body(): got_xy = lax.ppermute(to_xy, ('ctx', 'head'), both)  3.17 us
    ppermute x1, starting transfers between devices, body(): got_edge = lax.ppermute(edge, 'ctx', ahead_1)  3.02 us
    ppermute x1, waiting for transfers between devices, body(): got_x = lax.ppermute(to_x, 'head', [(i, i ^ 2) for i in range(head_count)])  2.51 us
    ppermute x1, waiting for transfers between devices, body(): got_xy = lax.ppermute(to_xy, ('ctx', 'head'), both)  2.15 us
    ppermute x1, waiting for transfers between devices, body(): got_edge = lax.ppermute(edge, 'ctx', ahead_1)  2.06 us
    ppermute x1, starting transfers between devices, body(): got_y = lax.ppermute(to_y, 'ctx', swap)  1.71 us
    ppermute x1, starting transfers between devices, from_earlier(): lax.ppermute(value, 'ctx', even_swap)  1.57 us
  transfers between devices with their start and end apart: 11, of which 6 were waited for; matrix products, arithmetic and copies ran while one was open for 0% of the time, Pallas kernels for 30%

profile of v7, /device:TPU:0, one launch (start us, length us, event | category | flops | bytes accessed | tf_op | source)
XLA Modules:
  0.0 32.2 jit_solution(16596988071737271619)
XLA Ops:
  0.0 1.1 %pack.1 = (bf16[16,1024]{1,0:T(8,128)(2,1)S(1)}, bf16[144,768]{1,0:T(8,128)(2,1)S(1)}, f32[8,128]{1,0:T(8,128)S(1)}) custom-call(bf16[128,512]{1,0:T(8,128)(2,1)} %q_ref.3, bf16[128,512]{1,0:T(8,128)(2,1)} %k_ref.3, bf16[128,1024]{1,0:T(8,128)(2,1)} %v_ref.3, f32[8,128]{1,0:T(8,128)} %decay_ref.1, f32[8,128]{1,0:T(8,128)} %beta_ref.1), custom_call_target="tpu_custom_call" | custom-call | tf_op jit(solution)/shard_map/pack/pallas_call | solution.py:471
  1.1 3.0 %collective-permute-start = (bf16[16,1024]{1,0:T(8,128)(2,1)S(1)}, bf16[16,1024]{1,0:T(8,128)(2,1)S(1)}, u32[]{:S(2)}, u32[]{:S(2)}) collective-permute-start(bf16[16,1024]{1,0:T(8,128)(2,1)S(1)} %get-tuple-element.51), channel_id=1, source_target_pairs={{0,4},{4,8},{8,12},{12,16},{16,20},{20,24},{24,28},{28,0},{1,5},{5... | collective-permute-start | bytes 98312 | tf_op jit(solution)/shard_map/ppermute | solution.py:547
  4.1 1.5 %collective-permute-start.1 = (bf16[144,768]{1,0:T(8,128)(2,1)S(1)}, bf16[144,768]{1,0:T(8,128)(2,1)S(1)}, u32[]{:S(2)}, u32[]{:S(2)}) collective-permute-start(bf16[144,768]{1,0:T(8,128)(2,1)S(1)} %get-tuple-element.58), channel_id=1, source_target_pairs={{0,4},{4,0},{8,12},{12,8},{16,20},{20,16},{24,28},{28,24},{1,5},{5... | collective-permute-start | bytes 663560 | tf_op jit(solution)/shard_map/ppermute | solution.py:548
  5.6 1.3 %early.1 = (bf16[16,1024]{1,0:T(8,128)(2,1)S(1)}, bf16[128,768]{1,0:T(8,128)(2,1)S(1)}, bf16[128,1024]{1,0:T(8,128)(2,1)S(1)}, f32[4,1024]{1,0:T(4,128)S(1)}, bf...) custom-call(bf16[128,512]{1,0:T(8,128)(2,1)} %q_ref.3, bf16[128,512]{1,0:T(8,128)(2,1)} %k_ref.3, ...), custom_call_target="tpu_custom_call" | custom-call | flops 10000000000 | bytes 2000000 | tf_op jit(solution)/shard_map/early/pallas_call | solution.py:471
  7.0 2.1 %collective-permute-done.halo_ref = bf16[16,1024]{1,0:T(8,128)(2,1)S(1)} collective-permute-done((bf16[16,1024]{1,0:T(8,128)(2,1)S(1)}, bf16[16,1024]{1,0:T(8,128)(2,1)S(1)}, u32[]{:S(2)}, u32[]{:S(2)}) %collective-permute-start) | collective-permute-done | bytes 32800 | tf_op jit(solution)/shard_map/ppermute | solution.py:547
  9.1 2.5 %own_terms.1 = (f32[4,128,128]{2,1,0:T(8,128)S(1)}, bf16[4,128,128]{2,1,0:T(8,128)(2,1)S(1)}, f32[128,512]{1,0:T(8,128)S(1)}, bf16[128,512]{1,0:T(8,128)(2,1)S(1)}) custom-call(s32[264,128]{1,0:T(8,128)S(1)} %get-tuple-element.46.down_ref, s32[8,256]{1,0:T(8,128)S(1)} %get-tuple-element.47.along_ref, bf16[128,1024]{1,0:T(8,128)(2,1)S(1)} %get-tuple-element.48.own_ref, ...), custom_call_target="tpu_custom_call" | custom-call | flops 1000000 | bytes 4000000 | tf_op jit(solution)/shard_map/own_terms/pallas_call | solution.py:471
  11.5 0.1 collective-permute-start.3
  11.7 2.4 %peer_terms.1 = (bf16[4,128,128]{2,1,0:T(8,128)(2,1)S(1)}, bf16[4,128,128]{2,1,0:T(8,128)(2,1)S(1)}, bf16[12,128,128]{2,1,0:T(8,128)(2,1)S(1)}, bf16[4,128,128]{...) custom-call(s32[264,128]{1,0:T(8,128)S(1)} %get-tuple-element.46.dow, ...), custom_call_target="tpu_custom_call" | custom-call | flops 2000000000 | bytes 4000000 | tf_op jit(solution)/shard_map/peer_terms/pallas_call | solution.py:471
  14.1 1.6 %collective-permute-start.4 = (bf16[4,128,128]{2,1,0:T(8,128)(2,1)S(1)}, bf16[4,128,128]{2,1,0:T(8,128)(2,1)S(1)}, u32[]{:S(2)}, u32[]{:S(2)}) collective-permute-start(bf16[4,128,128]{2,1,0:T(8,128)(2,1)S(1)} %get-tuple-element.74), channel_id=1, source_target_pairs={{0,8},{4,12},{8,0},{12,4},{16,24},{20,28},{24,16},{28,20},{1,9},{5... | collective-permute-start | bytes 393224 | tf_op jit(solution)/shard_map/ppermute | solution.py:584
  15.6 2.1 %passing.1 = (bf16[4,128,128]{2,1,0:T(8,128)(2,1)S(1)}, bf16[4,128,128]{2,1,0:T(8,128)(2,1)S(1)}, bf16[512,2048]{1,0:T(8,128)(2,1)S(1)}) custom-call(bf16[12,128,128]{2,1,0:T(8,128)(2,1)S(1)} %get-tuple-element.61.solver_ref, bf16[4,128,128]{2,1,0:T(8,128)(2,1)S(1)} %get-tuple-element.62.start_key_ref, bf16[4,128,128]{2,1,0:T(8,128)(2,1)S(1)} %get-tuple-element.63.ended_ref, ...), custom_call_target="tpu_custom_call" | custom-call | flops 1000000000 | bytes 4000000 | tf_op jit(solution)/shard_map/passing/pallas_call | solution.py:471
  17.7 0.6 %local_outputs.1 = (f32[256,512]{1,0:T(8,128)S(1)}, bf16[256,512]{1,0:T(8,128)(2,1)S(1)}) custom-call(f32[4,128,128]{2,1,0:T(8,128)S(1)} %get-tuple-element.52.own_state_ref, bf16[4,128,128]{2,1,0:T(8,128)(2,1)S(1)} %get-tuple-element.55.own_map_ref, f32[128,512]{1,0:T(8,128)S(1)} %get-tuple-element.56.own_out_ref, ...), custom_call_target="tpu_custom_call" | custom-call | flops 1000000000 | bytes 4000000 | tf_op jit(solution)/shard_map/local_outputs/pallas_call | solution.py:471
  18.3 0.8 %collective-permute-done.4.even_ref = bf16[4,128,128]{2,1,0:T(8,128)(2,1)S(1)} collective-permute-done((bf16[4,128,128]{2,1,0:T(8,128)(2,1)S(1)}, bf16[4,128,128]{2,1,0:T(8,128)(2,1)S(1)}, u32[]{:S(2)}, u32[]{:S(2)}) %collective-permute-start.4) | collective-permute-done | bytes 131104 | tf_op jit(solution)/shard_map/ppermute | solution.py:584
  19.1 0.7 %mix.1 = (bf16[256,512]{1,0:T(8,128)(2,1)S(1)}, bf16[128,512]{1,0:T(8,128)(2,1)S(1)}, bf16[128,512]{1,0:T(8,128)(2,1)S(1)}) custom-call(f32[256,512]{1,0:T(8,128)S(1)} %get-tuple-element.72.out_ref, bf16[256,512]{1,0:T(8,128)(2,1)S(1)} %get-tuple-element.73.through_ref, bf16[4,128,128]{2,1,0:T(8,128)(2,1)S(1)} %collective-permute-done.4.even_ref, ...), custom_call_target="tpu_custom_call" | custom-call | tf_op jit(solution)/shard_map/mix/pallas_call | solution.py:471
  19.8 0.1 collective-permute-start.6
  19.9 0.6 %project.1 = (bf16[3,128,512]{2,1,0:T(8,128)(2,1)S(1)}, bf16[3,128,512]{2,1,0:T(8,128)(2,1)S(1)}) custom-call(bf16[256,512]{1,0:T(8,128)(2,1)S(1)} %get-tuple-element.77.mixed_ref, bf16[512,2048]{1,0:T(8,128)(2,1)S(1)} %get-tuple-element.76.weight_ref), custom_call_target="tpu_custom_call" | custom-call | flops 2000000000 | bytes 4000000 | tf_op jit(solution)/shard_map/project/pallas_call | solution.py:471
  20.5 0.7 %collective-permute-done.6.got_ref = bf16[128,512]{1,0:T(8,128)(2,1)S(1)} collective-permute-done((bf16[128,512]{1,0:T(8,128)(2,1)S(1)}, bf16[128,512]{1,0:T(8,128)(2,1)S(1)}, u32[]{:S(2)}, u32[]{:S(2)}) %collective-permute-start.6) | collective-permute-done | bytes 131104 | tf_op jit(solution)/shard_map/ppermute | solution.py:619
  21.2 0.1 collective-permute-start.7
  21.4 3.2 %collective-permute-start.10 = (bf16[128,512]{1,0:T(8,128)(2,1)S(1)}, bf16[128,512]{1,0:T(8,128)(2,1)S(1)}, u32[]{:S(2)}, u32[]{:S(2)}) collective-permute-start(bf16[128,512]{1,0:T(8,128)(2,1)S(1)} %core_sum_xy.1), channel_id=1, source_target_pairs={{0,6},{1,7},{2,4},{3,5},{4,2},{5,3},{6,0},{7,1},{8,14},{9,15},{10,... | collective-permute-start | bytes 393224 | tf_op jit(solution)/shard_map/ppermute | solution.py:640
  24.6 0.1 core_sums.1
  24.7 0.4 %collective-permute-start.8 = (bf16[128,512]{1,0:T(8,128)(2,1)S(1)}, bf16[128,512]{1,0:T(8,128)(2,1)S(1)}, u32[]{:S(2)}, u32[]{:S(2)}) collective-permute-start(bf16[128,512]{1,0:T(8,128)(2,1)S(1)} %get-tuple-element.83), channel_id=1, source_target_pairs={{0,2},{1,3},{2,0},{3,1},{4,6},{5,7},{6,4},{7,5},{8,10},{9,11},{10,... | collective-permute-start | bytes 393224 | tf_op jit(solution)/shard_map/ppermute | solution.py:641
  25.1 1.7 %collective-permute-start.9 = (bf16[128,512]{1,0:T(8,128)(2,1)S(1)}, bf16[128,512]{1,0:T(8,128)(2,1)S(1)}, u32[]{:S(2)}, u32[]{:S(2)}) collective-permute-start(bf16[128,512]{1,0:T(8,128)(2,1)S(1)} %get-tuple-element.84), channel_id=1, source_target_pairs={{0,4},{4,0},{8,12},{12,8},{16,20},{20,16},{24,28},{28,24},{1,5},{5... | collective-permute-start | bytes 393224 | tf_op jit(solution)/shard_map/ppermute | solution.py:642
  26.8 2.2 %collective-permute-done.10.xy_ref = bf16[128,512]{1,0:T(8,128)(2,1)S(1)} collective-permute-done((bf16[128,512]{1,0:T(8,128)(2,1)S(1)}, bf16[128,512]{1,0:T(8,128)(2,1)S(1)}, u32[]{:S(2)}, u32[]{:S(2)}) %collective-permute-start.10) | collective-permute-done | bytes 131104 | tf_op jit(solution)/shard_map/ppermute | solution.py:640
  28.9 2.5 %collective-permute-done.8.x_ref = bf16[128,512]{1,0:T(8,128)(2,1)S(1)} collective-permute-done((bf16[128,512]{1,0:T(8,128)(2,1)S(1)}, bf16[128,512]{1,0:T(8,128)(2,1)S(1)}, u32[]{:S(2)}, u32[]{:S(2)}) %collective-permute-start.8) | collective-permute-done | bytes 131104 | tf_op jit(solution)/shard_map/ppermute | solution.py:641
  31.4 0.8 %last_sum.1 = bf16[512,128]{1,0:T(8,128)(2,1)} custom-call(f32[128,512]{1,0:T(8,128)S(1)} %get-tuple-element.82.mine_ref, bf16[128,512]{1,0:T(8,128)(2,1)S(1)} %collective-permute-done.8.x_ref, bf16[128,512]{1,0:T(8,128)(2,1)S(1)} %collective-permute-done.9.y_ref, bf16[128,512]{1,0:T(8,128)(2,1)S(1)} %collective-permute-done.10.xy_ref), custom_call_target="tpu_custom_call" | custom-call | tf_op jit(solution)/shard_map/last_sum/pallas_call | solution.py:471
  (11 shorter events, 0.2 us)
Async XLA Ops:
  1.1 8.0 %collective-permute-start = (bf16[16,1024]{1,0:T(8,128)(2,1)S(1)}, bf16[16,1024]{1,0:T(8,128)(2,1)S(1)}, u32[]{:S(2)}, u32[]{:S(2)}) collective-permute-start(bf16[16,1024]{1,0:T(8,128)(2,1)S(1)} %get-tuple-element.51), channel_id=1, source_target_pairs={{0,4},{4,8},{8,12},{12,16},{16,20},{20,24},{24,28},{28,0},{1,5},{5... | collective-permute-start | bytes 98312 | tf_op jit(solution)/shard_map/ppermute | solution.py:547
  4.1 7.6 %collective-permute-start.1 = (bf16[144,768]{1,0:T(8,128)(2,1)S(1)}, bf16[144,768]{1,0:T(8,128)(2,1)S(1)}, u32[]{:S(2)}, u32[]{:S(2)}) collective-permute-start(bf16[144,768]{1,0:T(8,128)(2,1)S(1)} %get-tuple-element.58), channel_id=1, source_target_pairs={{0,4},{4,0},{8,12},{12,8},{16,20},{20,16},{24,28},{28,24},{1,5},{5... | collective-permute-start | bytes 663560 | tf_op jit(solution)/shard_map/ppermute | solution.py:548
  7.0 4.7 %collective-permute-start.2 = (bf16[16,1024]{1,0:T(8,128)(2,1)S(1)}, bf16[16,1024]{1,0:T(8,128)(2,1)S(1)}, u32[]{:S(2)}, u32[]{:S(2)}) collective-permute-start(bf16[16,1024]{1,0:T(8,128)(2,1)S(1)} %get-tuple-element.59.own_edge_ref), channel_id=1, source_target_pairs={{0,1},{1,0},{2,3},{3,2},{4,12},{5,13},{6,14},{7,15},{8,9},{9,8},{1... | collective-permute-start | bytes 98312 | tf_op jit(solution)/shard_map/ppermute | solution.py:549
  11.5 6.2 %collective-permute-start.3 = (bf16[128,768]{1,0:T(8,128)(2,1)S(1)}, bf16[128,768]{1,0:T(8,128)(2,1)S(1)}, u32[]{:S(2)}, u32[]{:S(2)}) collective-permute-start(bf16[128,768]{1,0:T(8,128)(2,1)S(1)} %get-tuple-element.71), channel_id=1, source_target_pairs={{0,4},{4,0},{8,12},{12,8},{16,20},{20,16},{24,28},{28,24},{1,5},{5... | collective-permute-start | bytes 589832 | tf_op jit(solution)/shard_map/ppermute | solution.py:561
  14.1 5.0 %collective-permute-start.4 = (bf16[4,128,128]{2,1,0:T(8,128)(2,1)S(1)}, bf16[4,128,128]{2,1,0:T(8,128)(2,1)S(1)}, u32[]{:S(2)}, u32[]{:S(2)}) collective-permute-start(bf16[4,128,128]{2,1,0:T(8,128)(2,1)S(1)} %get-tuple-element.74), channel_id=1, source_target_pairs={{0,8},{4,12},{8,0},{12,4},{16,24},{20,28},{24,16},{28,20},{1,9},{5... | collective-permute-start | bytes 393224 | tf_op jit(solution)/shard_map/ppermute | solution.py:584
  15.6 3.5 %collective-permute-start.5 = (bf16[4,128,128]{2,1,0:T(8,128)(2,1)S(1)}, bf16[4,128,128]{2,1,0:T(8,128)(2,1)S(1)}, u32[]{:S(2)}, u32[]{:S(2)}) collective-permute-start(bf16[4,128,128]{2,1,0:T(8,128)(2,1)S(1)} %get-tuple-element.74), channel_id=1, source_target_pairs={{0,1},{1,0},{2,3},{3,2},{4,5},{5,4},{6,7},{7,6},{8,16},{9,17},{10,... | collective-permute-start | bytes 393224 | tf_op jit(solution)/shard_map/ppermute | solution.py:584
  15.6 3.5 %copy-start = (f32[128]{0:T(128)S(1)}, f32[128]{0:T(128)}, u32[]{:S(2)}) copy-start(f32[128]{0:T(128)} %param.21) | copy-start | bytes 1540
  19.8 1.4 %collective-permute-start.6 = (bf16[128,512]{1,0:T(8,128)(2,1)S(1)}, bf16[128,512]{1,0:T(8,128)(2,1)S(1)}, u32[]{:S(2)}, u32[]{:S(2)}) collective-permute-start(bf16[128,512]{1,0:T(8,128)(2,1)S(1)} %get-tuple-element.80), channel_id=1, source_target_pairs={{0,1},{1,0},{2,3},{3,2},{4,5},{5,4},{6,7},{7,6},{8,9},{9,8},{10,11... | collective-permute-start | bytes 393224 | tf_op jit(solution)/shard_map/ppermute | solution.py:619
  21.2 3.4 %collective-permute-start.7 = (bf16[3,128,512]{2,1,0:T(8,128)(2,1)S(1)}, bf16[3,128,512]{2,1,0:T(8,128)(2,1)S(1)}, u32[]{:S(2)}, u32[]{:S(2)}) collective-permute-start(bf16[3,128,512]{2,1,0:T(8,128)(2,1)S(1)} %get-tuple-element.81), channel_id=1, source_target_pairs={{0,1},{1,0},{2,3},{3,2},{4,5},{5,4},{6,7},{7,6},{8,9},{9,8},{10,11... | collective-permute-start | bytes 1179656 | tf_op jit(solution)/shard_map/ppermute | solution.py:629
  21.4 7.5 %collective-permute-start.10 = (bf16[128,512]{1,0:T(8,128)(2,1)S(1)}, bf16[128,512]{1,0:T(8,128)(2,1)S(1)}, u32[]{:S(2)}, u32[]{:S(2)}) collective-permute-start(bf16[128,512]{1,0:T(8,128)(2,1)S(1)} %core_sum_xy.1), channel_id=1, source_target_pairs={{0,6},{1,7},{2,4},{3,5},{4,2},{5,3},{6,0},{7,1},{8,14},{9,15},{10,... | collective-permute-start | bytes 393224 | tf_op jit(solution)/shard_map/ppermute | solution.py:640
  24.7 6.7 %collective-permute-start.8 = (bf16[128,512]{1,0:T(8,128)(2,1)S(1)}, bf16[128,512]{1,0:T(8,128)(2,1)S(1)}, u32[]{:S(2)}, u32[]{:S(2)}) collective-permute-start(bf16[128,512]{1,0:T(8,128)(2,1)S(1)} %get-tuple-element.83), channel_id=1, source_target_pairs={{0,2},{1,3},{2,0},{3,1},{4,6},{5,7},{6,4},{7,5},{8,10},{9,11},{10,... | collective-permute-start | bytes 393224 | tf_op jit(solution)/shard_map/ppermute | solution.py:641
  25.1 6.4 %collective-permute-start.9 = (bf16[128,512]{1,0:T(8,128)(2,1)S(1)}, bf16[128,512]{1,0:T(8,128)(2,1)S(1)}, u32[]{:S(2)}, u32[]{:S(2)}) collective-permute-start(bf16[128,512]{1,0:T(8,128)(2,1)S(1)} %get-tuple-element.84), channel_id=1, source_target_pairs={{0,4},{4,0},{8,12},{12,8},{16,20},{20,16},{24,28},{28,24},{1,5},{5... | collective-permute-start | bytes 393224 | tf_op jit(solution)/shard_map/ppermute | solution.py:642

commit v8 on v7

--- a/solution.py
+++ b/solution.py
@@ -382,8 +382,8 @@
 
 
 def local_kernel(own_state_ref, own_map_ref, own_out_ref, own_through_ref, state_ref, map_ref, solved_ref, solved_key_ref,
-                 decay_ref, start_ref, key_ref, down_ref, along_ref, late_ref, own_edge_ref, edge_ref, conv_ref,
-                 out_ref, through_ref):
+                 decay_ref, start_ref, key_ref, down_ref, along_ref, late_ref, own_edge_ref, edge_ref, conv_ref, gate_ref, gain_ref,
+                 out_ref, through_ref, factor_ref):
     y = lax.axis_index("ctx") % 2
     rows = own_out_ref.shape[0]
     heads = own_state_ref.shape[0]
@@ -413,6 +413,13 @@
         out_ref[rows:, lanes] = outs[h] + where_y(y, jnp.zeros_like(extra[h]), extra[h])
         through_ref[0:rows, lanes] = where_y(y, moved[h], own_throughs[h])
         through_ref[rows:, lanes] = where_y(y, throughs[h], moved[h])
+    key_width = heads // 2 * DK
+    for h in every:
+        lanes = slice(h * DV, h * DV + DV)
+        gates = (gate_ref[:, lanes], late_ref[:, key_width + h * DV : key_width + h * DV + DV])
+        for b, gate in enumerate(gates):
+            gate = gate.astype(F32)
+            factor_ref[b * rows : b * rows + rows, lanes] = gain_ref[...] * (gate / (1.0 + jnp.exp(-gate)))
 
 
 def feature_columns(weight_ref, other_core, other_x):
@@ -423,27 +430,25 @@
     return weight_ref[:, pl.ds(pl.multiple_of(block * width, width), width)]
 
 
-def mix_kernel(out_ref, through_ref, even_ref, odd_ref, gate_ref, late_ref, gain_ref, weight_ref, mixed_ref, send_ref, keep_ref):
+def mix_kernel(out_ref, through_ref, even_ref, odd_ref, factor_ref, weight_ref, mixed_ref, send_ref):
     from_even = lax.axis_index("ctx") // 2 % 2
     heads = even_ref.shape[0]
-    rows = gate_ref.shape[0]
-    key_width = late_ref.shape[1] - heads * DV
-    for h in range(heads):
-        lanes = slice(h * DV, h * DV + DV)
-        o = out_ref[:, lanes] + dot(through_ref[:, lanes], where_y(from_even, even_ref[h], odd_ref[h]))
-        gate = jnp.concatenate([gate_ref[:, lanes], late_ref[:, key_width + h * DV : key_width + h * DV + DV]], axis=0)
-        gate = gate.astype(F32)
+    rows = out_ref.shape[0] // 2
+    every = [slice(h * DV, h * DV + DV) for h in range(heads)]
+    moved = [dot(through_ref[:, lanes], where_y(from_even, even_ref[h], odd_ref[h])) for h, lanes in enumerate(every)]
+    for lanes, o in zip(every, moved):
+        o = out_ref[:, lanes] + o
         scale = lax.rsqrt(jnp.mean(o * o, axis=-1, keepdims=True) + 1e-6)
-        mixed_ref[:, lanes] = (o * scale * gain_ref[...] * (gate / (1.0 + jnp.exp(-gate)))).astype(BF16)
+        mixed_ref[:, lanes] = (o * scale * factor_ref[:, lanes]).astype(BF16)
     send_ref[...] = jnp.dot(mixed_ref[rows:, :], feature_columns(weight_ref, 1, 1), preferred_element_type=F32).astype(BF16)
-    keep_ref[...] = jnp.dot(mixed_ref[rows:, :], feature_columns(weight_ref, 0, 1), preferred_element_type=F32).astype(BF16)
 
 
 QUARTERS = ((0, 0), (0, 1), (1, 0))
 
 
-def project_kernel(mixed_ref, weight_ref, send_ref, keep_ref):
+def project_kernel(mixed_ref, weight_ref, far_ref, send_ref, keep_ref):
     rows = send_ref.shape[1]
+    far_ref[...] = jnp.dot(mixed_ref[rows:, :], feature_columns(weight_ref, 0, 1), preferred_element_type=F32).astype(BF16)
     for c, to_ref in ((0, send_ref), (1, keep_ref)):
         for i, (peer, far) in enumerate(QUARTERS):
             weights = feature_columns(weight_ref, 1 - c, far)
@@ -600,26 +605,26 @@
         flops=1_000_000_000,
         moved=4_000_000,
     )
-    out, through = call(
+    out, through, factor = call(
         local_kernel,
-        [((2 * rows, value_width), F32), ((2 * rows, value_width), BF16)],
+        [((2 * rows, value_width), F32), ((2 * rows, value_width), BF16), ((2 * rows, value_width), F32)],
         (own_state, own_map, own_out, own_through, state, map_, solved, solved_key, decay, start, key, down, along, got_late,
-         own_edge, got_far_edge, weights),
+         own_edge, got_far_edge, weights, own_gate, norm_gain.reshape(1, DV)),
         "local_outputs",
         flops=1_000_000_000,
         moved=4_000_000,
     )
     cores = [(i, i ^ 1) for i in range(head_count)]
-    mixed, send_far, keep_far = call(
+    mixed, send_far = call(
         mix_kernel,
-        [((2 * rows, value_width), BF16), ((rows, width), BF16), ((rows, width), BF16)],
-        (out, through, *entering, own_gate, got_late, norm_gain.reshape(1, DV), weight),
+        [((2 * rows, value_width), BF16), ((rows, width), BF16)],
+        (out, through, *entering, factor, weight),
         "mix",
     )
     got_far = lax.ppermute(send_far, "head", cores)
-    send, keep = call(
+    keep_far, send, keep = call(
         project_kernel,
-        [((3, rows, width), BF16), ((3, rows, width), BF16)],
+        [((rows, width), BF16), ((3, rows, width), BF16), ((3, rows, width), BF16)],
         (mixed, weight),
         "project",
         flops=2_000_000_000,

time: 32.4 us -> 32.2 us (level)
  no operation moved by 1% of the time
where the time goes in v8:
time: 32.2 us; the launch traced here: 32 us
  Pallas kernels  12.1 us (38%)
  starting transfers between devices  11.7 us (36%)
  waiting for transfers between devices  8.09 us (25%)
    pallas_call x11, Pallas kernels, call(): pl.pallas_call(kernel, out_shape=[jax.ShapeDtypeStruct(shape, kind) for s...  12.1 us
    ppermute x1, starting transfers between devices, body(): got_xy = lax.ppermute(to_xy, ('ctx', 'head'), both)  3.18 us
    ppermute x1, starting transfers between devices, body(): got_edge = lax.ppermute(edge, 'ctx', ahead_1)  3.02 us
    ppermute x1, waiting for transfers between devices, body(): got_x = lax.ppermute(to_x, 'head', [(i, i ^ 2) for i in range(head_count)])  2.51 us
    ppermute x1, waiting for transfers between devices, body(): got_xy = lax.ppermute(to_xy, ('ctx', 'head'), both)  2.15 us
    ppermute x1, waiting for transfers between devices, body(): got_edge = lax.ppermute(edge, 'ctx', ahead_1)  2.06 us
    ppermute x1, starting transfers between devices, body(): got_y = lax.ppermute(to_y, 'ctx', swap)  1.71 us
    ppermute x1, starting transfers between devices, from_earlier(): lax.ppermute(value, 'ctx', even_swap)  1.56 us
  transfers between devices with their start and end apart: 11, of which 6 were waited for; matrix products, arithmetic and copies ran while one was open for 0% of the time, Pallas kernels for 30%

profile of v8, /device:TPU:0, one launch (start us, length us, event | category | flops | bytes accessed | tf_op | source)
XLA Modules:
  0.0 32.0 jit_solution(11860540535220835961)
XLA Ops:
  0.0 1.1 %pack.1 = (bf16[16,1024]{1,0:T(8,128)(2,1)S(1)}, bf16[144,768]{1,0:T(8,128)(2,1)S(1)}, f32[8,128]{1,0:T(8,128)S(1)}) custom-call(bf16[128,512]{1,0:T(8,128)(2,1)} %q_ref.3, bf16[128,512]{1,0:T(8,128)(2,1)} %k_ref.3, bf16[128,1024]{1,0:T(8,128)(2,1)} %v_ref.3, f32[8,128]{1,0:T(8,128)} %decay_ref.1, f32[8,128]{1,0:T(8,128)} %beta_ref.1), custom_call_target="tpu_custom_call" | custom-call | tf_op jit(solution)/shard_map/pack/pallas_call | solution.py:476
  1.1 3.0 %collective-permute-start = (bf16[16,1024]{1,0:T(8,128)(2,1)S(1)}, bf16[16,1024]{1,0:T(8,128)(2,1)S(1)}, u32[]{:S(2)}, u32[]{:S(2)}) collective-permute-start(bf16[16,1024]{1,0:T(8,128)(2,1)S(1)} %get-tuple-element.52), channel_id=1, source_target_pairs={{0,4},{4,8},{8,12},{12,16},{16,20},{20,24},{24,28},{28,0},{1,5},{5... | collective-permute-start | bytes 98312 | tf_op jit(solution)/shard_map/ppermute | solution.py:552
  4.1 1.5 %collective-permute-start.1 = (bf16[144,768]{1,0:T(8,128)(2,1)S(1)}, bf16[144,768]{1,0:T(8,128)(2,1)S(1)}, u32[]{:S(2)}, u32[]{:S(2)}) collective-permute-start(bf16[144,768]{1,0:T(8,128)(2,1)S(1)} %get-tuple-element.59), channel_id=1, source_target_pairs={{0,4},{4,0},{8,12},{12,8},{16,20},{20,16},{24,28},{28,24},{1,5},{5... | collective-permute-start | bytes 663560 | tf_op jit(solution)/shard_map/ppermute | solution.py:553
  5.6 1.3 %early.1 = (bf16[16,1024]{1,0:T(8,128)(2,1)S(1)}, bf16[128,768]{1,0:T(8,128)(2,1)S(1)}, bf16[128,1024]{1,0:T(8,128)(2,1)S(1)}, f32[4,1024]{1,0:T(4,128)S(1)}, bf...) custom-call(bf16[128,512]{1,0:T(8,128)(2,1)} %q_ref.3, bf16[128,512]{1,0:T(8,128)(2,1)} %k_ref.3, ...), custom_call_target="tpu_custom_call" | custom-call | flops 10000000000 | bytes 2000000 | tf_op jit(solution)/shard_map/early/pallas_call | solution.py:476
  7.0 2.1 %collective-permute-done.halo_ref = bf16[16,1024]{1,0:T(8,128)(2,1)S(1)} collective-permute-done((bf16[16,1024]{1,0:T(8,128)(2,1)S(1)}, bf16[16,1024]{1,0:T(8,128)(2,1)S(1)}, u32[]{:S(2)}, u32[]{:S(2)}) %collective-permute-start) | collective-permute-done | bytes 32800 | tf_op jit(solution)/shard_map/ppermute | solution.py:552
  9.1 2.5 %own_terms.1 = (f32[4,128,128]{2,1,0:T(8,128)S(1)}, bf16[4,128,128]{2,1,0:T(8,128)(2,1)S(1)}, f32[128,512]{1,0:T(8,128)S(1)}, bf16[128,512]{1,0:T(8,128)(2,1)S(1)}) custom-call(s32[264,128]{1,0:T(8,128)S(1)} %get-tuple-element.47.down_ref, s32[8,256]{1,0:T(8,128)S(1)} %get-tuple-element.48.along_ref, bf16[128,1024]{1,0:T(8,128)(2,1)S(1)} %get-tuple-element.49.own_ref, ...), custom_call_target="tpu_custom_call" | custom-call | flops 1000000 | bytes 4000000 | tf_op jit(solution)/shard_map/own_terms/pallas_call | solution.py:476
  11.5 0.1 collective-permute-start.3
  11.7 2.3 %peer_terms.1 = (bf16[4,128,128]{2,1,0:T(8,128)(2,1)S(1)}, bf16[4,128,128]{2,1,0:T(8,128)(2,1)S(1)}, bf16[12,128,128]{2,1,0:T(8,128)(2,1)S(1)}, bf16[4,128,128]{...) custom-call(s32[264,128]{1,0:T(8,128)S(1)} %get-tuple-element.47.dow, ...), custom_call_target="tpu_custom_call" | custom-call | flops 2000000000 | bytes 4000000 | tf_op jit(solution)/shard_map/peer_terms/pallas_call | solution.py:476
  14.1 1.6 %collective-permute-start.4 = (bf16[4,128,128]{2,1,0:T(8,128)(2,1)S(1)}, bf16[4,128,128]{2,1,0:T(8,128)(2,1)S(1)}, u32[]{:S(2)}, u32[]{:S(2)}) collective-permute-start(bf16[4,128,128]{2,1,0:T(8,128)(2,1)S(1)} %get-tuple-element.76), channel_id=1, source_target_pairs={{0,8},{4,12},{8,0},{12,4},{16,24},{20,28},{24,16},{28,20},{1,9},{5... | collective-permute-start | bytes 393224 | tf_op jit(solution)/shard_map/ppermute | solution.py:589
  15.6 2.1 %passing.1 = (bf16[4,128,128]{2,1,0:T(8,128)(2,1)S(1)}, bf16[4,128,128]{2,1,0:T(8,128)(2,1)S(1)}, bf16[512,2048]{1,0:T(8,128)(2,1)S(1)}) custom-call(bf16[12,128,128]{2,1,0:T(8,128)(2,1)S(1)} %get-tuple-element.62.solver_ref, bf16[4,128,128]{2,1,0:T(8,128)(2,1)S(1)} %get-tuple-element.63.start_key_ref, bf16[4,128,128]{2,1,0:T(8,128)(2,1)S(1)} %get-tuple-element.64.ended_ref, ...), custom_call_target="tpu_custom_call" | custom-call | flops 1000000000 | bytes 4000000 | tf_op jit(solution)/shard_map/passing/pallas_call | solution.py:476
  17.7 0.7 %local_outputs.1 = (f32[256,512]{1,0:T(8,128)S(1)}, bf16[256,512]{1,0:T(8,128)(2,1)S(1)}, f32[256,512]{1,0:T(8,128)S(1)}) custom-call(f32[4,128,128]{2,1,0:T(8,128)S(1)} %get-tuple-element.53.own_state_ref, bf16[4,128,128]{2,1,0:T(8,128)(2,1)S(1)} %get-tuple-element.56.own_map_ref, f32[128,512]{1,0:T(8,128)S(1)} %get-tuple-element.57.own_out_ref, ...), custom_call_target="tpu_custom_call" | custom-call | flops 1000000000 | bytes 4000000 | tf_op jit(solution)/shard_map/local_outputs/pallas_call | solution.py:476
  18.5 0.6 %collective-permute-done.4.even_ref = bf16[4,128,128]{2,1,0:T(8,128)(2,1)S(1)} collective-permute-done((bf16[4,128,128]{2,1,0:T(8,128)(2,1)S(1)}, bf16[4,128,128]{2,1,0:T(8,128)(2,1)S(1)}, u32[]{:S(2)}, u32[]{:S(2)}) %collective-permute-start.4) | collective-permute-done | bytes 131104 | tf_op jit(solution)/shard_map/ppermute | solution.py:589
  19.1 0.5 %mix.1 = (bf16[256,512]{1,0:T(8,128)(2,1)S(1)}, bf16[128,512]{1,0:T(8,128)(2,1)S(1)}) custom-call(f32[256,512]{1,0:T(8,128)S(1)} %get-tuple-element.74.out_ref, bf16[256,512]{1,0:T(8,128)(2,1)S(1)} %get-tuple-element.75.through_ref, bf16[4,128,128]{2,1,0:T(8,128)(2,1)S(1)} %collective-permute-done.4.even_ref, ...), custom_call_target="tpu_custom_call" | custom-call | tf_op jit(solution)/shard_map/mix/pallas_call | solution.py:476
  19.6 0.1 collective-permute-start.6
  19.7 0.7 %project.1 = (bf16[128,512]{1,0:T(8,128)(2,1)S(1)}, bf16[3,128,512]{2,1,0:T(8,128)(2,1)S(1)}, bf16[3,128,512]{2,1,0:T(8,128)(2,1)S(1)}) custom-call(bf16[256,512]{1,0:T(8,128)(2,1)S(1)} %get-tuple-element.79.mixed_ref, bf16[512,2048]{1,0:T(8,128)(2,1)S(1)} %get-tuple-element.78.weight_ref), custom_call_target="tpu_custom_call" | custom-call | flops 2000000000 | bytes 4000000 | tf_op jit(solution)/shard_map/project/pallas_call | solution.py:476
  20.4 0.7 %collective-permute-done.6.got_ref = bf16[128,512]{1,0:T(8,128)(2,1)S(1)} collective-permute-done((bf16[128,512]{1,0:T(8,128)(2,1)S(1)}, bf16[128,512]{1,0:T(8,128)(2,1)S(1)}, u32[]{:S(2)}, u32[]{:S(2)}) %collective-permute-start.6) | collective-permute-done | bytes 131104 | tf_op jit(solution)/shard_map/ppermute | solution.py:624
  21.0 0.1 collective-permute-start.7
  21.2 3.2 %collective-permute-start.10 = (bf16[128,512]{1,0:T(8,128)(2,1)S(1)}, bf16[128,512]{1,0:T(8,128)(2,1)S(1)}, u32[]{:S(2)}, u32[]{:S(2)}) collective-permute-start(bf16[128,512]{1,0:T(8,128)(2,1)S(1)} %core_sum_xy.1), channel_id=1, source_target_pairs={{0,6},{1,7},{2,4},{3,5},{4,2},{5,3},{6,0},{7,1},{8,14},{9,15},{10,... | collective-permute-start | bytes 393224 | tf_op jit(solution)/shard_map/ppermute | solution.py:645
  24.4 0.1 core_sums.1
  24.5 0.4 %collective-permute-start.8 = (bf16[128,512]{1,0:T(8,128)(2,1)S(1)}, bf16[128,512]{1,0:T(8,128)(2,1)S(1)}, u32[]{:S(2)}, u32[]{:S(2)}) collective-permute-start(bf16[128,512]{1,0:T(8,128)(2,1)S(1)} %get-tuple-element.85), channel_id=1, source_target_pairs={{0,2},{1,3},{2,0},{3,1},{4,6},{5,7},{6,4},{7,5},{8,10},{9,11},{10,... | collective-permute-start | bytes 393224 | tf_op jit(solution)/shard_map/ppermute | solution.py:646
  24.9 1.7 %collective-permute-start.9 = (bf16[128,512]{1,0:T(8,128)(2,1)S(1)}, bf16[128,512]{1,0:T(8,128)(2,1)S(1)}, u32[]{:S(2)}, u32[]{:S(2)}) collective-permute-start(bf16[128,512]{1,0:T(8,128)(2,1)S(1)} %get-tuple-element.86), channel_id=1, source_target_pairs={{0,4},{4,0},{8,12},{12,8},{16,20},{20,16},{24,28},{28,24},{1,5},{5... | collective-permute-start | bytes 393224 | tf_op jit(solution)/shard_map/ppermute | solution.py:647
  26.6 2.2 %collective-permute-done.10.xy_ref = bf16[128,512]{1,0:T(8,128)(2,1)S(1)} collective-permute-done((bf16[128,512]{1,0:T(8,128)(2,1)S(1)}, bf16[128,512]{1,0:T(8,128)(2,1)S(1)}, u32[]{:S(2)}, u32[]{:S(2)}) %collective-permute-start.10) | collective-permute-done | bytes 131104 | tf_op jit(solution)/shard_map/ppermute | solution.py:645
  28.7 2.5 %collective-permute-done.8.x_ref = bf16[128,512]{1,0:T(8,128)(2,1)S(1)} collective-permute-done((bf16[128,512]{1,0:T(8,128)(2,1)S(1)}, bf16[128,512]{1,0:T(8,128)(2,1)S(1)}, u32[]{:S(2)}, u32[]{:S(2)}) %collective-permute-start.8) | collective-permute-done | bytes 131104 | tf_op jit(solution)/shard_map/ppermute | solution.py:646
  31.2 0.8 %last_sum.1 = bf16[512,128]{1,0:T(8,128)(2,1)} custom-call(f32[128,512]{1,0:T(8,128)S(1)} %get-tuple-element.84.mine_ref, bf16[128,512]{1,0:T(8,128)(2,1)S(1)} %collective-permute-done.8.x_ref, bf16[128,512]{1,0:T(8,128)(2,1)S(1)} %collective-permute-done.9.y_ref, bf16[128,512]{1,0:T(8,128)(2,1)S(1)} %collective-permute-done.10.xy_ref), custom_call_target="tpu_custom_call" | custom-call | tf_op jit(solution)/shard_map/last_sum/pallas_call | solution.py:476
  (11 shorter events, 0.2 us)
Async XLA Ops:
  1.1 8.0 %collective-permute-start = (bf16[16,1024]{1,0:T(8,128)(2,1)S(1)}, bf16[16,1024]{1,0:T(8,128)(2,1)S(1)}, u32[]{:S(2)}, u32[]{:S(2)}) collective-permute-start(bf16[16,1024]{1,0:T(8,128)(2,1)S(1)} %get-tuple-element.52), channel_id=1, source_target_pairs={{0,4},{4,8},{8,12},{12,16},{16,20},{20,24},{24,28},{28,0},{1,5},{5... | collective-permute-start | bytes 98312 | tf_op jit(solution)/shard_map/ppermute | solution.py:552
  4.1 7.6 %collective-permute-start.1 = (bf16[144,768]{1,0:T(8,128)(2,1)S(1)}, bf16[144,768]{1,0:T(8,128)(2,1)S(1)}, u32[]{:S(2)}, u32[]{:S(2)}) collective-permute-start(bf16[144,768]{1,0:T(8,128)(2,1)S(1)} %get-tuple-element.59), channel_id=1, source_target_pairs={{0,4},{4,0},{8,12},{12,8},{16,20},{20,16},{24,28},{28,24},{1,5},{5... | collective-permute-start | bytes 663560 | tf_op jit(solution)/shard_map/ppermute | solution.py:553
  7.0 4.7 %collective-permute-start.2 = (bf16[16,1024]{1,0:T(8,128)(2,1)S(1)}, bf16[16,1024]{1,0:T(8,128)(2,1)S(1)}, u32[]{:S(2)}, u32[]{:S(2)}) collective-permute-start(bf16[16,1024]{1,0:T(8,128)(2,1)S(1)} %get-tuple-element.60.own_edge_ref), channel_id=1, source_target_pairs={{0,1},{1,0},{2,3},{3,2},{4,12},{5,13},{6,14},{7,15},{8,9},{9,8},{1... | collective-permute-start | bytes 98312 | tf_op jit(solution)/shard_map/ppermute | solution.py:554
  11.5 6.2 %collective-permute-start.3 = (bf16[128,768]{1,0:T(8,128)(2,1)S(1)}, bf16[128,768]{1,0:T(8,128)(2,1)S(1)}, u32[]{:S(2)}, u32[]{:S(2)}) collective-permute-start(bf16[128,768]{1,0:T(8,128)(2,1)S(1)} %get-tuple-element.72), channel_id=1, source_target_pairs={{0,4},{4,0},{8,12},{12,8},{16,20},{20,16},{24,28},{28,24},{1,5},{5... | collective-permute-start | bytes 589832 | tf_op jit(solution)/shard_map/ppermute | solution.py:566
  14.1 3.7 %copy-start = (f32[128]{0:T(128)S(1)}, f32[128]{0:T(128)}, u32[]{:S(2)}) copy-start(f32[128]{0:T(128)} %param.21) | copy-start | bytes 1540
  14.1 5.0 %collective-permute-start.4 = (bf16[4,128,128]{2,1,0:T(8,128)(2,1)S(1)}, bf16[4,128,128]{2,1,0:T(8,128)(2,1)S(1)}, u32[]{:S(2)}, u32[]{:S(2)}) collective-permute-start(bf16[4,128,128]{2,1,0:T(8,128)(2,1)S(1)} %get-tuple-element.76), channel_id=1, source_target_pairs={{0,8},{4,12},{8,0},{12,4},{16,24},{20,28},{24,16},{28,20},{1,9},{5... | collective-permute-start | bytes 393224 | tf_op jit(solution)/shard_map/ppermute | solution.py:589
  15.6 3.5 %collective-permute-start.5 = (bf16[4,128,128]{2,1,0:T(8,128)(2,1)S(1)}, bf16[4,128,128]{2,1,0:T(8,128)(2,1)S(1)}, u32[]{:S(2)}, u32[]{:S(2)}) collective-permute-start(bf16[4,128,128]{2,1,0:T(8,128)(2,1)S(1)} %get-tuple-element.76), channel_id=1, source_target_pairs={{0,1},{1,0},{2,3},{3,2},{4,5},{5,4},{6,7},{7,6},{8,16},{9,17},{10,... | collective-permute-start | bytes 393224 | tf_op jit(solution)/shard_map/ppermute | solution.py:589
  19.6 1.4 %collective-permute-start.6 = (bf16[128,512]{1,0:T(8,128)(2,1)S(1)}, bf16[128,512]{1,0:T(8,128)(2,1)S(1)}, u32[]{:S(2)}, u32[]{:S(2)}) collective-permute-start(bf16[128,512]{1,0:T(8,128)(2,1)S(1)} %get-tuple-element.82), channel_id=1, source_target_pairs={{0,1},{1,0},{2,3},{3,2},{4,5},{5,4},{6,7},{7,6},{8,9},{9,8},{10,11... | collective-permute-start | bytes 393224 | tf_op jit(solution)/shard_map/ppermute | solution.py:624
  21.0 3.4 %collective-permute-start.7 = (bf16[3,128,512]{2,1,0:T(8,128)(2,1)S(1)}, bf16[3,128,512]{2,1,0:T(8,128)(2,1)S(1)}, u32[]{:S(2)}, u32[]{:S(2)}) collective-permute-start(bf16[3,128,512]{2,1,0:T(8,128)(2,1)S(1)} %get-tuple-element.83), channel_id=1, source_target_pairs={{0,1},{1,0},{2,3},{3,2},{4,5},{5,4},{6,7},{7,6},{8,9},{9,8},{10,11... | collective-permute-start | bytes 1179656 | tf_op jit(solution)/shard_map/ppermute | solution.py:634
  21.2 7.5 %collective-permute-start.10 = (bf16[128,512]{1,0:T(8,128)(2,1)S(1)}, bf16[128,512]{1,0:T(8,128)(2,1)S(1)}, u32[]{:S(2)}, u32[]{:S(2)}) collective-permute-start(bf16[128,512]{1,0:T(8,128)(2,1)S(1)} %core_sum_xy.1), channel_id=1, source_target_pairs={{0,6},{1,7},{2,4},{3,5},{4,2},{5,3},{6,0},{7,1},{8,14},{9,15},{10,... | collective-permute-start | bytes 393224 | tf_op jit(solution)/shard_map/ppermute | solution.py:645
  24.5 6.7 %collective-permute-start.8 = (bf16[128,512]{1,0:T(8,128)(2,1)S(1)}, bf16[128,512]{1,0:T(8,128)(2,1)S(1)}, u32[]{:S(2)}, u32[]{:S(2)}) collective-permute-start(bf16[128,512]{1,0:T(8,128)(2,1)S(1)} %get-tuple-element.85), channel_id=1, source_target_pairs={{0,2},{1,3},{2,0},{3,1},{4,6},{5,7},{6,4},{7,5},{8,10},{9,11},{10,... | collective-permute-start | bytes 393224 | tf_op jit(solution)/shard_map/ppermute | solution.py:646
  24.9 6.4 %collective-permute-start.9 = (bf16[128,512]{1,0:T(8,128)(2,1)S(1)}, bf16[128,512]{1,0:T(8,128)(2,1)S(1)}, u32[]{:S(2)}, u32[]{:S(2)}) collective-permute-start(bf16[128,512]{1,0:T(8,128)(2,1)S(1)} %get-tuple-element.86), channel_id=1, source_target_pairs={{0,4},{4,0},{8,12},{12,8},{16,20},{20,16},{24,28},{28,24},{1,5},{5... | collective-permute-start | bytes 393224 | tf_op jit(solution)/shard_map/ppermute | solution.py:647

commit v9 on v8

--- a/solution.py
+++ b/solution.py
@@ -268,7 +268,7 @@
 
 
 def own_kernel(down_ref, along_ref, own_ref, weight_ref, gates_ref, halo_ref,
-               state_ref, map_ref, out_ref, through_ref):
+               state_ref, map_ref, solved_ref, decay_ref, start_ref, key_ref):
     rows = own_ref.shape[0]
     heads = gates_ref.shape[0] // 2
     columns = groups(heads)
@@ -291,18 +291,15 @@
         gates_ref[heads:],
     )
     inverse, once = solve_terms(lower)
-    inside, start_queries = query_terms(
-        seg_down, halo, lambda g: own_ref[:, columns(0, g)], weights, decays, starts, keys_t
-    )
     both = [jnp.concatenate([r.astype(BF16), k], axis=1) for r, k in zip(right, start_keys)]
     solved, _ = solved_with(inverse, once, both)
     ended = [dot(e, s) for e, s in zip(ends, solved)]
-    result = [dot(i, s) for i, s in zip(inside, solved)]
     for h in range(heads):
         state_ref[h] = ended[h][:, :DV]
         map_ref[h] = (scaled_eye(throughs[h]) - ended[h][:, DV:]).astype(BF16)
-        out_ref[:, h * DV : h * DV + DV] = result[h][:, :DV]
-        through_ref[:, h * DK : h * DK + DK] = (start_queries[h] - result[h][:, DV:]).astype(BF16)
+        solved_ref[h], decay_ref[h], start_ref[h] = solved[h], decays[h], starts[h]
+    for g in range(heads // 2):
+        key_ref[g] = keys_t[g]
 
 
 def peer_halo(own_edge_ref, edge_ref, columns):
@@ -361,7 +358,9 @@
         key_ref[g] = keys_t[g]
 
 
-def passing_kernel(solver_ref, start_key_ref, ended_ref, passing_ref, weight_hbm, solved_ref, map_ref, weight_ref, sems):
+def passing_kernel(solver_ref, start_key_ref, ended_ref, passing_ref, own_solved_ref, decay_ref, start_ref, key_ref,
+                   down_ref, along_ref, own_ref, halo_ref, conv_ref, weight_hbm,
+                   solved_ref, map_ref, own_out_ref, own_through_ref, weight_ref, sems):
     depth = weight_ref.shape[0]
     copies = Copies(sems)
     part = depth // PARTS
@@ -375,7 +374,20 @@
     solved = [k + dot(m, k) for m, k in zip(once, solved)]
     solved = [(k + dot(m, k)).astype(BF16) for m, k in zip(twice, solved)]
     ended = [dot(ended_ref[h], solved[h]) for h in every]
+    columns = groups(heads)
+    inside, start_queries = query_terms(
+        counts(down_ref, along_ref, lax.axis_index("ctx") % 2, own_ref.shape[0])[0],
+        lambda which, g: halo_ref[:, columns(which, g)],
+        lambda g: own_ref[:, columns(0, g)],
+        lambda which, g: conv_ref[:, columns(which, g)],
+        [decay_ref[h] for h in every],
+        [start_ref[h] for h in every],
+        [key_ref[g] for g in range(heads // 2)],
+    )
+    result = [dot(inside[h], own_solved_ref[h]) for h in every]
     for h in every:
+        own_out_ref[:, h * DV : h * DV + DV] = result[h][:, :DV]
+        own_through_ref[:, h * DK : h * DK + DK] = (start_queries[h] - result[h][:, DV:]).astype(BF16)
         solved_ref[h] = solved[h]
         map_ref[h] = (scaled_eye(passing_ref[h : h + 1]) - ended[h]).astype(BF16)
     copies.wait()
@@ -554,9 +566,16 @@
     got_far_edge = lax.ppermute(own_edge, ("ctx", "head"), far_ahead)
 
     square = (heads, DK, DV)
-    own_state, own_map, own_out, own_through = call(
+    own_state, own_map, own_solved, own_decay, own_start, own_key = call(
         own_kernel,
-        [(square, F32), (square, BF16), ((rows, value_width), F32), ((rows, value_width), BF16)],
+        [
+            (square, F32),
+            (square, BF16),
+            ((heads, rows, DK + DV), BF16),
+            ((heads, rows, rows), F32),
+            ((heads, rows, DK), F32),
+            ((heads // 2, DK, rows), BF16),
+        ],
         (down, along, own, weights, gates, got_edge),
         "own_terms",
         flops=1_000_000,
@@ -595,12 +614,19 @@
         moved = jnp.where(lax.axis_index("ctx") < 2, 0.0, moved)
         entering = from_earlier((end.astype(F32) + moved).astype(BF16))
     state, solved, solver, start_key, ended, passing, decay, start, key = peer[:9]
-    solved_key, map_, weight = call(
+    solved_key, map_, own_out, own_through, weight = call(
         passing_kernel,
-        [(square, BF16), (square, BF16), ((value_width, out_weight.shape[1]), BF16)],
-        (solver, start_key, ended, passing, out_weight),
+        [
+            (square, BF16),
+            (square, BF16),
+            ((rows, value_width), F32),
+            ((rows, value_width), BF16),
+            ((value_width, out_weight.shape[1]), BF16),
+        ],
+        (solver, start_key, ended, passing, own_solved, own_decay, own_start, own_key, down, along, own, got_edge, weights,
+         out_weight),
         "passing",
-        hbm=(4,),
+        hbm=(13,),
         scratch=(pltpu.SemaphoreType.DMA((PARTS,)),),
         flops=1_000_000_000,
         moved=4_000_000,

time: 32.2 us -> 32 us (level)
  no operation moved by 1% of the time
where the time goes in v9:
time: 32 us; the launch traced here: 31.8 us
  Pallas kernels  12 us (38%)
  starting transfers between devices  11.4 us (36%)
  waiting for transfers between devices  8.33 us (26%)
    pallas_call x11, Pallas kernels, call(): pl.pallas_call(kernel, out_shape=[jax.ShapeDtypeStruct(shape, kind) for s...  12 us
    ppermute x1, starting transfers between devices, body(): got_edge = lax.ppermute(edge, 'ctx', ahead_1)  3.02 us
    ppermute x1, starting transfers between devices, body(): got_xy = lax.ppermute(to_xy, ('ctx', 'head'), both)  3 us
    ppermute x1, waiting for transfers between devices, body(): got_x = lax.ppermute(to_x, 'head', [(i, i ^ 2) for i in range(head_count)])  2.5 us
    ppermute x1, waiting for transfers between devices, body(): got_xy = lax.ppermute(to_xy, ('ctx', 'head'), both)  2.16 us
    ppermute x1, waiting for transfers between devices, body(): got_edge = lax.ppermute(edge, 'ctx', ahead_1)  2.06 us
    ppermute x1, starting transfers between devices, body(): got_y = lax.ppermute(to_y, 'ctx', swap)  1.71 us
    ppermute x1, starting transfers between devices, body(): got_pack = lax.ppermute(pack, 'ctx', swap)  1.52 us
  transfers between devices with their start and end apart: 11, of which 6 were waited for; matrix products, arithmetic and copies ran while one was open for 0% of the time, Pallas kernels for 30%

profile of v9, /device:TPU:0, one launch (start us, length us, event | category | flops | bytes accessed | tf_op | source)
XLA Modules:
  0.0 31.8 jit_solution(10373953319896967996)
XLA Ops:
  0.0 1.1 %pack.1 = (bf16[16,1024]{1,0:T(8,128)(2,1)S(1)}, bf16[144,768]{1,0:T(8,128)(2,1)S(1)}, f32[8,128]{1,0:T(8,128)S(1)}) custom-call(bf16[128,512]{1,0:T(8,128)(2,1)} %q_ref.3, bf16[128,512]{1,0:T(8,128)(2,1)} %k_ref.3, bf16[128,1024]{1,0:T(8,128)(2,1)} %v_ref.3, f32[8,128]{1,0:T(8,128)} %decay_ref.1, f32[8,128]{1,0:T(8,128)} %beta_ref.1), custom_call_target="tpu_custom_call" | custom-call | tf_op jit(solution)/shard_map/pack/pallas_call | solution.py:488
  1.1 3.0 %collective-permute-start = (bf16[16,1024]{1,0:T(8,128)(2,1)S(1)}, bf16[16,1024]{1,0:T(8,128)(2,1)S(1)}, u32[]{:S(2)}, u32[]{:S(2)}) collective-permute-start(bf16[16,1024]{1,0:T(8,128)(2,1)S(1)} %get-tuple-element.56), channel_id=1, source_target_pairs={{0,4},{4,8},{8,12},{12,16},{16,20},{20,24},{24,28},{28,0},{1,5},{5... | collective-permute-start | bytes 98312 | tf_op jit(solution)/shard_map/ppermute | solution.py:564
  4.1 1.5 %collective-permute-start.1 = (bf16[144,768]{1,0:T(8,128)(2,1)S(1)}, bf16[144,768]{1,0:T(8,128)(2,1)S(1)}, u32[]{:S(2)}, u32[]{:S(2)}) collective-permute-start(bf16[144,768]{1,0:T(8,128)(2,1)S(1)} %get-tuple-element.61), channel_id=1, source_target_pairs={{0,4},{4,0},{8,12},{12,8},{16,20},{20,16},{24,28},{28,24},{1,5},{5... | collective-permute-start | bytes 663560 | tf_op jit(solution)/shard_map/ppermute | solution.py:565
  5.6 1.3 %early.1 = (bf16[16,1024]{1,0:T(8,128)(2,1)S(1)}, bf16[128,768]{1,0:T(8,128)(2,1)S(1)}, bf16[128,1024]{1,0:T(8,128)(2,1)S(1)}, f32[4,1024]{1,0:T(4,128)S(1)}, bf...) custom-call(bf16[128,512]{1,0:T(8,128)(2,1)} %q_ref.3, bf16[128,512]{1,0:T(8,128)(2,1)} %k_ref.3, ...), custom_call_target="tpu_custom_call" | custom-call | flops 10000000000 | bytes 2000000 | tf_op jit(solution)/shard_map/early/pallas_call | solution.py:488
  7.0 2.1 %collective-permute-done.halo_ref = bf16[16,1024]{1,0:T(8,128)(2,1)S(1)} collective-permute-done((bf16[16,1024]{1,0:T(8,128)(2,1)S(1)}, bf16[16,1024]{1,0:T(8,128)(2,1)S(1)}, u32[]{:S(2)}, u32[]{:S(2)}) %collective-permute-start) | collective-permute-done | bytes 32800 | tf_op jit(solution)/shard_map/ppermute | solution.py:564
  9.1 2.3 %own_terms.1 = (f32[4,128,128]{2,1,0:T(8,128)S(1)}, bf16[4,128,128]{2,1,0:T(8,128)(2,1)S(1)}, bf16[4,128,256]{2,1,0:T(8,128)(2,1)S(1)}, f32[4,128,128]{2,1,0:T(8...) custom-call(s32[264,128]{1,0:T(8,128)S(1)} %get-tuple-element.51.down_ref, ...), custom_call_target="tpu_custom_call" | custom-call | flops 1000000 | bytes 4000000 | tf_op jit(solution)/shard_map/own_terms/pallas_call | solution.py:488
  11.4 0.1 collective-permute-start.3
  11.5 0.2 collective-permute-done.1.pack_ref
  11.7 2.3 %peer_terms.1 = (bf16[4,128,128]{2,1,0:T(8,128)(2,1)S(1)}, bf16[4,128,128]{2,1,0:T(8,128)(2,1)S(1)}, bf16[12,128,128]{2,1,0:T(8,128)(2,1)S(1)}, bf16[4,128,128]{...) custom-call(s32[264,128]{1,0:T(8,128)S(1)} %get-tuple-element.51.dow, ...), custom_call_target="tpu_custom_call" | custom-call | flops 2000000000 | bytes 4000000 | tf_op jit(solution)/shard_map/peer_terms/pallas_call | solution.py:488
  14.1 1.4 %collective-permute-start.4 = (bf16[4,128,128]{2,1,0:T(8,128)(2,1)S(1)}, bf16[4,128,128]{2,1,0:T(8,128)(2,1)S(1)}, u32[]{:S(2)}, u32[]{:S(2)}) collective-permute-start(bf16[4,128,128]{2,1,0:T(8,128)(2,1)S(1)} %get-tuple-element.84), channel_id=1, source_target_pairs={{0,8},{4,12},{8,0},{12,4},{16,24},{20,28},{24,16},{28,20},{1,9},{5... | collective-permute-start | bytes 393224 | tf_op jit(solution)/shard_map/ppermute | solution.py:608
  15.5 2.2 %passing.1 = (bf16[4,128,128]{2,1,0:T(8,128)(2,1)S(1)}, bf16[4,128,128]{2,1,0:T(8,128)(2,1)S(1)}, f32[128,512]{1,0:T(8,128)S(1)}, bf16[128,512]{1,0:T(8,128)(2,1)S(1)}, bf16[512,2048]{1,0:T(8,128)(2,1)S(1)}) custom-call(bf16[12,128,128]{2,1,0:T(8,128)(2,1)S(1)} %get-tuple-element.63.solver_ref, bf16[4,128,128]{2,1,0:T(8,128)(2,1)S(1)} %get-tuple-element.64.start_key_ref, ...), custom_call_target="tpu_custom_call" | custom-call | flops 1000000000 | bytes 4000000 | tf_op jit(solution)/shard_map/passing/pallas_call | solution.py:488
  17.7 0.7 %local_outputs.1 = (f32[256,512]{1,0:T(8,128)S(1)}, bf16[256,512]{1,0:T(8,128)(2,1)S(1)}, f32[256,512]{1,0:T(8,128)S(1)}) custom-call(f32[4,128,128]{2,1,0:T(8,128)S(1)} %get-tuple-element.57.own_state_ref, bf16[4,128,128]{2,1,0:T(8,128)(2,1)S(1)} %get-tuple-element.60.own_map_ref, f32[128,512]{1,0:T(8,128)S(1)} %get-tuple-element.71.own_out_ref, ...), custom_call_target="tpu_custom_call" | custom-call | flops 1000000000 | bytes 4000000 | tf_op jit(solution)/shard_map/local_outputs/pallas_call | solution.py:488
  18.4 0.7 %collective-permute-done.4.even_ref = bf16[4,128,128]{2,1,0:T(8,128)(2,1)S(1)} collective-permute-done((bf16[4,128,128]{2,1,0:T(8,128)(2,1)S(1)}, bf16[4,128,128]{2,1,0:T(8,128)(2,1)S(1)}, u32[]{:S(2)}, u32[]{:S(2)}) %collective-permute-start.4) | collective-permute-done | bytes 131104 | tf_op jit(solution)/shard_map/ppermute | solution.py:608
  19.1 0.5 %mix.1 = (bf16[256,512]{1,0:T(8,128)(2,1)S(1)}, bf16[128,512]{1,0:T(8,128)(2,1)S(1)}) custom-call(f32[256,512]{1,0:T(8,128)S(1)} %get-tuple-element.82.out_ref, bf16[256,512]{1,0:T(8,128)(2,1)S(1)} %get-tuple-element.83.through_ref, bf16[4,128,128]{2,1,0:T(8,128)(2,1)S(1)} %collective-permute-done.4.even_ref, ...), custom_call_target="tpu_custom_call" | custom-call | tf_op jit(solution)/shard_map/mix/pallas_call | solution.py:488
  19.7 0.7 %project.1 = (bf16[128,512]{1,0:T(8,128)(2,1)S(1)}, bf16[3,128,512]{2,1,0:T(8,128)(2,1)S(1)}, bf16[3,128,512]{2,1,0:T(8,128)(2,1)S(1)}) custom-call(bf16[256,512]{1,0:T(8,128)(2,1)S(1)} %get-tuple-element.87.mixed_ref, bf16[512,2048]{1,0:T(8,128)(2,1)S(1)} %get-tuple-element.86.weight_ref), custom_call_target="tpu_custom_call" | custom-call | flops 2000000000 | bytes 4000000 | tf_op jit(solution)/shard_map/project/pallas_call | solution.py:488
  20.3 0.7 %collective-permute-done.6.got_ref = bf16[128,512]{1,0:T(8,128)(2,1)S(1)} collective-permute-done((bf16[128,512]{1,0:T(8,128)(2,1)S(1)}, bf16[128,512]{1,0:T(8,128)(2,1)S(1)}, u32[]{:S(2)}, u32[]{:S(2)}) %collective-permute-start.6) | collective-permute-done | bytes 131104 | tf_op jit(solution)/shard_map/ppermute | solution.py:650
  21.0 0.1 collective-permute-start.7
  21.2 3.0 %collective-permute-start.10 = (bf16[128,512]{1,0:T(8,128)(2,1)S(1)}, bf16[128,512]{1,0:T(8,128)(2,1)S(1)}, u32[]{:S(2)}, u32[]{:S(2)}) collective-permute-start(bf16[128,512]{1,0:T(8,128)(2,1)S(1)} %core_sum_xy.1), channel_id=1, source_target_pairs={{0,6},{1,7},{2,4},{3,5},{4,2},{5,3},{6,0},{7,1},{8,14},{9,15},{10,... | collective-permute-start | bytes 393224 | tf_op jit(solution)/shard_map/ppermute | solution.py:671
  24.2 0.1 core_sums.1
  24.3 0.4 %collective-permute-start.8 = (bf16[128,512]{1,0:T(8,128)(2,1)S(1)}, bf16[128,512]{1,0:T(8,128)(2,1)S(1)}, u32[]{:S(2)}, u32[]{:S(2)}) collective-permute-start(bf16[128,512]{1,0:T(8,128)(2,1)S(1)} %get-tuple-element.93), channel_id=1, source_target_pairs={{0,2},{1,3},{2,0},{3,1},{4,6},{5,7},{6,4},{7,5},{8,10},{9,11},{10,... | collective-permute-start | bytes 393224 | tf_op jit(solution)/shard_map/ppermute | solution.py:672
  24.7 1.7 %collective-permute-start.9 = (bf16[128,512]{1,0:T(8,128)(2,1)S(1)}, bf16[128,512]{1,0:T(8,128)(2,1)S(1)}, u32[]{:S(2)}, u32[]{:S(2)}) collective-permute-start(bf16[128,512]{1,0:T(8,128)(2,1)S(1)} %get-tuple-element.94), channel_id=1, source_target_pairs={{0,4},{4,0},{8,12},{12,8},{16,20},{20,16},{24,28},{28,24},{1,5},{5... | collective-permute-start | bytes 393224 | tf_op jit(solution)/shard_map/ppermute | solution.py:673
  26.4 2.2 %collective-permute-done.10.xy_ref = bf16[128,512]{1,0:T(8,128)(2,1)S(1)} collective-permute-done((bf16[128,512]{1,0:T(8,128)(2,1)S(1)}, bf16[128,512]{1,0:T(8,128)(2,1)S(1)}, u32[]{:S(2)}, u32[]{:S(2)}) %collective-permute-start.10) | collective-permute-done | bytes 131104 | tf_op jit(solution)/shard_map/ppermute | solution.py:671
  28.5 2.5 %collective-permute-done.8.x_ref = bf16[128,512]{1,0:T(8,128)(2,1)S(1)} collective-permute-done((bf16[128,512]{1,0:T(8,128)(2,1)S(1)}, bf16[128,512]{1,0:T(8,128)(2,1)S(1)}, u32[]{:S(2)}, u32[]{:S(2)}) %collective-permute-start.8) | collective-permute-done | bytes 131104 | tf_op jit(solution)/shard_map/ppermute | solution.py:672
  31.0 0.8 %last_sum.1 = bf16[512,128]{1,0:T(8,128)(2,1)} custom-call(f32[128,512]{1,0:T(8,128)S(1)} %get-tuple-element.92.mine_ref, bf16[128,512]{1,0:T(8,128)(2,1)S(1)} %collective-permute-done.8.x_ref, bf16[128,512]{1,0:T(8,128)(2,1)S(1)} %collective-permute-done.9.y_ref, bf16[128,512]{1,0:T(8,128)(2,1)S(1)} %collective-permute-done.10.xy_ref), custom_call_target="tpu_custom_call" | custom-call | tf_op jit(solution)/shard_map/last_sum/pallas_call | solution.py:488
  (11 shorter events, 0.2 us)
Async XLA Ops:
  1.1 8.0 %collective-permute-start = (bf16[16,1024]{1,0:T(8,128)(2,1)S(1)}, bf16[16,1024]{1,0:T(8,128)(2,1)S(1)}, u32[]{:S(2)}, u32[]{:S(2)}) collective-permute-start(bf16[16,1024]{1,0:T(8,128)(2,1)S(1)} %get-tuple-element.56), channel_id=1, source_target_pairs={{0,4},{4,8},{8,12},{12,16},{16,20},{20,24},{24,28},{28,0},{1,5},{5... | collective-permute-start | bytes 98312 | tf_op jit(solution)/shard_map/ppermute | solution.py:564
  4.1 7.6 %collective-permute-start.1 = (bf16[144,768]{1,0:T(8,128)(2,1)S(1)}, bf16[144,768]{1,0:T(8,128)(2,1)S(1)}, u32[]{:S(2)}, u32[]{:S(2)}) collective-permute-start(bf16[144,768]{1,0:T(8,128)(2,1)S(1)} %get-tuple-element.61), channel_id=1, source_target_pairs={{0,4},{4,0},{8,12},{12,8},{16,20},{20,16},{24,28},{28,24},{1,5},{5... | collective-permute-start | bytes 663560 | tf_op jit(solution)/shard_map/ppermute | solution.py:565
  7.0 4.5 %collective-permute-start.2 = (bf16[16,1024]{1,0:T(8,128)(2,1)S(1)}, bf16[16,1024]{1,0:T(8,128)(2,1)S(1)}, u32[]{:S(2)}, u32[]{:S(2)}) collective-permute-start(bf16[16,1024]{1,0:T(8,128)(2,1)S(1)} %get-tuple-element.62.own_edge_ref), channel_id=1, source_target_pairs={{0,1},{1,0},{2,3},{3,2},{4,12},{5,13},{6,14},{7,15},{8,9},{9,8},{1... | collective-permute-start | bytes 98312 | tf_op jit(solution)/shard_map/ppermute | solution.py:566
  11.4 6.3 %collective-permute-start.3 = (bf16[128,768]{1,0:T(8,128)(2,1)S(1)}, bf16[128,768]{1,0:T(8,128)(2,1)S(1)}, u32[]{:S(2)}, u32[]{:S(2)}) collective-permute-start(bf16[128,768]{1,0:T(8,128)(2,1)S(1)} %get-tuple-element.80), channel_id=1, source_target_pairs={{0,4},{4,0},{8,12},{12,8},{16,20},{20,16},{24,28},{28,24},{1,5},{5... | collective-permute-start | bytes 589832 | tf_op jit(solution)/shard_map/ppermute | solution.py:585
  14.0 3.6 %copy-start = (f32[128]{0:T(128)S(1)}, f32[128]{0:T(128)}, u32[]{:S(2)}) copy-start(f32[128]{0:T(128)} %param.21) | copy-start | bytes 1540
  14.1 5.0 %collective-permute-start.4 = (bf16[4,128,128]{2,1,0:T(8,128)(2,1)S(1)}, bf16[4,128,128]{2,1,0:T(8,128)(2,1)S(1)}, u32[]{:S(2)}, u32[]{:S(2)}) collective-permute-start(bf16[4,128,128]{2,1,0:T(8,128)(2,1)S(1)} %get-tuple-element.84), channel_id=1, source_target_pairs={{0,8},{4,12},{8,0},{12,4},{16,24},{20,28},{24,16},{28,20},{1,9},{5... | collective-permute-start | bytes 393224 | tf_op jit(solution)/shard_map/ppermute | solution.py:608
  15.5 3.6 %collective-permute-start.5 = (bf16[4,128,128]{2,1,0:T(8,128)(2,1)S(1)}, bf16[4,128,128]{2,1,0:T(8,128)(2,1)S(1)}, u32[]{:S(2)}, u32[]{:S(2)}) collective-permute-start(bf16[4,128,128]{2,1,0:T(8,128)(2,1)S(1)} %get-tuple-element.84), channel_id=1, source_target_pairs={{0,1},{1,0},{2,3},{3,2},{4,5},{5,4},{6,7},{7,6},{8,16},{9,17},{10,... | collective-permute-start | bytes 393224 | tf_op jit(solution)/shard_map/ppermute | solution.py:608
  19.6 1.4 %collective-permute-start.6 = (bf16[128,512]{1,0:T(8,128)(2,1)S(1)}, bf16[128,512]{1,0:T(8,128)(2,1)S(1)}, u32[]{:S(2)}, u32[]{:S(2)}) collective-permute-start(bf16[128,512]{1,0:T(8,128)(2,1)S(1)} %get-tuple-element.90), channel_id=1, source_target_pairs={{0,1},{1,0},{2,3},{3,2},{4,5},{5,4},{6,7},{7,6},{8,9},{9,8},{10,11... | collective-permute-start | bytes 393224 | tf_op jit(solution)/shard_map/ppermute | solution.py:650
  21.0 3.2 %collective-permute-start.7 = (bf16[3,128,512]{2,1,0:T(8,128)(2,1)S(1)}, bf16[3,128,512]{2,1,0:T(8,128)(2,1)S(1)}, u32[]{:S(2)}, u32[]{:S(2)}) collective-permute-start(bf16[3,128,512]{2,1,0:T(8,128)(2,1)S(1)} %get-tuple-element.91), channel_id=1, source_target_pairs={{0,1},{1,0},{2,3},{3,2},{4,5},{5,4},{6,7},{7,6},{8,9},{9,8},{10,11... | collective-permute-start | bytes 1179656 | tf_op jit(solution)/shard_map/ppermute | solution.py:660
  21.2 7.3 %collective-permute-start.10 = (bf16[128,512]{1,0:T(8,128)(2,1)S(1)}, bf16[128,512]{1,0:T(8,128)(2,1)S(1)}, u32[]{:S(2)}, u32[]{:S(2)}) collective-permute-start(bf16[128,512]{1,0:T(8,128)(2,1)S(1)} %core_sum_xy.1), channel_id=1, source_target_pairs={{0,6},{1,7},{2,4},{3,5},{4,2},{5,3},{6,0},{7,1},{8,14},{9,15},{10,... | collective-permute-start | bytes 393224 | tf_op jit(solution)/shard_map/ppermute | solution.py:671
  24.3 6.7 %collective-permute-start.8 = (bf16[128,512]{1,0:T(8,128)(2,1)S(1)}, bf16[128,512]{1,0:T(8,128)(2,1)S(1)}, u32[]{:S(2)}, u32[]{:S(2)}) collective-permute-start(bf16[128,512]{1,0:T(8,128)(2,1)S(1)} %get-tuple-element.93), channel_id=1, source_target_pairs={{0,2},{1,3},{2,0},{3,1},{4,6},{5,7},{6,4},{7,5},{8,10},{9,11},{10,... | collective-permute-start | bytes 393224 | tf_op jit(solution)/shard_map/ppermute | solution.py:672
  24.7 6.4 %collective-permute-start.9 = (bf16[128,512]{1,0:T(8,128)(2,1)S(1)}, bf16[128,512]{1,0:T(8,128)(2,1)S(1)}, u32[]{:S(2)}, u32[]{:S(2)}) collective-permute-start(bf16[128,512]{1,0:T(8,128)(2,1)S(1)} %get-tuple-element.94), channel_id=1, source_target_pairs={{0,4},{4,0},{8,12},{12,8},{16,20},{20,16},{24,28},{28,24},{1,5},{5... | collective-permute-start | bytes 393224 | tf_op jit(solution)/shard_map/ppermute | solution.py:673

commit v10 on v9

--- a/solution.py
+++ b/solution.py
@@ -8,6 +8,7 @@
 DK = 128
 DV = 128
 EDGE = 16
+GATE_ROWS = 8
 PARTS = 8
 F32 = jnp.float32
 BF16 = jnp.bfloat16
@@ -94,7 +95,7 @@
         width = ref.shape[1] // 2
         copies.start(ref.at[:, half_columns(ref, other)], pack_ref.at[pl.ds(0, rows), pl.ds(at, width)])
         at += width
-    pack_ref[rows : rows + EDGE, :] = jnp.zeros((EDGE, pack_ref.shape[1]), BF16)
+    pack_ref[rows : rows + GATE_ROWS, :] = jnp.zeros((GATE_ROWS, pack_ref.shape[1]), BF16)
     copies.wait(0, 2)
     decay = raw_gates[0]
     log_gamma = -(jnp.maximum(decay, 0.0) + jnp.log1p(jnp.exp(-jnp.abs(decay))))
@@ -311,7 +312,7 @@
                 state_ref, solved_ref, solver_ref, start_key_ref, ended_ref, passing_ref, decay_ref, start_ref, key_ref,
                 pair_state_ref, *pair_map_ref):
     y = lax.axis_index("ctx") % 2
-    rows = pack_ref.shape[0] - EDGE
+    rows = pack_ref.shape[0] - GATE_ROWS
     heads = own_state_ref.shape[0]
     columns = groups(heads)
     key_width = heads // 2 * DK
@@ -537,7 +538,7 @@
 
     edge, pack, gates = call(
         pack_kernel,
-        [((EDGE, half_width), BF16), ((rows + EDGE, key_width + value_width), BF16), ((2 * heads, rows), F32)],
+        [((EDGE, half_width), BF16), ((rows + GATE_ROWS, key_width + value_width), BF16), ((2 * heads, rows), F32)],
         (query_in, key_in, value_in, decay_in, beta_in),
         "pack",
         hbm=range(5),

time: 32 us -> 32 us (level)
  starting transfers between devices: 11.4 us -> 11.9 us
  waiting for transfers between devices: 8.33 us -> 7.85 us
  transfers between devices with their start and end apart: 11 -> 11, of which waited for: 6 -> 5; matrix products, arithmetic and copies ran while one was open for 0% -> 0% of each run, Pallas kernels for 30% -> 30%
where the time goes in v10:
time: 32 us; the launch traced here: 31.8 us
  Pallas kernels  12 us (38%)
  starting transfers between devices  11.9 us (37%)
  waiting for transfers between devices  7.85 us (25%)
    pallas_call x11, Pallas kernels, call(): pl.pallas_call(kernel, out_shape=[jax.ShapeDtypeStruct(shape, kind) for s...  12 us
    ppermute x1, starting transfers between devices, body(): got_xy = lax.ppermute(to_xy, ('ctx', 'head'), both)  3.23 us
    ppermute x1, starting transfers between devices, body(): got_edge = lax.ppermute(edge, 'ctx', ahead_1)  3.02 us
    ppermute x1, waiting for transfers between devices, body(): got_x = lax.ppermute(to_x, 'head', [(i, i ^ 2) for i in range(head_count)])  2.51 us
    ppermute x1, waiting for transfers between devices, body(): got_xy = lax.ppermute(to_xy, ('ctx', 'head'), both)  2.15 us
    ppermute x1, waiting for transfers between devices, body(): got_edge = lax.ppermute(edge, 'ctx', ahead_1)  2.06 us
    ppermute x1, starting transfers between devices, body(): got_y = lax.ppermute(to_y, 'ctx', swap)  1.71 us
    ppermute x1, starting transfers between devices, from_earlier(): lax.ppermute(value, 'ctx', even_swap)  1.63 us
  transfers between devices with their start and end apart: 11, of which 5 were waited for; matrix products, arithmetic and copies ran while one was open for 0% of the time, Pallas kernels for 30%

profile of v10, /device:TPU:0, one launch (start us, length us, event | category | flops | bytes accessed | tf_op | source)
XLA Modules:
  0.0 31.8 jit_solution(966544657348908163)
XLA Ops:
  0.0 1.1 %pack.1 = (bf16[16,1024]{1,0:T(8,128)(2,1)S(1)}, bf16[136,768]{1,0:T(8,128)(2,1)S(1)}, f32[8,128]{1,0:T(8,128)S(1)}) custom-call(bf16[128,512]{1,0:T(8,128)(2,1)} %q_ref.3, bf16[128,512]{1,0:T(8,128)(2,1)} %k_ref.3, bf16[128,1024]{1,0:T(8,128)(2,1)} %v_ref.3, f32[8,128]{1,0:T(8,128)} %decay_ref.1, f32[8,128]{1,0:T(8,128)} %beta_ref.1), custom_call_target="tpu_custom_call" | custom-call | tf_op jit(solution)/shard_map/pack/pallas_call | solution.py:489
  1.1 3.0 %collective-permute-start = (bf16[16,1024]{1,0:T(8,128)(2,1)S(1)}, bf16[16,1024]{1,0:T(8,128)(2,1)S(1)}, u32[]{:S(2)}, u32[]{:S(2)}) collective-permute-start(bf16[16,1024]{1,0:T(8,128)(2,1)S(1)} %get-tuple-element.56), channel_id=1, source_target_pairs={{0,4},{4,8},{8,12},{12,16},{16,20},{20,24},{24,28},{28,0},{1,5},{5... | collective-permute-start | bytes 98312 | tf_op jit(solution)/shard_map/ppermute | solution.py:565
  4.1 1.5 %collective-permute-start.1 = (bf16[136,768]{1,0:T(8,128)(2,1)S(1)}, bf16[136,768]{1,0:T(8,128)(2,1)S(1)}, u32[]{:S(2)}, u32[]{:S(2)}) collective-permute-start(bf16[136,768]{1,0:T(8,128)(2,1)S(1)} %get-tuple-element.61), channel_id=1, source_target_pairs={{0,4},{4,0},{8,12},{12,8},{16,20},{20,16},{24,28},{28,24},{1,5},{5... | collective-permute-start | bytes 626696 | tf_op jit(solution)/shard_map/ppermute | solution.py:566
  5.6 1.3 %early.1 = (bf16[16,1024]{1,0:T(8,128)(2,1)S(1)}, bf16[128,768]{1,0:T(8,128)(2,1)S(1)}, bf16[128,1024]{1,0:T(8,128)(2,1)S(1)}, f32[4,1024]{1,0:T(4,128)S(1)}, bf...) custom-call(bf16[128,512]{1,0:T(8,128)(2,1)} %q_ref.3, bf16[128,512]{1,0:T(8,128)(2,1)} %k_ref.3, ...), custom_call_target="tpu_custom_call" | custom-call | flops 10000000000 | bytes 2000000 | tf_op jit(solution)/shard_map/early/pallas_call | solution.py:489
  7.0 2.1 %collective-permute-done.halo_ref = bf16[16,1024]{1,0:T(8,128)(2,1)S(1)} collective-permute-done((bf16[16,1024]{1,0:T(8,128)(2,1)S(1)}, bf16[16,1024]{1,0:T(8,128)(2,1)S(1)}, u32[]{:S(2)}, u32[]{:S(2)}) %collective-permute-start) | collective-permute-done | bytes 32800 | tf_op jit(solution)/shard_map/ppermute | solution.py:565
  9.1 2.3 %own_terms.1 = (f32[4,128,128]{2,1,0:T(8,128)S(1)}, bf16[4,128,128]{2,1,0:T(8,128)(2,1)S(1)}, bf16[4,128,256]{2,1,0:T(8,128)(2,1)S(1)}, f32[4,128,128]{2,1,0:T(8...) custom-call(s32[264,128]{1,0:T(8,128)S(1)} %get-tuple-element.51.down_ref, ...), custom_call_target="tpu_custom_call" | custom-call | flops 1000000 | bytes 4000000 | tf_op jit(solution)/shard_map/own_terms/pallas_call | solution.py:489
  11.4 0.1 collective-permute-start.3
  11.5 2.3 %peer_terms.1 = (bf16[4,128,128]{2,1,0:T(8,128)(2,1)S(1)}, bf16[4,128,128]{2,1,0:T(8,128)(2,1)S(1)}, bf16[12,128,128]{2,1,0:T(8,128)(2,1)S(1)}, bf16[4,128,128]{...) custom-call(s32[264,128]{1,0:T(8,128)S(1)} %get-tuple-element.51.dow, ...), custom_call_target="tpu_custom_call" | custom-call | flops 2000000000 | bytes 4000000 | tf_op jit(solution)/shard_map/peer_terms/pallas_call | solution.py:489
  13.8 1.6 %collective-permute-start.4 = (bf16[4,128,128]{2,1,0:T(8,128)(2,1)S(1)}, bf16[4,128,128]{2,1,0:T(8,128)(2,1)S(1)}, u32[]{:S(2)}, u32[]{:S(2)}) collective-permute-start(bf16[4,128,128]{2,1,0:T(8,128)(2,1)S(1)} %get-tuple-element.84), channel_id=1, source_target_pairs={{0,8},{4,12},{8,0},{12,4},{16,24},{20,28},{24,16},{28,20},{1,9},{5... | collective-permute-start | bytes 393224 | tf_op jit(solution)/shard_map/ppermute | solution.py:609
  15.5 2.2 %passing.1 = (bf16[4,128,128]{2,1,0:T(8,128)(2,1)S(1)}, bf16[4,128,128]{2,1,0:T(8,128)(2,1)S(1)}, f32[128,512]{1,0:T(8,128)S(1)}, bf16[128,512]{1,0:T(8,128)(2,1)S(1)}, bf16[512,2048]{1,0:T(8,128)(2,1)S(1)}) custom-call(bf16[12,128,128]{2,1,0:T(8,128)(2,1)S(1)} %get-tuple-element.63.solver_ref, bf16[4,128,128]{2,1,0:T(8,128)(2,1)S(1)} %get-tuple-element.64.start_key_ref, ...), custom_call_target="tpu_custom_call" | custom-call | flops 1000000000 | bytes 4000000 | tf_op jit(solution)/shard_map/passing/pallas_call | solution.py:489
  17.7 0.7 %local_outputs.1 = (f32[256,512]{1,0:T(8,128)S(1)}, bf16[256,512]{1,0:T(8,128)(2,1)S(1)}, f32[256,512]{1,0:T(8,128)S(1)}) custom-call(f32[4,128,128]{2,1,0:T(8,128)S(1)} %get-tuple-element.57.own_state_ref, bf16[4,128,128]{2,1,0:T(8,128)(2,1)S(1)} %get-tuple-element.60.own_map_ref, f32[128,512]{1,0:T(8,128)S(1)} %get-tuple-element.71.own_out_ref, ...), custom_call_target="tpu_custom_call" | custom-call | flops 1000000000 | bytes 4000000 | tf_op jit(solution)/shard_map/local_outputs/pallas_call | solution.py:489
  18.4 0.5 %collective-permute-done.4.even_ref = bf16[4,128,128]{2,1,0:T(8,128)(2,1)S(1)} collective-permute-done((bf16[4,128,128]{2,1,0:T(8,128)(2,1)S(1)}, bf16[4,128,128]{2,1,0:T(8,128)(2,1)S(1)}, u32[]{:S(2)}, u32[]{:S(2)}) %collective-permute-start.4) | collective-permute-done | bytes 131104 | tf_op jit(solution)/shard_map/ppermute | solution.py:609
  18.9 0.5 %mix.1 = (bf16[256,512]{1,0:T(8,128)(2,1)S(1)}, bf16[128,512]{1,0:T(8,128)(2,1)S(1)}) custom-call(f32[256,512]{1,0:T(8,128)S(1)} %get-tuple-element.82.out_ref, bf16[256,512]{1,0:T(8,128)(2,1)S(1)} %get-tuple-element.83.through_ref, bf16[4,128,128]{2,1,0:T(8,128)(2,1)S(1)} %collective-permute-done.4.even_ref, ...), custom_call_target="tpu_custom_call" | custom-call | tf_op jit(solution)/shard_map/mix/pallas_call | solution.py:489
  19.4 0.1 collective-permute-start.6
  19.5 0.6 %project.1 = (bf16[128,512]{1,0:T(8,128)(2,1)S(1)}, bf16[3,128,512]{2,1,0:T(8,128)(2,1)S(1)}, bf16[3,128,512]{2,1,0:T(8,128)(2,1)S(1)}) custom-call(bf16[256,512]{1,0:T(8,128)(2,1)S(1)} %get-tuple-element.87.mixed_ref, bf16[512,2048]{1,0:T(8,128)(2,1)S(1)} %get-tuple-element.86.weight_ref), custom_call_target="tpu_custom_call" | custom-call | flops 2000000000 | bytes 4000000 | tf_op jit(solution)/shard_map/project/pallas_call | solution.py:489
  20.1 0.6 %collective-permute-done.6.got_ref = bf16[128,512]{1,0:T(8,128)(2,1)S(1)} collective-permute-done((bf16[128,512]{1,0:T(8,128)(2,1)S(1)}, bf16[128,512]{1,0:T(8,128)(2,1)S(1)}, u32[]{:S(2)}, u32[]{:S(2)}) %collective-permute-start.6) | collective-permute-done | bytes 131104 | tf_op jit(solution)/shard_map/ppermute | solution.py:651
  20.8 0.1 collective-permute-start.7
  21.0 3.2 %collective-permute-start.10 = (bf16[128,512]{1,0:T(8,128)(2,1)S(1)}, bf16[128,512]{1,0:T(8,128)(2,1)S(1)}, u32[]{:S(2)}, u32[]{:S(2)}) collective-permute-start(bf16[128,512]{1,0:T(8,128)(2,1)S(1)} %core_sum_xy.1), channel_id=1, source_target_pairs={{0,6},{1,7},{2,4},{3,5},{4,2},{5,3},{6,0},{7,1},{8,14},{9,15},{10,... | collective-permute-start | bytes 393224 | tf_op jit(solution)/shard_map/ppermute | solution.py:672
  24.2 0.1 core_sums.1
  24.3 0.4 %collective-permute-start.8 = (bf16[128,512]{1,0:T(8,128)(2,1)S(1)}, bf16[128,512]{1,0:T(8,128)(2,1)S(1)}, u32[]{:S(2)}, u32[]{:S(2)}) collective-permute-start(bf16[128,512]{1,0:T(8,128)(2,1)S(1)} %get-tuple-element.93), channel_id=1, source_target_pairs={{0,2},{1,3},{2,0},{3,1},{4,6},{5,7},{6,4},{7,5},{8,10},{9,11},{10,... | collective-permute-start | bytes 393224 | tf_op jit(solution)/shard_map/ppermute | solution.py:673
  24.7 1.7 %collective-permute-start.9 = (bf16[128,512]{1,0:T(8,128)(2,1)S(1)}, bf16[128,512]{1,0:T(8,128)(2,1)S(1)}, u32[]{:S(2)}, u32[]{:S(2)}) collective-permute-start(bf16[128,512]{1,0:T(8,128)(2,1)S(1)} %get-tuple-element.94), channel_id=1, source_target_pairs={{0,4},{4,0},{8,12},{12,8},{16,20},{20,16},{24,28},{28,24},{1,5},{5... | collective-permute-start | bytes 393224 | tf_op jit(solution)/shard_map/ppermute | solution.py:674
  26.4 2.2 %collective-permute-done.10.xy_ref = bf16[128,512]{1,0:T(8,128)(2,1)S(1)} collective-permute-done((bf16[128,512]{1,0:T(8,128)(2,1)S(1)}, bf16[128,512]{1,0:T(8,128)(2,1)S(1)}, u32[]{:S(2)}, u32[]{:S(2)}) %collective-permute-start.10) | collective-permute-done | bytes 131104 | tf_op jit(solution)/shard_map/ppermute | solution.py:672
  28.5 2.5 %collective-permute-done.8.x_ref = bf16[128,512]{1,0:T(8,128)(2,1)S(1)} collective-permute-done((bf16[128,512]{1,0:T(8,128)(2,1)S(1)}, bf16[128,512]{1,0:T(8,128)(2,1)S(1)}, u32[]{:S(2)}, u32[]{:S(2)}) %collective-permute-start.8) | collective-permute-done | bytes 131104 | tf_op jit(solution)/shard_map/ppermute | solution.py:673
  31.0 0.8 %last_sum.1 = bf16[512,128]{1,0:T(8,128)(2,1)} custom-call(f32[128,512]{1,0:T(8,128)S(1)} %get-tuple-element.92.mine_ref, bf16[128,512]{1,0:T(8,128)(2,1)S(1)} %collective-permute-done.8.x_ref, bf16[128,512]{1,0:T(8,128)(2,1)S(1)} %collective-permute-done.9.y_ref, bf16[128,512]{1,0:T(8,128)(2,1)S(1)} %collective-permute-done.10.xy_ref), custom_call_target="tpu_custom_call" | custom-call | tf_op jit(solution)/shard_map/last_sum/pallas_call | solution.py:489
  (11 shorter events, 0.1 us)
Async XLA Ops:
  1.1 8.0 %collective-permute-start = (bf16[16,1024]{1,0:T(8,128)(2,1)S(1)}, bf16[16,1024]{1,0:T(8,128)(2,1)S(1)}, u32[]{:S(2)}, u32[]{:S(2)}) collective-permute-start(bf16[16,1024]{1,0:T(8,128)(2,1)S(1)} %get-tuple-element.56), channel_id=1, source_target_pairs={{0,4},{4,8},{8,12},{12,16},{16,20},{20,24},{24,28},{28,0},{1,5},{5... | collective-permute-start | bytes 98312 | tf_op jit(solution)/shard_map/ppermute | solution.py:565
  4.1 7.3 %collective-permute-start.1 = (bf16[136,768]{1,0:T(8,128)(2,1)S(1)}, bf16[136,768]{1,0:T(8,128)(2,1)S(1)}, u32[]{:S(2)}, u32[]{:S(2)}) collective-permute-start(bf16[136,768]{1,0:T(8,128)(2,1)S(1)} %get-tuple-element.61), channel_id=1, source_target_pairs={{0,4},{4,0},{8,12},{12,8},{16,20},{20,16},{24,28},{28,24},{1,5},{5... | collective-permute-start | bytes 626696 | tf_op jit(solution)/shard_map/ppermute | solution.py:566
  7.0 4.5 %collective-permute-start.2 = (bf16[16,1024]{1,0:T(8,128)(2,1)S(1)}, bf16[16,1024]{1,0:T(8,128)(2,1)S(1)}, u32[]{:S(2)}, u32[]{:S(2)}) collective-permute-start(bf16[16,1024]{1,0:T(8,128)(2,1)S(1)} %get-tuple-element.62.own_edge_ref), channel_id=1, source_target_pairs={{0,1},{1,0},{2,3},{3,2},{4,12},{5,13},{6,14},{7,15},{8,9},{9,8},{1... | collective-permute-start | bytes 98312 | tf_op jit(solution)/shard_map/ppermute | solution.py:567
  11.4 6.3 %collective-permute-start.3 = (bf16[128,768]{1,0:T(8,128)(2,1)S(1)}, bf16[128,768]{1,0:T(8,128)(2,1)S(1)}, u32[]{:S(2)}, u32[]{:S(2)}) collective-permute-start(bf16[128,768]{1,0:T(8,128)(2,1)S(1)} %get-tuple-element.80), channel_id=1, source_target_pairs={{0,4},{4,0},{8,12},{12,8},{16,20},{20,16},{24,28},{28,24},{1,5},{5... | collective-permute-start | bytes 589832 | tf_op jit(solution)/shard_map/ppermute | solution.py:586
  13.8 3.8 %copy-start = (f32[128]{0:T(128)S(1)}, f32[128]{0:T(128)}, u32[]{:S(2)}) copy-start(f32[128]{0:T(128)} %param.21) | copy-start | bytes 1540
  13.8 5.0 %collective-permute-start.4 = (bf16[4,128,128]{2,1,0:T(8,128)(2,1)S(1)}, bf16[4,128,128]{2,1,0:T(8,128)(2,1)S(1)}, u32[]{:S(2)}, u32[]{:S(2)}) collective-permute-start(bf16[4,128,128]{2,1,0:T(8,128)(2,1)S(1)} %get-tuple-element.84), channel_id=1, source_target_pairs={{0,8},{4,12},{8,0},{12,4},{16,24},{20,28},{24,16},{28,20},{1,9},{5... | collective-permute-start | bytes 393224 | tf_op jit(solution)/shard_map/ppermute | solution.py:609
  15.5 3.4 %collective-permute-start.5 = (bf16[4,128,128]{2,1,0:T(8,128)(2,1)S(1)}, bf16[4,128,128]{2,1,0:T(8,128)(2,1)S(1)}, u32[]{:S(2)}, u32[]{:S(2)}) collective-permute-start(bf16[4,128,128]{2,1,0:T(8,128)(2,1)S(1)} %get-tuple-element.84), channel_id=1, source_target_pairs={{0,1},{1,0},{2,3},{3,2},{4,5},{5,4},{6,7},{7,6},{8,16},{9,17},{10,... | collective-permute-start | bytes 393224 | tf_op jit(solution)/shard_map/ppermute | solution.py:609
  19.4 1.4 %collective-permute-start.6 = (bf16[128,512]{1,0:T(8,128)(2,1)S(1)}, bf16[128,512]{1,0:T(8,128)(2,1)S(1)}, u32[]{:S(2)}, u32[]{:S(2)}) collective-permute-start(bf16[128,512]{1,0:T(8,128)(2,1)S(1)} %get-tuple-element.90), channel_id=1, source_target_pairs={{0,1},{1,0},{2,3},{3,2},{4,5},{5,4},{6,7},{7,6},{8,9},{9,8},{10,11... | collective-permute-start | bytes 393224 | tf_op jit(solution)/shard_map/ppermute | solution.py:651
  20.8 3.4 %collective-permute-start.7 = (bf16[3,128,512]{2,1,0:T(8,128)(2,1)S(1)}, bf16[3,128,512]{2,1,0:T(8,128)(2,1)S(1)}, u32[]{:S(2)}, u32[]{:S(2)}) collective-permute-start(bf16[3,128,512]{2,1,0:T(8,128)(2,1)S(1)} %get-tuple-element.91), channel_id=1, source_target_pairs={{0,1},{1,0},{2,3},{3,2},{4,5},{5,4},{6,7},{7,6},{8,9},{9,8},{10,11... | collective-permute-start | bytes 1179656 | tf_op jit(solution)/shard_map/ppermute | solution.py:661
  21.0 7.6 %collective-permute-start.10 = (bf16[128,512]{1,0:T(8,128)(2,1)S(1)}, bf16[128,512]{1,0:T(8,128)(2,1)S(1)}, u32[]{:S(2)}, u32[]{:S(2)}) collective-permute-start(bf16[128,512]{1,0:T(8,128)(2,1)S(1)} %core_sum_xy.1), channel_id=1, source_target_pairs={{0,6},{1,7},{2,4},{3,5},{4,2},{5,3},{6,0},{7,1},{8,14},{9,15},{10,... | collective-permute-start | bytes 393224 | tf_op jit(solution)/shard_map/ppermute | solution.py:672
  24.3 6.7 %collective-permute-start.8 = (bf16[128,512]{1,0:T(8,128)(2,1)S(1)}, bf16[128,512]{1,0:T(8,128)(2,1)S(1)}, u32[]{:S(2)}, u32[]{:S(2)}) collective-permute-start(bf16[128,512]{1,0:T(8,128)(2,1)S(1)} %get-tuple-element.93), channel_id=1, source_target_pairs={{0,2},{1,3},{2,0},{3,1},{4,6},{5,7},{6,4},{7,5},{8,10},{9,11},{10,... | collective-permute-start | bytes 393224 | tf_op jit(solution)/shard_map/ppermute | solution.py:673
  24.7 6.4 %collective-permute-start.9 = (bf16[128,512]{1,0:T(8,128)(2,1)S(1)}, bf16[128,512]{1,0:T(8,128)(2,1)S(1)}, u32[]{:S(2)}, u32[]{:S(2)}) collective-permute-start(bf16[128,512]{1,0:T(8,128)(2,1)S(1)} %get-tuple-element.94), channel_id=1, source_target_pairs={{0,4},{4,0},{8,12},{12,8},{16,20},{20,16},{24,28},{28,24},{1,5},{5... | collective-permute-start | bytes 393224 | tf_op jit(solution)/shard_map/ppermute | solution.py:674
